TPU v7x, 32 devices: a whole 2x2x4 slice. The times are simulated.
32 devices in a mesh: grp: 2 (over x), date: 16 (over z, y, core).
Axes of the slice: x: 2, y: 2, z: 4, core: 2. Of those that a mesh axis runs over, the one named last changes fastest.
Arguments:
- radar_stack: bfloat16 [2, 128, 256, 256], P(None, 'date', 'grp'), parts along dimension 2, may hold values from -6 to 6
- filter_taps: float32 [2, 128, 128], P(None, 'date'), may hold values from -0.6 to 0.6
- filter_lengths: int32 [128], P('date'), may hold values from 64 to 128
- resample_kernel: float32 [4], replicated, may hold values from 0.2 to 1
- tile_owner: int32 [512, 1], P(('grp', 'date')), parts along dimension 0, may hold values from 0 to 15; in each aligned block of 16 rows (0 to 15, 16 to 31, ...) at most 2 rows name the same one
- map_slot: int32 [512], P(('grp', 'date')), parts along dimension 0, may hold values from 0 to 7
- correlation: int32 [512], P(('grp', 'date')), parts along dimension 0, may hold values from 1 to 128
- offsets: int32 [512], P(('grp', 'date')), parts along dimension 0, may hold values from 0 to 127
Outputs:
- geocoded: float32 [256, 256, 128], P(('grp', 'date')), parts along dimension 0
There are 2 independent parts, one for each index of `grp`. A program takes and returns all parts, laid end to end along the dimension named above; an argument that names none is the same for every part. Nothing has to cross between parts.
Inputs may be any that keep to these rules, and one draw needn't show every extreme that they name: `tile_owner`: among the 16 tiles of one device, at most 2 name the same owner.
All inputs are finite; a program needn't handle non-finite values. Where the computation divides by a largest or mean magnitude, that divisor is 1e-20 or more.
Results may differ from a plain program's by a relative error of at most 0.0055.
Values may be sent and summed in bfloat16 or wider, within the bound.
No kernel may reach another device: no remote copies, remote signals or barrier semaphores. Data moves between devices by JAX's collectives and lax.ppermute only.
A program may use at most 64 MiB of HBM per device.

v0:
```python
from functools import partial

import jax
import jax.numpy as jnp
from jax import lax
from jax.experimental import pallas as pl
from jax.experimental.pallas import tpu as pltpu
from jax.sharding import PartitionSpec as P

PATCH_AZ = 8
PATCH_RG = 16
TILE = 128
KW = 4
CAP = 2
MAP_DEV = 8
GROUP = 4

diag_load = 0.5
small_eps = 1e-05
VMEM = pl.BlockSpec(memory_space=pltpu.VMEM)
SMEM = pl.BlockSpec(memory_space=pltpu.SMEM)
params = pltpu.CompilerParams(vmem_limit_bytes=48 * 1024 * 1024)


def filter_kernel(lengths, taps, radar, sent, staged):
    _, dates_here, rows_count, ranges_count = radar.shape
    tap_count = taps.shape[2]
    period = rows_count + tap_count
    position = lax.broadcasted_iota(jnp.int32, (1, tap_count), 1)
    for date in range(dates_here):
        mats = []
        for part in range(2):
            used = jnp.where(position < lengths[date], taps[part, pl.ds(date, 1), :], 0.0)
            padded = jnp.concatenate([used, jnp.zeros((1, period - tap_count), jnp.float32)], axis=1)
            spread = jnp.broadcast_to(padded, (rows_count, period))
            rolled = pltpu.roll(spread, period - tap_count // 2, 1, stride=1, stride_axis=0)
            mats.append(rolled[:, :rows_count])
        real_mat, imag_mat = mats
        columns = radar[:, date].reshape(2 * rows_count, ranges_count)
        for part, halves in enumerate(((real_mat, -imag_mat), (imag_mat, real_mat))):
            operator = jnp.concatenate(halves, axis=1).astype(jnp.bfloat16)
            product = jnp.dot(operator, columns, preferred_element_type=jnp.float32)
            for side in range(ranges_count // TILE):
                skewed = pltpu.roll(
                    product[:, side * TILE : (side + 1) * TILE], 0, 1, stride=PATCH_RG, stride_axis=0
                )
                first = part * dates_here + date
                staged[side, pl.ds(first, rows_count, stride=2 * dates_here), :] = skewed
    for side in range(ranges_count // TILE):
        sent[:, side * TILE : (side + 1) * TILE] = staged[side].astype(jnp.bfloat16)


def barrel(blocks, lane_block):
    count = len(blocks)
    step = 1
    while step < count:
        taken = (lane_block & step) != 0
        blocks = [jnp.where(taken, blocks[(i + step) % count], blocks[i]) for i in range(count)]
        step *= 2
    return blocks


def embedded(real_part, imag_part):
    upper = jnp.concatenate([real_part, -imag_part], axis=1)
    lower = jnp.concatenate([imag_part, real_part], axis=1)
    return jnp.concatenate([upper, lower], axis=0)


def whiten_group(cells):
    dates, looks = cells[0].shape[0] // 2, cells[0].shape[1]
    row = lax.broadcasted_iota(jnp.int32, (dates, dates), 0)
    col = lax.broadcasted_iota(jnp.int32, (dates, dates), 1)
    diagonal = row == col
    grams = []
    for cell in cells:
        real_part, imag_part = cell[:dates], cell[dates:]
        straight = jnp.concatenate([real_part, imag_part], axis=1)
        turned = jnp.concatenate([imag_part, -real_part], axis=1)
        left = jnp.concatenate([straight, turned], axis=0)
        grams.append(
            lax.dot_general(left, straight, (((1,), (1,)), ((), ())), preferred_element_type=jnp.float32)
        )
    scaled, bounds = [], []
    for gram in grams:
        gram_re, gram_im = gram[:dates], gram[dates:]
        power = jnp.where(diagonal, gram_re, 0.0)
        row_scale = lax.rsqrt(jnp.sum(power, axis=1, keepdims=True) * (1.0 / looks) + small_eps)
        col_scale = lax.rsqrt(jnp.sum(power, axis=0, keepdims=True) * (1.0 / looks) + small_eps)
        col_scale = col_scale * (1.0 / looks)
        size = (jnp.abs(gram_re) + jnp.abs(gram_im)) * row_scale
        sums = jnp.sum(size, axis=0, keepdims=True) * col_scale + diag_load
        inv_bound = 1.0 / jnp.max(sums, axis=1, keepdims=True)
        factor = row_scale * (col_scale * inv_bound)
        load = jnp.where(diagonal, diag_load * inv_bound, 0.0)
        scaled.append(jnp.concatenate([gram_re * factor + load, gram_im * factor], axis=0))
        bounds.append(inv_bound)
    values = [cell.astype(jnp.float32) for cell in cells]
    rounded = list(cells)
    for sweep in range(2):
        mats = [s.astype(jnp.bfloat16) for s in scaled]
        products = [
            jnp.dot(
                embedded(m[:dates], m[dates:]),
                jnp.concatenate([m, r], axis=1),
                preferred_element_type=jnp.float32,
            )
            for m, r in zip(mats, rounded)
        ]
        scaled = [2.0 * s - p[:, :dates] for s, p in zip(scaled, products)]
        values = [2.0 * v - p[:, dates:] for v, p in zip(values, products)]
        rounded = [v.astype(jnp.bfloat16) for v in values]
    mats = [s.astype(jnp.bfloat16) for s in scaled]
    products = [
        jnp.dot(embedded(m[:dates], m[dates:]), r, preferred_element_type=jnp.float32)
        for m, r in zip(mats, rounded)
    ]
    return [
        ((2.0 * v - p) * b).astype(jnp.bfloat16) for v, p, b in zip(values, products, bounds)
    ]


def whiten_kernel(slots, lines, packed, windows, *, mixed):
    senders, line_count, part_rows, ranges_count = lines.shape
    dates = windows.shape[1] // 2
    sides = ranges_count // TILE
    lane_block = lax.broadcasted_iota(jnp.int32, (1, TILE), 1) // PATCH_RG
    per_side = TILE // PATCH_RG
    for side in range(sides):
        lanes = pl.ds(side * TILE, TILE)
        if mixed:
            half = part_rows // 2
            for first in range(0, senders, 2):
                blocks = [
                    lines[first : first + 2, a, :, lanes].astype(jnp.float32) for a in range(line_count)
                ]
                found = barrel(blocks, lane_block[:, None])
                rows = pl.ds(first * half, 2 * half)
                rows_im = pl.ds(dates + first * half, 2 * half)
                for w in range(per_side):
                    block = found[-w % per_side]
                    real_part = block[:, :half].reshape(2 * half, TILE)
                    imag_part = block[:, half:].reshape(2 * half, TILE)
                    windows[side * per_side + w, rows, :] = real_part.astype(jnp.bfloat16)
                    windows[side * per_side + w, rows_im, :] = imag_part.astype(jnp.bfloat16)
        else:
            for first in range(0, 2 * dates, 16):
                rows = pl.ds(first, 16)
                blocks = [lines[0, a, rows, lanes].astype(jnp.float32) for a in range(line_count)]
                found = barrel(blocks, lane_block)
                for w in range(per_side):
                    windows[side * per_side + w, rows, :] = found[-w % per_side].astype(jnp.bfloat16)

    def group_step(step, carry):
        first = step * GROUP
        results = whiten_group([windows[first + k] for k in range(GROUP)])
        for k in range(GROUP):
            windows[first + k] = results[k]
        return carry

    lax.fori_loop(0, windows.shape[0] // GROUP, group_step, 0)
    for side in range(sides):
        for first in range(0, 2 * dates, 16):
            rows = pl.ds(first, 16)
            blocks = [
                windows[side * per_side + w, rows, :].astype(jnp.float32) for w in range(per_side)
            ]
            found = barrel(blocks, lane_block)
            for a in range(line_count):
                packed[slots[a * sides + side], rows, :] = found[-a % per_side].astype(jnp.bfloat16)


def map_kernel(order, targets, starts, count, kernel, scales, got, out, circulant):
    source = lax.broadcasted_iota(jnp.int32, circulant.shape, 0)
    column = lax.broadcasted_iota(jnp.int32, circulant.shape, 1)
    lag = (source - column) & (TILE - 1)
    taps = jnp.zeros(circulant.shape, jnp.float32)
    for k in range(KW):
        taps = jnp.where(lag == k, kernel[k], taps)
    circulant[...] = taps
    out[...] = jnp.zeros(out.shape, jnp.float32)

    def pair_step(step, carry):
        products = []
        for k in range(2):
            at = step * 2 + k
            matrix = circulant[pl.ds(starts[at], TILE), :].astype(jnp.bfloat16)
            products.append(
                jnp.dot(got[order[at]], matrix, preferred_element_type=jnp.float32) * scales[at]
            )
        for k in range(2):
            target = targets[step * 2 + k]
            out[target] = out[target] + products[k]
        return carry

    lax.fori_loop(0, (count[0] + 1) // 2, pair_step, 0)


def shards(
    radar_stack,
    filter_taps,
    filter_lengths,
    resample_kernel,
    tile_owner,
    map_slot,
    correlation,
    offsets,
):
    peers = lax.axis_size("date")
    me = lax.axis_index("date")
    _, dates_here, rows_count, ranges_count = radar_stack.shape
    dates = dates_here * peers
    line_count = rows_count // peers
    sides = ranges_count // TILE
    tile_count = line_count * sides
    slot_count = peers * CAP
    window_count = (line_count // PATCH_AZ) * (ranges_count // PATCH_RG)
    assert line_count == PATCH_AZ

    owners = tile_owner[:, 0]
    tile_iota = jnp.arange(tile_count, dtype=jnp.int32)
    starts_here = offsets + PATCH_RG * (tile_iota // sides)
    earlier = jnp.logical_and(
        owners[:, None] == owners[None, :], tile_iota[None, :] < tile_iota[:, None]
    )
    slots = owners * CAP + jnp.sum(earlier, axis=1).astype(jnp.int32)
    details = jnp.stack([slots, map_slot, starts_here, correlation], axis=0)[None]

    sent = pl.pallas_call(
        filter_kernel,
        out_shape=jax.ShapeDtypeStruct((rows_count * 2 * dates_here, ranges_count), jnp.bfloat16),
        in_specs=[SMEM, VMEM, VMEM],
        out_specs=VMEM,
        scratch_shapes=[pltpu.VMEM((sides, rows_count * 2 * dates_here, TILE), jnp.float32)],
        compiler_params=params,
        name="filter",
    )(filter_lengths, filter_taps, radar_stack)
    sent = sent.reshape(peers, line_count * 2 * dates_here, ranges_count)
    got_lines = lax.all_to_all(sent, "date", split_axis=0, concat_axis=0, tiled=True)
    all_details = lax.all_gather(details, "date", axis=0, tiled=True)

    mixed = dates_here == 8 and peers % 2 == 0
    got_lines = got_lines.reshape(peers, line_count, 2 * dates_here, ranges_count)
    if not mixed:
        got_lines = got_lines.reshape(peers, line_count, 2, dates_here, ranges_count)
        got_lines = got_lines.transpose(1, 2, 0, 3, 4).reshape(1, line_count, 2 * dates, ranges_count)
    packed = pl.pallas_call(
        partial(whiten_kernel, mixed=mixed),
        out_shape=jax.ShapeDtypeStruct((slot_count, 2 * dates, TILE), jnp.bfloat16),
        in_specs=[SMEM, VMEM],
        out_specs=VMEM,
        scratch_shapes=[pltpu.VMEM((window_count, 2 * dates, TILE), jnp.bfloat16)],
        compiler_params=params,
        name="whiten",
    )(slots, got_lines)
    packed = packed.reshape(peers, CAP, 2 * dates, TILE)
    got_tiles = lax.all_to_all(packed, "date", split_axis=0, concat_axis=0, tiled=True)
    got_tiles = got_tiles.reshape(slot_count, 2 * dates, TILE)

    here = me * CAP + jnp.arange(CAP, dtype=jnp.int32)
    match = (all_details[:, None, 0, :] == here[None, :, None]).reshape(slot_count, tile_count)
    fields = jnp.repeat(all_details[:, 1:], CAP, axis=0).reshape(slot_count, 3, tile_count)
    chosen = jnp.sum(jnp.where(match[:, None, :], fields, 0), axis=2)
    filled = jnp.any(match, axis=1)
    weights = chosen[:, 2].astype(jnp.float32)
    map_iota = jnp.arange(MAP_DEV, dtype=jnp.int32)
    on_map = jnp.logical_and(chosen[:, 0][:, None] == map_iota[None, :], filled[:, None])
    sums = jnp.sum(jnp.where(on_map, weights[:, None], 0.0), axis=0)
    scale = jnp.sum(jnp.where(on_map, 1.0 / jnp.maximum(sums, 1.0)[None, :], 0.0), axis=1) * weights
    slot_iota = jnp.arange(slot_count, dtype=jnp.int32)
    place = jnp.sum(jnp.logical_and(filled[None, :], slot_iota[None, :] < slot_iota[:, None]), axis=1)
    count = jnp.sum(filled).astype(jnp.int32)
    taken = jnp.logical_and(place[None, :] == slot_iota[:, None], filled[None, :])

    def listed(values, empty):
        return jnp.where(
            slot_iota < count, jnp.sum(jnp.where(taken, values[None, :], 0), axis=1), empty
        )

    first = jnp.min(jnp.where(filled, slot_iota, slot_count - 1))
    order = listed(slot_iota, first)
    targets = listed(chosen[:, 0], 0)
    begins = listed((TILE - chosen[:, 1]) & (TILE - 1), 0)
    scales = listed(scale, 0.0)
    rounded_kernel = lax.optimization_barrier(resample_kernel.astype(jnp.bfloat16)).astype(jnp.float32)

    return pl.pallas_call(
        map_kernel,
        out_shape=jax.ShapeDtypeStruct((MAP_DEV, 2 * dates, TILE), jnp.float32),
        in_specs=[SMEM, SMEM, SMEM, SMEM, SMEM, SMEM, VMEM],
        out_specs=VMEM,
        scratch_shapes=[pltpu.VMEM((2 * TILE, TILE), jnp.float32)],
        compiler_params=params,
        name="map",
    )(order, targets, begins, count[None], rounded_kernel, scales, got_tiles)


def solution(mesh):
    in_specs = (
        P(None, "date", "grp", None),
        P(None, "date", None),
        P("date"),
        P(),
        P(("grp", "date"), None),
        P(("grp", "date")),
        P(("grp", "date")),
        P(("grp", "date")),
    )
    out_specs = P(("grp", "date"), None, None)
    return jax.shard_map(shards, mesh=mesh, in_specs=in_specs, out_specs=out_specs, check_vma=False)
```

profile of v0, /device:TPU:17, one launch (start us, length us, event | category | flops | bytes accessed | tf_op | source)
XLA Modules:
  0.0 117.8 jit_solution(17677986856081543691)
XLA Ops:
  0.0 1.2 %copy-done.1 = bf16[2,8,128,256]{3,2,1,0:T(8,128)(2,1)S(1)} copy-done((bf16[2,8,128,256]{3,2,1,0:T(8,128)(2,1)S(1)}, bf16[2,8,128,256]{3,2,1,0:T(8,128)(2,1)}, u32[]{:S(2)}) %copy-start.1) | copy-done | bytes 1048600
  1.2 0.7 copy-done.2
  1.9 0.7 copy-done.3
  2.6 3.7 %filter.1 = bf16[2048,256]{1,0:T(8,128)(2,1)} custom-call(s32[8]{0:T(128)S(1)} %copy-done.3, f32[2,8,128]{2,1,0:T(8,128)S(1)} %copy-done.2, bf16[2,8,128,256]{3,2,1,0:T(8,128)(2,1)S(1)} %copy-done.1), custom_call_target="tpu_custom_call" | custom-call | tf_op jit(solution)/shard_map/filter/pallas_call | solution.py:228
  6.3 6.5 %all-to-all-start = ((bf16[16,128,256]{2,1,0:T(8,128)(2,1)}), bf16[16,128,256]{2,1,0:T(8,128)(2,1)S(1)}, u32[]{:S(2)}, u32[]{:S(2)}) async-start(bf16[16,128,256]{2,1,0:T(8,128)(2,1)} %bitcast.12), calls=%async_computation | async-start | bytes 2097152 | tf_op jit(solution)/shard_map/all_to_all | solution.py:238
  12.8 0.2 convert_reduce_fusion.1
  13.0 24.5 %all-to-all-done = bf16[16,128,256]{2,1,0:T(8,128)(2,1)S(1)} async-done(((bf16[16,128,256]{2,1,0:T(8,128)(2,1)}), bf16[16,128,256]{2,1,0:T(8,128)(2,1)S(1)}, u32[]{:S(2)}, u32[]{:S(2)}) %all-to-all-start) | async-done | bytes 1048608 | tf_op jit(solution)/shard_map/all_to_all | solution.py:238
  37.4 5.9 %whiten.1 = bf16[32,256,128]{2,1,0:T(8,128)(2,1)S(1)} custom-call(s32[16]{0:T(128)S(1)} %multiply_add_fusion.slots, bf16[16,8,16,256]{3,2,1,0:T(8,128)(2,1)S(1)} %bitcast.30), custom_call_target="tpu_custom_call" | custom-call | tf_op jit(solution)/shard_map/whiten/pallas_call | solution.py:246
  43.3 1.3 %copy-done = bf16[32,256,128]{2,1,0:T(8,128)(2,1)} copy-done((bf16[32,256,128]{2,1,0:T(8,128)(2,1)}, bf16[32,256,128]{2,1,0:T(8,128)(2,1)S(1)}, u32[]{:S(2)}) %copy-start) | copy-done | bytes 2097176
  44.7 5.3 %all-to-all-start.1 = ((bf16[16,2,256,128]{3,2,1,0:T(8,128)(2,1)}), bf16[16,2,256,128]{3,2,1,0:T(8,128)(2,1)S(1)}, u32[]{:S(2)}, u32[]{:S(2)}) async-start(bf16[16,2,256,128]{3,2,1,0:T(8,128)(2,1)} %bitcast.29), calls=%async_computation.1 | async-start | bytes 4194304 | tf_op jit(solution)/shard_map/all_to_all | solution.py:256
  50.0 57.8 %all-gather.1 = s32[16,4,16]{2,1,0:T(4,128)S(1)} all-gather(s32[1,4,16]{2,1,0:T(4,128)S(1)} %add_bitcast_fusion), channel_id=2, replica_groups=mesh['grp'=2,'date'=16] {'date'}, dimensions={0}, use_global_device_ids=true | all-gather | bytes 4352 | tf_op jit(solution)/shard_map/all_gather | solution.py:239
  107.8 0.2 fusion.12
  108.0 0.2 select_reduce_fusion
  108.4 0.1 copy.9
  108.5 0.1 and.48
  108.7 0.1 select_reduce_fusion.6
  108.8 0.6 convert_reduce_fusion.2
  109.4 0.1 convert_reduce_fusion
  109.6 0.1 select_reduce_fusion.1
  109.8 0.2 select_reduce_fusion.2
  109.9 0.6 fusion.7.scales
  110.5 1.3 %fusion.10.order = s32[32]{0:T(128)S(1)} fusion(s32[32]{0:T(128)S(1)} %get-tuple-element.7, s32[]{:T(128)} %get-tuple-element.9, s32[]{:T(128)} %get-tuple-element.8), kind=kLoop, calls=%fused_computation.39 | loop fusion | flops 64 | bytes 264 | tf_op jit(solution)/shard_map/jit(_where)/select_n | solution.py:275
  111.8 0.6 fusion.8
  112.5 5.3 %map.1 = f32[8,256,128]{2,1,0:T(8,128)} custom-call(s32[32]{0:T(128)S(1)} %fusion.10.order, s32[32]{0:T(128)S(1)} %get-tuple-element.16.targets, s32[32]{0:T(128)S(1)} %get-tuple-element.15.starts, s32[1]{0:T(128)} %bitcast.10.count, f32[4]{0:T(128)S(1)} %convert_element_type.31.kernel, f32[32]{0:T(128)S(1)} %fusion.7.scales, bf16[32,256,128]{2,1,0:T(8,128)(2,1)S(1)} %bitcast.28), custom_call_target="tpu_custom_call" | custom-call | tf_op jit(solution)/shard_map/map/pallas_call | solution.py:286
  (31 shorter events, 0.4 us)
Async XLA Ops:
  0.0 1.2 %copy-start.1 = (bf16[2,8,128,256]{3,2,1,0:T(8,128)(2,1)S(1)}, bf16[2,8,128,256]{3,2,1,0:T(8,128)(2,1)}, u32[]{:S(2)}) copy-start(bf16[2,8,128,256]{3,2,1,0:T(8,128)(2,1)} %radar.1) | copy-start | bytes 3145732
  1.2 0.7 copy-start.2
  1.9 0.7 copy-start.3
  2.6 10.2 %copy-start.7 = (s32[16,1]{0,1:T(1,128)S(1)}, s32[16,1]{0,1:T(1,128)}, u32[]{:S(2)}) copy-start(s32[16,1]{0,1:T(1,128)} %param.12) | copy-start | bytes 196
  6.3 31.2 %all-to-all-start = ((bf16[16,128,256]{2,1,0:T(8,128)(2,1)}), bf16[16,128,256]{2,1,0:T(8,128)(2,1)S(1)}, u32[]{:S(2)}, u32[]{:S(2)}) async-start(bf16[16,128,256]{2,1,0:T(8,128)(2,1)} %bitcast.12), calls=%async_computation | async-start | bytes 2097152 | tf_op jit(solution)/shard_map/all_to_all | solution.py:238
  43.3 1.4 %copy-start = (bf16[32,256,128]{2,1,0:T(8,128)(2,1)}, bf16[32,256,128]{2,1,0:T(8,128)(2,1)S(1)}, u32[]{:S(2)}) copy-start(bf16[32,256,128]{2,1,0:T(8,128)(2,1)S(1)} %whiten.1) | copy-start | bytes 6291460
  44.7 5.3 %copy-start.6 = (s32[16]{0:T(128)S(1)}, s32[16]{0:T(128)}, u32[]{:S(2)}) copy-start(s32[16]{0:T(128)} %param.15) | copy-start | bytes 196
  44.7 5.3 %copy-start.4 = (s32[16]{0:T(128)S(1)}, s32[16]{0:T(128)}, u32[]{:S(2)}) copy-start(s32[16]{0:T(128)} %param.14) | copy-start | bytes 196
  44.7 5.3 %copy-start.5 = (s32[16]{0:T(128)S(1)}, s32[16]{0:T(128)}, u32[]{:S(2)}) copy-start(s32[16]{0:T(128)} %param.13) | copy-start | bytes 196
  44.7 63.9 %copy-start.8 = (f32[4]{0:T(128)S(1)}, f32[4]{0:T(128)}, u32[]{:S(2)}) copy-start(f32[4]{0:T(128)} %param.11) | copy-start | bytes 52
  44.7 67.8 %all-to-all-start.1 = ((bf16[16,2,256,128]{3,2,1,0:T(8,128)(2,1)}), bf16[16,2,256,128]{3,2,1,0:T(8,128)(2,1)S(1)}, u32[]{:S(2)}, u32[]{:S(2)}) async-start(bf16[16,2,256,128]{3,2,1,0:T(8,128)(2,1)} %bitcast.29), calls=%async_computation.1 | async-start | bytes 4194304 | tf_op jit(solution)/shard_map/all_to_all | solution.py:256
where the time goes:
time: 118 us
  blocking collectives  57.8 us (49%)
  waiting for transfers between devices  24.5 us (21%)
  Pallas kernels  14.9 us (13%)
  starting transfers between devices  11.8 us (10%)
  local copies, waits for them, and re-layouts  4.35 us (4%)
  other arithmetic  4.35 us (4%)
    all_gather x1, blocking collectives, shards(): all_details = lax.all_gather(details, 'date', axis=0, tiled=True)  57.8 us
    all_to_all x1, waiting for transfers between devices, shards(): lax.all_to_all(sent, 'date', split_axis=0, concat_axis=0, tiled=True)  24.5 us
    all_to_all x1, starting transfers between devices, shards(): lax.all_to_all(sent, 'date', split_axis=0, concat_axis=0, tiled=True)  6.49 us
    pallas_call x1, Pallas kernels, shards(): pl.pallas_call(partial(whiten_kernel, mixed=mixed), out_shape=jax.ShapeDt...  5.87 us
    pallas_call x1, Pallas kernels, shards(): pl.pallas_call(map_kernel, out_shape=jax.ShapeDtypeStruct((MAP_DEV, 2 * d...  5.3 us
    all_to_all x1, starting transfers between devices, shards(): lax.all_to_all(packed, 'date', split_axis=0, concat_axis=0, tiled=True)  5.29 us
    unnamed x18, local copies, waits for them, and re-layouts  3.94 us
    pallas_call x1, Pallas kernels, shards(): pl.pallas_call(filter_kernel, out_shape=jax.ShapeDtypeStruct((rows_count...  3.69 us
  transfers between devices with their start and end apart: 2, of which 1 were waited for; matrix products, arithmetic and copies ran while one was open for 4% of the time, Pallas kernels for 0%

commit v1 on v0

--- a/solution.py
+++ b/solution.py
@@ -14,18 +14,35 @@
 CAP = 2
 MAP_DEV = 8
 GROUP = 4
+PIECES = 4
+ARRIVALS = 4
 
 diag_load = 0.5
 small_eps = 1e-05
 VMEM = pl.BlockSpec(memory_space=pltpu.VMEM)
 SMEM = pl.BlockSpec(memory_space=pltpu.SMEM)
-params = pltpu.CompilerParams(vmem_limit_bytes=48 * 1024 * 1024)
-
-
-def filter_kernel(lengths, taps, radar, sent, staged):
+HBM = pl.BlockSpec(memory_space=pltpu.HBM)
+MIB = 1024 * 1024
+params = pltpu.CompilerParams(vmem_limit_bytes=32 * MIB)
+wide_params = pltpu.CompilerParams(vmem_limit_bytes=60 * MIB)
+
+
+def filter_kernel(lengths_hbm, taps_hbm, radar, sent, lengths, taps, columns, staged, rounded, sems, out_sems):
     _, dates_here, rows_count, ranges_count = radar.shape
     tap_count = taps.shape[2]
     period = rows_count + tap_count
+    copy_lengths = pltpu.make_async_copy(lengths_hbm, lengths, sems.at[dates_here])
+    copy_taps = pltpu.make_async_copy(taps_hbm, taps, sems.at[dates_here + 1])
+    copies = [
+        pltpu.make_async_copy(radar.at[:, date], columns.at[date], sems.at[date])
+        for date in range(dates_here)
+    ]
+    copy_lengths.start()
+    copy_taps.start()
+    for copy in copies:
+        copy.start()
+    copy_lengths.wait()
+    copy_taps.wait()
     position = lax.broadcasted_iota(jnp.int32, (1, tap_count), 1)
     for date in range(dates_here):
         mats = []
@@ -36,18 +53,27 @@
             rolled = pltpu.roll(spread, period - tap_count // 2, 1, stride=1, stride_axis=0)
             mats.append(rolled[:, :rows_count])
         real_mat, imag_mat = mats
-        columns = radar[:, date].reshape(2 * rows_count, ranges_count)
+        copies[date].wait()
+        cells = columns[date].reshape(2 * rows_count, ranges_count)
         for part, halves in enumerate(((real_mat, -imag_mat), (imag_mat, real_mat))):
             operator = jnp.concatenate(halves, axis=1).astype(jnp.bfloat16)
-            product = jnp.dot(operator, columns, preferred_element_type=jnp.float32)
+            product = jnp.dot(operator, cells, preferred_element_type=jnp.float32)
             for side in range(ranges_count // TILE):
                 skewed = pltpu.roll(
                     product[:, side * TILE : (side + 1) * TILE], 0, 1, stride=PATCH_RG, stride_axis=0
                 )
                 first = part * dates_here + date
                 staged[side, pl.ds(first, rows_count, stride=2 * dates_here), :] = skewed
-    for side in range(ranges_count // TILE):
-        sent[:, side * TILE : (side + 1) * TILE] = staged[side].astype(jnp.bfloat16)
+    total = sent.shape[0]
+    pieces = []
+    for piece in range(PIECES):
+        rows = pl.ds(piece * (total // PIECES), total // PIECES)
+        for side in range(ranges_count // TILE):
+            rounded[rows, side * TILE : (side + 1) * TILE] = staged[side, rows, :].astype(jnp.bfloat16)
+        pieces.append(pltpu.make_async_copy(rounded.at[rows], sent.at[rows], out_sems.at[piece]))
+        pieces[-1].start()
+    for piece in pieces:
+        piece.wait()
 
 
 def barrel(blocks, lane_block):
@@ -119,7 +145,7 @@
     ]
 
 
-def whiten_kernel(slots, lines, packed, windows, *, mixed):
+def whiten_kernel(slots, lines, packed, windows, tiles, sems, *, mixed):
     senders, line_count, part_rows, ranges_count = lines.shape
     dates = windows.shape[1] // 2
     sides = ranges_count // TILE
@@ -158,6 +184,7 @@
         return carry
 
     lax.fori_loop(0, windows.shape[0] // GROUP, group_step, 0)
+    copies = []
     for side in range(sides):
         for first in range(0, 2 * dates, 16):
             rows = pl.ds(first, 16)
@@ -166,10 +193,17 @@
             ]
             found = barrel(blocks, lane_block)
             for a in range(line_count):
-                packed[slots[a * sides + side], rows, :] = found[-a % per_side].astype(jnp.bfloat16)
+                tiles[a * sides + side, rows, :] = found[-a % per_side].astype(jnp.bfloat16)
+        for a in range(line_count):
+            at = a * sides + side
+            copies.append(pltpu.make_async_copy(tiles.at[at], packed.at[slots[at]], sems.at[at]))
+            copies[-1].start()
+    for copy in copies:
+        copy.wait()
 
 
 def map_kernel(order, targets, starts, count, kernel, scales, got, out, circulant):
+    found = count[0]
     source = lax.broadcasted_iota(jnp.int32, circulant.shape, 0)
     column = lax.broadcasted_iota(jnp.int32, circulant.shape, 1)
     lag = (source - column) & (TILE - 1)
@@ -179,20 +213,36 @@
     circulant[...] = taps
     out[...] = jnp.zeros(out.shape, jnp.float32)
 
-    def pair_step(step, carry):
+    def group_step(step, carry):
+        first = step * ARRIVALS
         products = []
-        for k in range(2):
-            at = step * 2 + k
+        for k in range(ARRIVALS):
+            at = first + k
             matrix = circulant[pl.ds(starts[at], TILE), :].astype(jnp.bfloat16)
-            products.append(
-                jnp.dot(got[order[at]], matrix, preferred_element_type=jnp.float32) * scales[at]
-            )
-        for k in range(2):
-            target = targets[step * 2 + k]
+            product = jnp.dot(got[order[at]], matrix, preferred_element_type=jnp.float32)
+            products.append(product * scales[at])
+        for k in range(ARRIVALS):
+            target = targets[first + k]
             out[target] = out[target] + products[k]
         return carry
 
-    lax.fori_loop(0, (count[0] + 1) // 2, pair_step, 0)
+    lax.fori_loop(0, (found + ARRIVALS - 1) // ARRIVALS, group_step, 0)
+
+
+def gathered(block, axis_name):
+    peers = lax.axis_size(axis_name)
+    if peers & (peers - 1):
+        return lax.all_gather(block, axis_name, axis=0, tiled=True)
+    me = lax.axis_index(axis_name)
+    step = 1
+    while step < peers:
+        other = lax.ppermute(block, axis_name, [(i, i ^ step) for i in range(peers)])
+        lower = (me & step) == 0
+        block = jnp.where(
+            lower, jnp.concatenate([block, other], axis=0), jnp.concatenate([other, block], axis=0)
+        )
+        step *= 2
+    return block
 
 
 def shards(
@@ -216,6 +266,26 @@
     window_count = (line_count // PATCH_AZ) * (ranges_count // PATCH_RG)
     assert line_count == PATCH_AZ
 
+    sent = pl.pallas_call(
+        filter_kernel,
+        out_shape=pltpu.HBM((rows_count * 2 * dates_here, ranges_count), jnp.bfloat16),
+        in_specs=[HBM, HBM, HBM],
+        out_specs=HBM,
+        scratch_shapes=[
+            pltpu.SMEM((dates_here,), jnp.int32),
+            pltpu.VMEM(filter_taps.shape, jnp.float32),
+            pltpu.VMEM((dates_here, 2, rows_count, ranges_count), jnp.bfloat16),
+            pltpu.VMEM((sides, rows_count * 2 * dates_here, TILE), jnp.float32),
+            pltpu.VMEM((rows_count * 2 * dates_here, ranges_count), jnp.bfloat16),
+            pltpu.SemaphoreType.DMA((dates_here + 2,)),
+            pltpu.SemaphoreType.DMA((PIECES,)),
+        ],
+        compiler_params=wide_params,
+        name="filter",
+    )(filter_lengths, filter_taps, radar_stack)
+    sent, tile_owner, map_slot, correlation, offsets = lax.optimization_barrier(
+        (sent, tile_owner, map_slot, correlation, offsets)
+    )
     owners = tile_owner[:, 0]
     tile_iota = jnp.arange(tile_count, dtype=jnp.int32)
     starts_here = offsets + PATCH_RG * (tile_iota // sides)
@@ -224,19 +294,9 @@
     )
     slots = owners * CAP + jnp.sum(earlier, axis=1).astype(jnp.int32)
     details = jnp.stack([slots, map_slot, starts_here, correlation], axis=0)[None]
-
-    sent = pl.pallas_call(
-        filter_kernel,
-        out_shape=jax.ShapeDtypeStruct((rows_count * 2 * dates_here, ranges_count), jnp.bfloat16),
-        in_specs=[SMEM, VMEM, VMEM],
-        out_specs=VMEM,
-        scratch_shapes=[pltpu.VMEM((sides, rows_count * 2 * dates_here, TILE), jnp.float32)],
-        compiler_params=params,
-        name="filter",
-    )(filter_lengths, filter_taps, radar_stack)
     sent = sent.reshape(peers, line_count * 2 * dates_here, ranges_count)
     got_lines = lax.all_to_all(sent, "date", split_axis=0, concat_axis=0, tiled=True)
-    all_details = lax.all_gather(details, "date", axis=0, tiled=True)
+    all_details = gathered(details, "date")
 
     mixed = dates_here == 8 and peers % 2 == 0
     got_lines = got_lines.reshape(peers, line_count, 2 * dates_here, ranges_count)
@@ -245,13 +305,18 @@
         got_lines = got_lines.transpose(1, 2, 0, 3, 4).reshape(1, line_count, 2 * dates, ranges_count)
     packed = pl.pallas_call(
         partial(whiten_kernel, mixed=mixed),
-        out_shape=jax.ShapeDtypeStruct((slot_count, 2 * dates, TILE), jnp.bfloat16),
+        out_shape=pltpu.HBM((slot_count, 2 * dates, TILE), jnp.bfloat16),
         in_specs=[SMEM, VMEM],
-        out_specs=VMEM,
-        scratch_shapes=[pltpu.VMEM((window_count, 2 * dates, TILE), jnp.bfloat16)],
+        out_specs=HBM,
+        scratch_shapes=[
+            pltpu.VMEM((window_count, 2 * dates, TILE), jnp.bfloat16),
+            pltpu.VMEM((tile_count, 2 * dates, TILE), jnp.bfloat16),
+            pltpu.SemaphoreType.DMA((tile_count,)),
+        ],
         compiler_params=params,
         name="whiten",
     )(slots, got_lines)
+    packed, all_details = lax.optimization_barrier((packed, all_details))
     packed = packed.reshape(peers, CAP, 2 * dates, TILE)
     got_tiles = lax.all_to_all(packed, "date", split_axis=0, concat_axis=0, tiled=True)
     got_tiles = got_tiles.reshape(slot_count, 2 * dates, TILE)

time: 118 us -> 101 us (0.86)
  the two profiles are of different devices: /device:TPU:17 before, /device:TPU:13 now
where the time goes in v1:
time: 101 us
  waiting for transfers between devices  66 us (65%)
  Pallas kernels  15.6 us (15%)
  starting transfers between devices  14 us (14%)
  other arithmetic  4.37 us (4%)
    all_to_all x1, waiting for transfers between devices, shards(): lax.all_to_all(packed, 'date', split_axis=0, concat_axis=0, tiled=True)  42.8 us
    ppermute x4, waiting for transfers between devices, gathered(): lax.ppermute(block, axis_name, [(i, i ^ step) for i in range(peers)])  21.1 us
    pallas_call x1, Pallas kernels, shards(): pl.pallas_call(partial(whiten_kernel, mixed=mixed), out_shape=pltpu.HBM((...  6.89 us
    all_to_all x1, starting transfers between devices, shards(): lax.all_to_all(sent, 'date', split_axis=0, concat_axis=0, tiled=True)  6.56 us
    all_to_all x1, starting transfers between devices, shards(): lax.all_to_all(packed, 'date', split_axis=0, concat_axis=0, tiled=True)  5.6 us
    pallas_call x1, Pallas kernels, shards(): pl.pallas_call(filter_kernel, out_shape=pltpu.HBM((rows_count * 2 * dates...  4.55 us
    pallas_call x1, Pallas kernels, shards(): pl.pallas_call(map_kernel, out_shape=jax.ShapeDtypeStruct((MAP_DEV, 2 * d...  4.15 us
    select_n x3, other arithmetic, listed(): jnp.where(slot_iota < count, jnp.sum(jnp.where(taken, values[None, :], 0)...  2.51 us
  transfers between devices with their start and end apart: 6, of which 6 were waited for; matrix products, arithmetic and copies ran while one was open for 5% of the time, Pallas kernels for 0%

profile of v1, /device:TPU:13, one launch (start us, length us, event | category | flops | bytes accessed | tf_op | source)
XLA Modules:
  0.0 100.6 jit_solution(10539456692444707473)
XLA Ops:
  0.0 4.6 %filter.1 = bf16[2048,256]{1,0:T(8,128)(2,1)} custom-call(s32[8]{0:T(128)} %lengths_hbm.1, f32[2,8,128]{2,1,0:T(8,128)} %taps_hbm.1, bf16[2,8,128,256]{3,2,1,0:T(8,128)(2,1)} %radar.1), custom_call_target="tpu_custom_call" | custom-call | tf_op jit(solution)/shard_map/filter/pallas_call | solution.py:269
  4.6 6.6 %all-to-all-start = ((bf16[16,128,256]{2,1,0:T(8,128)(2,1)}), bf16[16,128,256]{2,1,0:T(8,128)(2,1)S(1)}, u32[]{:S(2)}, u32[]{:S(2)}) async-start(bf16[16,128,256]{2,1,0:T(8,128)(2,1)} %bitcast.31), calls=%async_computation | async-start | bytes 2097152 | tf_op jit(solution)/shard_map/all_to_all | solution.py:298
  11.2 0.2 convert_reduce_fusion.1
  11.4 0.4 collective-permute-start
  11.8 0.8 collective-permute-done
  12.7 0.3 collective-permute-start.1
  12.9 3.8 %collective-permute-done.1 = s32[2,4,16]{2,1,0:T(4,128)S(1)} collective-permute-done((s32[2,4,16]{2,1,0:T(4,128)S(1)}, s32[2,4,16]{2,1,0:T(4,128)S(1)}, u32[]{:S(2)}, u32[]{:S(2)}) %collective-permute-start.1) | collective-permute-done | bytes 544 | tf_op jit(solution)/shard_map/ppermute | solution.py:239
  16.7 12.8 %collective-permute-done.2 = s32[4,4,16]{2,1,0:T(4,128)S(1)} collective-permute-done((s32[4,4,16]{2,1,0:T(4,128)S(1)}, s32[4,4,16]{2,1,0:T(4,128)S(1)}, u32[]{:S(2)}, u32[]{:S(2)}) %collective-permute-start.2) | collective-permute-done | bytes 1056 | tf_op jit(solution)/shard_map/ppermute | solution.py:239
  29.5 1.1 %collective-permute-start.3 = (s32[8,4,16]{2,1,0:T(4,128)S(1)}, s32[8,4,16]{2,1,0:T(4,128)S(1)}, u32[]{:S(2)}, u32[]{:S(2)}) collective-permute-start(s32[8,4,16]{2,1,0:T(4,128)S(1)} %add_select_fusion.1), channel_id=1, source_target_pairs={{0,8},{1,9},{2,10},{3,11},{4,12},{5,13},{6,14},{7,15},{8,0},{9,1},... | collective-permute-start | bytes 6152 | tf_op jit(solution)/shard_map/ppermute | solution.py:239
  30.7 3.8 %collective-permute-done.3 = s32[8,4,16]{2,1,0:T(4,128)S(1)} collective-permute-done((s32[8,4,16]{2,1,0:T(4,128)S(1)}, s32[8,4,16]{2,1,0:T(4,128)S(1)}, u32[]{:S(2)}, u32[]{:S(2)}) %collective-permute-start.3) | collective-permute-done | bytes 2080 | tf_op jit(solution)/shard_map/ppermute | solution.py:239
  34.4 2.1 %all-to-all-done = bf16[16,128,256]{2,1,0:T(8,128)(2,1)S(1)} async-done(((bf16[16,128,256]{2,1,0:T(8,128)(2,1)}), bf16[16,128,256]{2,1,0:T(8,128)(2,1)S(1)}, u32[]{:S(2)}, u32[]{:S(2)}) %all-to-all-start) | async-done | bytes 1048608 | tf_op jit(solution)/shard_map/all_to_all | solution.py:298
  36.5 6.9 %whiten.1 = bf16[32,256,128]{2,1,0:T(8,128)(2,1)} custom-call(s32[16]{0:T(128)S(1)} %multiply_add_fusion.slots, bf16[16,8,16,256]{3,2,1,0:T(8,128)(2,1)S(1)} %bitcast.29), custom_call_target="tpu_custom_call" | custom-call | tf_op jit(solution)/shard_map/whiten/pallas_call | solution.py:306
  43.5 5.6 %all-to-all-start.1 = ((bf16[16,2,256,128]{3,2,1,0:T(8,128)(2,1)}), bf16[16,2,256,128]{3,2,1,0:T(8,128)(2,1)S(1)}, u32[]{:S(2)}, u32[]{:S(2)}) async-start(bf16[16,2,256,128]{3,2,1,0:T(8,128)(2,1)} %bitcast.30), calls=%async_computation.1 | async-start | bytes 4194304 | tf_op jit(solution)/shard_map/all_to_all | solution.py:321
  49.1 0.2 fusion.12
  49.3 0.2 select_reduce_fusion
  49.9 0.1 select_reduce_fusion.6
  50.0 0.6 convert_reduce_fusion.2
  50.9 0.1 select_reduce_fusion.1
  51.0 0.2 select_reduce_fusion.2
  51.2 0.6 fusion.7.scales
  51.8 1.3 %fusion.10.order = s32[32]{0:T(128)S(1)} fusion(s32[32]{0:T(128)S(1)} %get-tuple-element.21, s32[]{:T(128)} %get-tuple-element.23, s32[]{:T(128)} %get-tuple-element.22), kind=kLoop, calls=%fused_computation.43 | loop fusion | flops 64 | bytes 264 | tf_op jit(solution)/shard_map/jit(_where)/select_n | solution.py:340
  53.1 0.6 fusion.8
  53.7 42.8 %all-to-all-done.1 = bf16[16,2,256,128]{3,2,1,0:T(8,128)(2,1)S(1)} async-done(((bf16[16,2,256,128]{3,2,1,0:T(8,128)(2,1)}), bf16[16,2,256,128]{3,2,1,0:T(8,128)(2,1)S(1)}, u32[]{:S(2)}, u32[]{:S(2)}) %all-to-all-start.1) | async-done | bytes 2097184 | tf_op jit(solution)/shard_map/all_to_all | solution.py:321
  96.5 4.2 %map.1 = f32[8,256,128]{2,1,0:T(8,128)} custom-call(s32[32]{0:T(128)S(1)} %fusion.10.order, s32[32]{0:T(128)S(1)} %get-tuple-element.30.targets, s32[32]{0:T(128)S(1)} %get-tuple-element.29.starts, s32[1]{0:T(128)} %bitcast.12.count, f32[4]{0:T(128)S(1)} %convert_element_type.31.kernel, f32[32]{0:T(128)S(1)} %fusion.7.scales, bf16[32,256,128]{2,1,0:T(8,128)(2,1)S(1)} %bitcast.28), custom_call_target="tpu_custom_call" | custom-call | tf_op jit(solution)/shard_map/map/pallas_call | solution.py:351
  (34 shorter events, 0.7 us)
Async XLA Ops:
  0.0 11.1 %copy-start.3 = (s32[16,1]{0,1:T(1,128)S(1)}, s32[16,1]{0,1:T(1,128)}, u32[]{:S(2)}) copy-start(s32[16,1]{0,1:T(1,128)} %param.12) | copy-start | bytes 196
  0.0 11.4 %copy-start.1 = (s32[16]{0:T(128)S(1)}, s32[16]{0:T(128)}, u32[]{:S(2)}) copy-start(s32[16]{0:T(128)} %param.13) | copy-start | bytes 196
  0.0 11.4 %copy-start = (s32[16]{0:T(128)S(1)}, s32[16]{0:T(128)}, u32[]{:S(2)}) copy-start(s32[16]{0:T(128)} %param.14) | copy-start | bytes 196
  0.0 11.3 %copy-start.2 = (s32[16]{0:T(128)S(1)}, s32[16]{0:T(128)}, u32[]{:S(2)}) copy-start(s32[16]{0:T(128)} %param.15) | copy-start | bytes 196
  4.6 32.0 %all-to-all-start = ((bf16[16,128,256]{2,1,0:T(8,128)(2,1)}), bf16[16,128,256]{2,1,0:T(8,128)(2,1)S(1)}, u32[]{:S(2)}, u32[]{:S(2)}) async-start(bf16[16,128,256]{2,1,0:T(8,128)(2,1)} %bitcast.31), calls=%async_computation | async-start | bytes 2097152 | tf_op jit(solution)/shard_map/all_to_all | solution.py:298
  11.4 1.2 %collective-permute-start = (s32[1,4,16]{2,1,0:T(4,128)S(1)}, s32[1,4,16]{2,1,0:T(4,128)S(1)}, u32[]{:S(2)}, u32[]{:S(2)}) collective-permute-start(s32[1,4,16]{2,1,0:T(4,128)S(1)} %add_bitcast_fusion), channel_id=1, source_target_pairs={{0,1},{1,0},{2,3},{3,2},{4,5},{5,4},{6,7},{7,6},{8,9},{9,8},{10,11... | collective-permute-start | bytes 776 | tf_op jit(solution)/shard_map/ppermute | solution.py:239
  12.7 4.0 %collective-permute-start.1 = (s32[2,4,16]{2,1,0:T(4,128)S(1)}, s32[2,4,16]{2,1,0:T(4,128)S(1)}, u32[]{:S(2)}, u32[]{:S(2)}) collective-permute-start(s32[2,4,16]{2,1,0:T(4,128)S(1)} %add_select_fusion.3), channel_id=1, source_target_pairs={{0,2},{1,3},{2,0},{3,1},{4,6},{5,7},{6,4},{7,5},{8,10},{9,11},{10,... | collective-permute-start | bytes 1544 | tf_op jit(solution)/shard_map/ppermute | solution.py:239
  16.7 12.8 %collective-permute-start.2 = (s32[4,4,16]{2,1,0:T(4,128)S(1)}, s32[4,4,16]{2,1,0:T(4,128)S(1)}, u32[]{:S(2)}, u32[]{:S(2)}) collective-permute-start(s32[4,4,16]{2,1,0:T(4,128)S(1)} %add_select_fusion.2), channel_id=1, source_target_pairs={{0,4},{1,5},{2,6},{3,7},{4,0},{5,1},{6,2},{7,3},{8,12},{9,13},{10,... | collective-permute-start | bytes 3080 | tf_op jit(solution)/shard_map/ppermute | solution.py:239
  29.5 4.9 %collective-permute-start.3 = (s32[8,4,16]{2,1,0:T(4,128)S(1)}, s32[8,4,16]{2,1,0:T(4,128)S(1)}, u32[]{:S(2)}, u32[]{:S(2)}) collective-permute-start(s32[8,4,16]{2,1,0:T(4,128)S(1)} %add_select_fusion.1), channel_id=1, source_target_pairs={{0,8},{1,9},{2,10},{3,11},{4,12},{5,13},{6,14},{7,15},{8,0},{9,1},... | collective-permute-start | bytes 6152 | tf_op jit(solution)/shard_map/ppermute | solution.py:239
  43.4 5.6 %copy-start.4 = (f32[4]{0:T(128)S(1)}, f32[4]{0:T(128)}, u32[]{:S(2)}) copy-start(f32[4]{0:T(128)} %param.11) | copy-start | bytes 52
  43.5 53.0 %all-to-all-start.1 = ((bf16[16,2,256,128]{3,2,1,0:T(8,128)(2,1)}), bf16[16,2,256,128]{3,2,1,0:T(8,128)(2,1)S(1)}, u32[]{:S(2)}, u32[]{:S(2)}) async-start(bf16[16,2,256,128]{3,2,1,0:T(8,128)(2,1)} %bitcast.30), calls=%async_computation.1 | async-start | bytes 4194304 | tf_op jit(solution)/shard_map/all_to_all | solution.py:321

commit v2 on v1

--- a/solution.py
+++ b/solution.py
@@ -13,9 +13,10 @@
 KW = 4
 CAP = 2
 MAP_DEV = 8
-GROUP = 4
+GROUP = 8
 PIECES = 4
 ARRIVALS = 4
+HALVES = 1
 
 diag_load = 0.5
 small_eps = 1e-05
@@ -145,7 +146,7 @@
     ]
 
 
-def whiten_kernel(slots, lines, packed, windows, tiles, sems, *, mixed):
+def whiten_kernel(slots, crossing, lines, leaving, staying, windows, tiles, sems, *, mixed):
     senders, line_count, part_rows, ranges_count = lines.shape
     dates = windows.shape[1] // 2
     sides = ranges_count // TILE
@@ -196,14 +197,22 @@
                 tiles[a * sides + side, rows, :] = found[-a % per_side].astype(jnp.bfloat16)
         for a in range(line_count):
             at = a * sides + side
-            copies.append(pltpu.make_async_copy(tiles.at[at], packed.at[slots[at]], sems.at[at]))
-            copies[-1].start()
+            copies.append(pltpu.make_async_copy(tiles.at[at], leaving.at[slots[at]], sems.at[at]))
+
+            @pl.when(crossing[at] != 0)
+            def _():
+                copies[-1].start()
+
+            @pl.when(crossing[at] == 0)
+            def _():
+                pltpu.make_async_copy(tiles.at[at], staying.at[slots[at]], sems.at[at]).start()
+
     for copy in copies:
         copy.wait()
 
 
-def map_kernel(order, targets, starts, count, kernel, scales, got, out, circulant):
-    found = count[0]
+def map_kernel(targets, starts, scales, kernel, got, out, circulant, total, *, first_row):
+    slot_count, rows_here = got.shape[0], out.shape[1]
     source = lax.broadcasted_iota(jnp.int32, circulant.shape, 0)
     column = lax.broadcasted_iota(jnp.int32, circulant.shape, 1)
     lag = (source - column) & (TILE - 1)
@@ -211,22 +220,24 @@
     for k in range(KW):
         taps = jnp.where(lag == k, kernel[k], taps)
     circulant[...] = taps
-    out[...] = jnp.zeros(out.shape, jnp.float32)
+    total[...] = jnp.zeros(total.shape, jnp.float32)
 
     def group_step(step, carry):
-        first = step * ARRIVALS
         products = []
         for k in range(ARRIVALS):
-            at = first + k
+            at = step * ARRIVALS + k
             matrix = circulant[pl.ds(starts[at], TILE), :].astype(jnp.bfloat16)
-            product = jnp.dot(got[order[at]], matrix, preferred_element_type=jnp.float32)
+            tile = got[at, pl.ds(first_row, rows_here), :]
+            tile = jnp.where(scales[at] > 0.0, tile, jnp.zeros_like(tile))
+            product = jnp.dot(tile, matrix, preferred_element_type=jnp.float32)
             products.append(product * scales[at])
         for k in range(ARRIVALS):
-            target = targets[first + k]
-            out[target] = out[target] + products[k]
+            target = targets[step * ARRIVALS + k]
+            total[target] = total[target] + products[k]
         return carry
 
-    lax.fori_loop(0, (found + ARRIVALS - 1) // ARRIVALS, group_step, 0)
+    lax.fori_loop(0, slot_count // ARRIVALS, group_step, 0)
+    out[...] = total[...].astype(out.dtype)
 
 
 def gathered(block, axis_name):
@@ -243,6 +254,36 @@
         )
         step *= 2
     return block
+
+
+def arrivals(owner, details, everything):
+    senders, _, tile_count = details.shape
+    slot_count = senders * CAP
+    here = owner * CAP + jnp.arange(CAP, dtype=jnp.int32)
+    match = (details[:, None, 0, :] == here[None, :, None]).reshape(slot_count, 1, tile_count)
+    fields = jnp.repeat(details[:, 1:], CAP, axis=0).reshape(slot_count, 3, tile_count)
+    chosen = jnp.sum(jnp.where(match, fields, 0), axis=2)
+    map_iota = jnp.arange(MAP_DEV, dtype=jnp.int32)
+    owned = jnp.where(everything[:, 0] // CAP == owner, everything[:, 3], 0).astype(jnp.float32)
+    on_map = everything[:, 1][None] == map_iota[:, None, None]
+    sums = jnp.sum(jnp.where(on_map, owned[None], 0.0), axis=(1, 2))
+    inverse = 1.0 / jnp.maximum(sums, 1.0)
+    picked = chosen[:, 0][:, None] == map_iota[None, :]
+    scales = jnp.sum(jnp.where(picked, inverse[None, :], 0.0), axis=1) * chosen[:, 2].astype(jnp.float32)
+    return chosen[:, 0], (TILE - chosen[:, 1]) & (TILE - 1), scales
+
+
+def map_sum(lists, rounded_kernel, tiles, kind, name, first_row, rows_here):
+    extent = (MAP_DEV, rows_here, TILE)
+    return pl.pallas_call(
+        partial(map_kernel, first_row=first_row),
+        out_shape=jax.ShapeDtypeStruct(extent, kind),
+        in_specs=[SMEM, SMEM, SMEM, SMEM, VMEM],
+        out_specs=VMEM,
+        scratch_shapes=[pltpu.VMEM((2 * TILE, TILE), jnp.float32), pltpu.VMEM(extent, jnp.float32)],
+        compiler_params=params,
+        name=name,
+    )(*lists, rounded_kernel, tiles)
 
 
 def shards(
@@ -292,8 +333,11 @@
     earlier = jnp.logical_and(
         owners[:, None] == owners[None, :], tile_iota[None, :] < tile_iota[:, None]
     )
-    slots = owners * CAP + jnp.sum(earlier, axis=1).astype(jnp.int32)
-    details = jnp.stack([slots, map_slot, starts_here, correlation], axis=0)[None]
+    half = peers // 2
+    ranks = jnp.sum(earlier, axis=1).astype(jnp.int32)
+    slots = (owners % half) * CAP + ranks
+    crossing = (owners // half != me // half).astype(jnp.int32)
+    details = jnp.stack([owners * CAP + ranks, map_slot, starts_here, correlation], axis=0)[None]
     sent = sent.reshape(peers, line_count * 2 * dates_here, ranges_count)
     got_lines = lax.all_to_all(sent, "date", split_axis=0, concat_axis=0, tiled=True)
     all_details = gathered(details, "date")
@@ -303,11 +347,13 @@
     if not mixed:
         got_lines = got_lines.reshape(peers, line_count, 2, dates_here, ranges_count)
         got_lines = got_lines.transpose(1, 2, 0, 3, 4).reshape(1, line_count, 2 * dates, ranges_count)
-    packed = pl.pallas_call(
+    slot_count = half * CAP
+    buffer = pltpu.HBM((slot_count, 2 * dates, TILE), jnp.bfloat16)
+    leaving, staying = pl.pallas_call(
         partial(whiten_kernel, mixed=mixed),
-        out_shape=pltpu.HBM((slot_count, 2 * dates, TILE), jnp.bfloat16),
-        in_specs=[SMEM, VMEM],
-        out_specs=HBM,
+        out_shape=(buffer, buffer),
+        in_specs=[SMEM, SMEM, VMEM],
+        out_specs=(HBM, HBM),
         scratch_shapes=[
             pltpu.VMEM((window_count, 2 * dates, TILE), jnp.bfloat16),
             pltpu.VMEM((tile_count, 2 * dates, TILE), jnp.bfloat16),
@@ -315,48 +361,39 @@
         ],
         compiler_params=params,
         name="whiten",
-    )(slots, got_lines)
-    packed, all_details = lax.optimization_barrier((packed, all_details))
-    packed = packed.reshape(peers, CAP, 2 * dates, TILE)
-    got_tiles = lax.all_to_all(packed, "date", split_axis=0, concat_axis=0, tiled=True)
-    got_tiles = got_tiles.reshape(slot_count, 2 * dates, TILE)
-
-    here = me * CAP + jnp.arange(CAP, dtype=jnp.int32)
-    match = (all_details[:, None, 0, :] == here[None, :, None]).reshape(slot_count, tile_count)
-    fields = jnp.repeat(all_details[:, 1:], CAP, axis=0).reshape(slot_count, 3, tile_count)
-    chosen = jnp.sum(jnp.where(match[:, None, :], fields, 0), axis=2)
-    filled = jnp.any(match, axis=1)
-    weights = chosen[:, 2].astype(jnp.float32)
-    map_iota = jnp.arange(MAP_DEV, dtype=jnp.int32)
-    on_map = jnp.logical_and(chosen[:, 0][:, None] == map_iota[None, :], filled[:, None])
-    sums = jnp.sum(jnp.where(on_map, weights[:, None], 0.0), axis=0)
-    scale = jnp.sum(jnp.where(on_map, 1.0 / jnp.maximum(sums, 1.0)[None, :], 0.0), axis=1) * weights
-    slot_iota = jnp.arange(slot_count, dtype=jnp.int32)
-    place = jnp.sum(jnp.logical_and(filled[None, :], slot_iota[None, :] < slot_iota[:, None]), axis=1)
-    count = jnp.sum(filled).astype(jnp.int32)
-    taken = jnp.logical_and(place[None, :] == slot_iota[:, None], filled[None, :])
-
-    def listed(values, empty):
-        return jnp.where(
-            slot_iota < count, jnp.sum(jnp.where(taken, values[None, :], 0), axis=1), empty
+    )(slots, crossing, got_lines)
+    leaving, all_details, resample_kernel = lax.optimization_barrier(
+        (leaving, all_details, resample_kernel)
+    )
+    halves = [list(range(half)), list(range(half, peers))]
+
+    def within_half(tiles):
+        return lax.all_to_all(
+            tiles, "date", split_axis=0, concat_axis=0, axis_index_groups=halves, tiled=True
         )
 
-    first = jnp.min(jnp.where(filled, slot_iota, slot_count - 1))
-    order = listed(slot_iota, first)
-    targets = listed(chosen[:, 0], 0)
-    begins = listed((TILE - chosen[:, 1]) & (TILE - 1), 0)
-    scales = listed(scale, 0.0)
     rounded_kernel = lax.optimization_barrier(resample_kernel.astype(jnp.bfloat16)).astype(jnp.float32)
-
-    return pl.pallas_call(
-        map_kernel,
-        out_shape=jax.ShapeDtypeStruct((MAP_DEV, 2 * dates, TILE), jnp.float32),
-        in_specs=[SMEM, SMEM, SMEM, SMEM, SMEM, SMEM, VMEM],
-        out_specs=VMEM,
-        scratch_shapes=[pltpu.VMEM((2 * TILE, TILE), jnp.float32)],
-        compiler_params=params,
-        name="map",
-    )(order, targets, begins, count[None], rounded_kernel, scales, got_tiles)
+    near = lax.dynamic_slice_in_dim(all_details, me // half * half, half, axis=0)
+    gathered_here = within_half(leaving)
+    far_lists = arrivals((me + half) % peers, near, all_details)
+    near_lists = arrivals(me, near, all_details)
+    gathered_here, staying, far_lists, near_lists, rounded_kernel = lax.optimization_barrier(
+        (gathered_here, staying, far_lists, near_lists, rounded_kernel)
+    )
+    across = [(i, (i + half) % peers) for i in range(peers)]
+    rows_each = 2 * dates // HALVES
+    from_far = []
+    for piece in range(HALVES):
+        partial_sums = map_sum(
+            far_lists, rounded_kernel, gathered_here, jnp.bfloat16, "far_sum", piece * rows_each, rows_each
+        )
+        if piece + 1 < HALVES:
+            partial_sums, gathered_here = lax.optimization_barrier((partial_sums, gathered_here))
+        from_far.append(lax.ppermute(partial_sums, "date", across))
+    own_sums = map_sum(
+        near_lists, rounded_kernel, within_half(staying), jnp.float32, "near_sum", 0, 2 * dates
+    )
+    return own_sums + jnp.concatenate(from_far, axis=1).astype(jnp.float32)
 
 
 def solution(mesh):

time: 101 us -> 95.8 us (0.949)
  the two profiles are of different devices: /device:TPU:13 before, /device:TPU:0 now
where the time goes in v2:
time: 95.8 us; the launch traced here: 95.4 us
  waiting for transfers between devices  53.9 us (56%)
  starting transfers between devices  23.2 us (24%)
  Pallas kernels  13.3 us (14%)
  local copies, waits for them, and re-layouts  2.76 us (3%)
  other arithmetic  2.04 us (2%)
    all_to_all x2, waiting for transfers between devices, within_half(): lax.all_to_all(tiles, 'date', split_axis=0, concat_axis=0, axis_index_gro...  33.5 us
    ppermute x4, waiting for transfers between devices, gathered(): lax.ppermute(block, axis_name, [(i, i ^ step) for i in range(peers)])  17.8 us
    all_to_all x1, starting transfers between devices, shards(): lax.all_to_all(sent, 'date', split_axis=0, concat_axis=0, tiled=True)  7.39 us
    ppermute x4, starting transfers between devices, gathered(): lax.ppermute(block, axis_name, [(i, i ^ step) for i in range(peers)])  7.34 us
    all_to_all x2, starting transfers between devices, within_half(): lax.all_to_all(tiles, 'date', split_axis=0, concat_axis=0, axis_index_gro...  7.13 us
    pallas_call x1, Pallas kernels, shards(): pl.pallas_call(partial(whiten_kernel, mixed=mixed), out_shape=(buffer, bu...  5.47 us
    pallas_call x1, Pallas kernels, shards(): pl.pallas_call(filter_kernel, out_shape=pltpu.HBM((rows_count * 2 * dates...  4.52 us
    pallas_call x2, Pallas kernels, map_sum(): pl.pallas_call(partial(map_kernel, first_row=first_row), out_shape=jax.Sh...  3.34 us
  transfers between devices with their start and end apart: 8, of which 7 were waited for; matrix products, arithmetic and copies ran while one was open for 1% of the time, Pallas kernels for 3%

profile of v2, /device:TPU:0, one launch (start us, length us, event | category | flops | bytes accessed | tf_op | source)
XLA Modules:
  0.0 95.4 jit_solution(3167338448010457420)
XLA Ops:
  0.0 4.5 %filter.1 = bf16[2048,256]{1,0:T(8,128)(2,1)} custom-call(s32[8]{0:T(128)} %lengths_hbm.1, f32[2,8,128]{2,1,0:T(8,128)} %taps_hbm.1, bf16[2,8,128,256]{3,2,1,0:T(8,128)(2,1)} %radar.1), custom_call_target="tpu_custom_call" | custom-call | tf_op jit(solution)/shard_map/filter/pallas_call | solution.py:310
  4.5 7.4 %all-to-all-start = ((bf16[16,128,256]{2,1,0:T(8,128)(2,1)}), bf16[16,128,256]{2,1,0:T(8,128)(2,1)S(1)}, u32[]{:S(2)}, u32[]{:S(2)}) async-start(bf16[16,128,256]{2,1,0:T(8,128)(2,1)} %bitcast.47), calls=%async_computation | async-start | bytes 2097152 | tf_op jit(solution)/shard_map/all_to_all | solution.py:342
  11.9 0.6 copy-done.3
  12.8 0.5 copy-done.2
  13.3 0.6 copy-done
  13.9 0.5 collective-permute-start
  14.4 0.8 collective-permute-done
  15.2 1.9 %collective-permute-start.1 = (s32[2,4,16]{2,1,0:T(4,128)S(1)}, s32[2,4,16]{2,1,0:T(4,128)S(1)}, u32[]{:S(2)}, u32[]{:S(2)}) collective-permute-start(s32[2,4,16]{2,1,0:T(4,128)S(1)} %add_select_fusion.4), channel_id=1, source_target_pairs={{0,2},{1,3},{2,0},{3,1},{4,6},{5,7},{6,4},{7,5},{8,10},{9,11},{10,... | collective-permute-start | bytes 1544 | tf_op jit(solution)/shard_map/ppermute | solution.py:250
  17.1 3.2 %collective-permute-done.1 = s32[2,4,16]{2,1,0:T(4,128)S(1)} collective-permute-done((s32[2,4,16]{2,1,0:T(4,128)S(1)}, s32[2,4,16]{2,1,0:T(4,128)S(1)}, u32[]{:S(2)}, u32[]{:S(2)}) %collective-permute-start.1) | collective-permute-done | bytes 544 | tf_op jit(solution)/shard_map/ppermute | solution.py:250
  20.3 0.6 collective-permute-start.2
  20.9 9.2 %collective-permute-done.2 = s32[4,4,16]{2,1,0:T(4,128)S(1)} collective-permute-done((s32[4,4,16]{2,1,0:T(4,128)S(1)}, s32[4,4,16]{2,1,0:T(4,128)S(1)}, u32[]{:S(2)}, u32[]{:S(2)}) %collective-permute-start.2) | collective-permute-done | bytes 1056 | tf_op jit(solution)/shard_map/ppermute | solution.py:250
  30.2 4.4 %collective-permute-start.3 = (s32[8,4,16]{2,1,0:T(4,128)S(1)}, s32[8,4,16]{2,1,0:T(4,128)S(1)}, u32[]{:S(2)}, u32[]{:S(2)}) collective-permute-start(s32[8,4,16]{2,1,0:T(4,128)S(1)} %add_select_fusion.1), channel_id=1, source_target_pairs={{0,8},{1,9},{2,10},{3,11},{4,12},{5,13},{6,14},{7,15},{8,0},{9,1},... | collective-permute-start | bytes 6152 | tf_op jit(solution)/shard_map/ppermute | solution.py:250
  34.6 4.6 %collective-permute-done.3 = s32[8,4,16]{2,1,0:T(4,128)S(1)} collective-permute-done((s32[8,4,16]{2,1,0:T(4,128)S(1)}, s32[8,4,16]{2,1,0:T(4,128)S(1)}, u32[]{:S(2)}, u32[]{:S(2)}) %collective-permute-start.3) | collective-permute-done | bytes 2080 | tf_op jit(solution)/shard_map/ppermute | solution.py:250
  39.2 5.5 %whiten.1 = (bf16[16,256,128]{2,1,0:T(8,128)(2,1)}, bf16[16,256,128]{2,1,0:T(8,128)(2,1)}) custom-call(s32[16]{0:T(128)S(1)} %fusion.7.slots, s32[16]{0:T(128)S(1)} %compare_convert_fusion.crossing, bf16[16,8,16,256]{3,2,1,0:T(8,128)(2,1)S(1)} %bitcast.46), custom_call_target="tpu_custom_call" | custom-call | tf_op jit(solution)/shard_map/whiten/pallas_call | solution.py:352
  44.7 3.6 %all-to-all-start.1 = ((bf16[16,256,128]{2,1,0:T(8,128)(2,1)}), bf16[16,256,128]{2,1,0:T(8,128)(2,1)S(1)}, u32[]{:S(2)}, u32[]{:S(2)}) async-start(bf16[16,256,128]{2,1,0:T(8,128)(2,1)} %get-tuple-element.30), calls=%async_computation.1 | async-start | bytes 2097152 | tf_op jit(solution)/shard_map/all_to_all | solution.py:371
  49.0 0.6 copy-done.4
  50.0 12.6 %all-to-all-done.1.got = bf16[16,256,128]{2,1,0:T(8,128)(2,1)S(1)} async-done(((bf16[16,256,128]{2,1,0:T(8,128)(2,1)}), bf16[16,256,128]{2,1,0:T(8,128)(2,1)S(1)}, u32[]{:S(2)}, u32[]{:S(2)}) %all-to-all-start.1) | async-done | bytes 1048608 | tf_op jit(solution)/shard_map/all_to_all | solution.py:371
  62.6 3.6 %all-to-all-start.2 = ((bf16[16,256,128]{2,1,0:T(8,128)(2,1)}), bf16[16,256,128]{2,1,0:T(8,128)(2,1)S(1)}, u32[]{:S(2)}, u32[]{:S(2)}) async-start(bf16[16,256,128]{2,1,0:T(8,128)(2,1)} %get-tuple-element.38), calls=%async_computation.2 | async-start | bytes 2097152 | tf_op jit(solution)/shard_map/all_to_all | solution.py:371
  66.2 1.7 %far_sum.1 = bf16[8,256,128]{2,1,0:T(8,128)(2,1)S(1)} custom-call(s32[16]{0:T(128)S(1)} %get-tuple-element.39.targets, s32[16]{0:T(128)S(1)} %get-tuple-element.40.starts, f32[16]{0:T(128)S(1)} %bitcast_multiply_fusion.1.scales, f32[4]{0:T(128)S(1)} %convert_element_type.50.kernel, bf16[16,256,128]{2,1,0:T(8,128)(2,1)S(1)} %all-to-all-done.1.got), custom_call_target="tpu_custom_call" | custom-call | tf_op jit(solution)/shard_map/far_sum/pallas_call | solution.py:278
  67.9 1.4 %collective-permute-start.4 = (bf16[8,256,128]{2,1,0:T(8,128)(2,1)S(1)}, bf16[8,256,128]{2,1,0:T(8,128)(2,1)S(1)}, u32[]{:S(2)}, u32[]{:S(2)}) collective-permute-start(bf16[8,256,128]{2,1,0:T(8,128)(2,1)S(1)} %far_sum.1), channel_id=1, source_target_pairs={{0,8},{1,9},{2,10},{3,11},{4,12},{5,13},{6,14},{7,15},{8,0},{9,1},... | collective-permute-start | bytes 1572872 | tf_op jit(solution)/shard_map/ppermute | solution.py:392
  69.2 20.9 %all-to-all-done.2.got = bf16[16,256,128]{2,1,0:T(8,128)(2,1)S(1)} async-done(((bf16[16,256,128]{2,1,0:T(8,128)(2,1)}), bf16[16,256,128]{2,1,0:T(8,128)(2,1)S(1)}, u32[]{:S(2)}, u32[]{:S(2)}) %all-to-all-start.2) | async-done | bytes 1048608 | tf_op jit(solution)/shard_map/all_to_all | solution.py:371
  90.1 1.7 %near_sum.1 = f32[8,256,128]{2,1,0:T(8,128)S(1)} custom-call(s32[16]{0:T(128)S(1)} %get-tuple-element.34.targets, s32[16]{0:T(128)S(1)} %get-tuple-element.35.starts, f32[16]{0:T(128)S(1)} %bitcast_multiply_fusion.scales, f32[4]{0:T(128)S(1)} %convert_element_type.50.kernel, bf16[16,256,128]{2,1,0:T(8,128)(2,1)S(1)} %all-to-all-done.2.got), custom_call_target="tpu_custom_call" | custom-call | tf_op jit(solution)/shard_map/near_sum/pallas_call | solution.py:278
  91.8 2.6 %collective-permute-done.4 = bf16[8,256,128]{2,1,0:T(8,128)(2,1)S(1)} collective-permute-done((bf16[8,256,128]{2,1,0:T(8,128)(2,1)S(1)}, bf16[8,256,128]{2,1,0:T(8,128)(2,1)S(1)}, u32[]{:S(2)}, u32[]{:S(2)}) %collective-permute-start.4) | collective-permute-done | bytes 524320 | tf_op jit(solution)/shard_map/ppermute | solution.py:392
  94.3 1.1 %convert_add_fusion = f32[8,256,128]{2,1,0:T(8,128)} fusion(f32[8,256,128]{2,1,0:T(8,128)S(1)} %near_sum.1, bf16[8,256,128]{2,1,0:T(8,128)(2,1)S(1)} %collective-permute-done.4), kind=kLoop, calls=%fused_computation | loop fusion | flops 524288 | bytes 2621440 | tf_op jit(solution)/shard_map/add | solution.py:396
  (40 shorter events, 1.4 us)
Async XLA Ops:
  4.5 34.7 %all-to-all-start = ((bf16[16,128,256]{2,1,0:T(8,128)(2,1)}), bf16[16,128,256]{2,1,0:T(8,128)(2,1)S(1)}, u32[]{:S(2)}, u32[]{:S(2)}) async-start(bf16[16,128,256]{2,1,0:T(8,128)(2,1)} %bitcast.47), calls=%async_computation | async-start | bytes 2097152 | tf_op jit(solution)/shard_map/all_to_all | solution.py:342
  11.9 0.7 copy-start.3
  12.6 0.7 copy-start.2
  13.3 0.7 copy-start
  13.3 0.7 copy-start.1
  13.9 1.3 %collective-permute-start = (s32[1,4,16]{2,1,0:T(4,128)S(1)}, s32[1,4,16]{2,1,0:T(4,128)S(1)}, u32[]{:S(2)}, u32[]{:S(2)}) collective-permute-start(s32[1,4,16]{2,1,0:T(4,128)S(1)} %add_bitcast_fusion), channel_id=1, source_target_pairs={{0,1},{1,0},{2,3},{3,2},{4,5},{5,4},{6,7},{7,6},{8,9},{9,8},{10,11... | collective-permute-start | bytes 776 | tf_op jit(solution)/shard_map/ppermute | solution.py:250
  15.2 5.1 %collective-permute-start.1 = (s32[2,4,16]{2,1,0:T(4,128)S(1)}, s32[2,4,16]{2,1,0:T(4,128)S(1)}, u32[]{:S(2)}, u32[]{:S(2)}) collective-permute-start(s32[2,4,16]{2,1,0:T(4,128)S(1)} %add_select_fusion.4), channel_id=1, source_target_pairs={{0,2},{1,3},{2,0},{3,1},{4,6},{5,7},{6,4},{7,5},{8,10},{9,11},{10,... | collective-permute-start | bytes 1544 | tf_op jit(solution)/shard_map/ppermute | solution.py:250
  20.3 9.8 %collective-permute-start.2 = (s32[4,4,16]{2,1,0:T(4,128)S(1)}, s32[4,4,16]{2,1,0:T(4,128)S(1)}, u32[]{:S(2)}, u32[]{:S(2)}) collective-permute-start(s32[4,4,16]{2,1,0:T(4,128)S(1)} %add_select_fusion.3), channel_id=1, source_target_pairs={{0,4},{1,5},{2,6},{3,7},{4,0},{5,1},{6,2},{7,3},{8,12},{9,13},{10,... | collective-permute-start | bytes 3080 | tf_op jit(solution)/shard_map/ppermute | solution.py:250
  30.2 9.0 %collective-permute-start.3 = (s32[8,4,16]{2,1,0:T(4,128)S(1)}, s32[8,4,16]{2,1,0:T(4,128)S(1)}, u32[]{:S(2)}, u32[]{:S(2)}) collective-permute-start(s32[8,4,16]{2,1,0:T(4,128)S(1)} %add_select_fusion.1), channel_id=1, source_target_pairs={{0,8},{1,9},{2,10},{3,11},{4,12},{5,13},{6,14},{7,15},{8,0},{9,1},... | collective-permute-start | bytes 6152 | tf_op jit(solution)/shard_map/ppermute | solution.py:250
  44.7 18.0 %all-to-all-start.1 = ((bf16[16,256,128]{2,1,0:T(8,128)(2,1)}), bf16[16,256,128]{2,1,0:T(8,128)(2,1)S(1)}, u32[]{:S(2)}, u32[]{:S(2)}) async-start(bf16[16,256,128]{2,1,0:T(8,128)(2,1)} %get-tuple-element.30), calls=%async_computation.1 | async-start | bytes 2097152 | tf_op jit(solution)/shard_map/all_to_all | solution.py:371
  48.9 0.7 copy-start.4
  62.6 27.5 %all-to-all-start.2 = ((bf16[16,256,128]{2,1,0:T(8,128)(2,1)}), bf16[16,256,128]{2,1,0:T(8,128)(2,1)S(1)}, u32[]{:S(2)}, u32[]{:S(2)}) async-start(bf16[16,256,128]{2,1,0:T(8,128)(2,1)} %get-tuple-element.38), calls=%async_computation.2 | async-start | bytes 2097152 | tf_op jit(solution)/shard_map/all_to_all | solution.py:371
  67.9 26.5 %collective-permute-start.4 = (bf16[8,256,128]{2,1,0:T(8,128)(2,1)S(1)}, bf16[8,256,128]{2,1,0:T(8,128)(2,1)S(1)}, u32[]{:S(2)}, u32[]{:S(2)}) collective-permute-start(bf16[8,256,128]{2,1,0:T(8,128)(2,1)S(1)} %far_sum.1), channel_id=1, source_target_pairs={{0,8},{1,9},{2,10},{3,11},{4,12},{5,13},{6,14},{7,15},{8,0},{9,1},... | collective-permute-start | bytes 1572872 | tf_op jit(solution)/shard_map/ppermute | solution.py:392

commit v3 on v2

--- a/solution.py
+++ b/solution.py
@@ -13,9 +13,9 @@
 KW = 4
 CAP = 2
 MAP_DEV = 8
-GROUP = 8
+GROUP = 16
 PIECES = 4
-ARRIVALS = 4
+ARRIVALS = 8
 HALVES = 1
 
 diag_load = 0.5
@@ -45,6 +45,7 @@
     copy_lengths.wait()
     copy_taps.wait()
     position = lax.broadcasted_iota(jnp.int32, (1, tap_count), 1)
+    operators = []
     for date in range(dates_here):
         mats = []
         for part in range(2):
@@ -52,12 +53,14 @@
             padded = jnp.concatenate([used, jnp.zeros((1, period - tap_count), jnp.float32)], axis=1)
             spread = jnp.broadcast_to(padded, (rows_count, period))
             rolled = pltpu.roll(spread, period - tap_count // 2, 1, stride=1, stride_axis=0)
-            mats.append(rolled[:, :rows_count])
-        real_mat, imag_mat = mats
-        copies[date].wait()
+            mats.append(rolled[:, :rows_count].astype(jnp.bfloat16))
+        operators.append(mats)
+    for copy in copies:
+        copy.wait()
+    for date, (real_mat, imag_mat) in enumerate(operators):
         cells = columns[date].reshape(2 * rows_count, ranges_count)
         for part, halves in enumerate(((real_mat, -imag_mat), (imag_mat, real_mat))):
-            operator = jnp.concatenate(halves, axis=1).astype(jnp.bfloat16)
+            operator = jnp.concatenate(halves, axis=1)
             product = jnp.dot(operator, cells, preferred_element_type=jnp.float32)
             for side in range(ranges_count // TILE):
                 skewed = pltpu.roll(

time: 95.8 us -> 94.2 us (0.983)
  Pallas kernels: 13.3 us -> 11.4 us
where the time goes in v3:
time: 94.2 us; the launch traced here: 93.8 us
  waiting for transfers between devices  54.3 us (58%)
  starting transfers between devices  23.2 us (25%)
  Pallas kernels  11.4 us (12%)
  local copies, waits for them, and re-layouts  2.76 us (3%)
  other arithmetic  2.04 us (2%)
    all_to_all x2, waiting for transfers between devices, within_half(): lax.all_to_all(tiles, 'date', split_axis=0, concat_axis=0, axis_index_gro...  34.2 us
    ppermute x4, waiting for transfers between devices, gathered(): lax.ppermute(block, axis_name, [(i, i ^ step) for i in range(peers)])  17.8 us
    all_to_all x1, starting transfers between devices, shards(): lax.all_to_all(sent, 'date', split_axis=0, concat_axis=0, tiled=True)  7.4 us
    ppermute x4, starting transfers between devices, gathered(): lax.ppermute(block, axis_name, [(i, i ^ step) for i in range(peers)])  7.34 us
    all_to_all x2, starting transfers between devices, within_half(): lax.all_to_all(tiles, 'date', split_axis=0, concat_axis=0, axis_index_gro...  7.13 us
    pallas_call x1, Pallas kernels, shards(): pl.pallas_call(partial(whiten_kernel, mixed=mixed), out_shape=(buffer, bu...  5.11 us
    pallas_call x1, Pallas kernels, shards(): pl.pallas_call(filter_kernel, out_shape=pltpu.HBM((rows_count * 2 * dates...  3.58 us
    pallas_call x2, Pallas kernels, map_sum(): pl.pallas_call(partial(map_kernel, first_row=first_row), out_shape=jax.Sh...  2.67 us
  transfers between devices with their start and end apart: 8, of which 7 were waited for; matrix products, arithmetic and copies ran while one was open for 1% of the time, Pallas kernels for 3%

profile of v3, /device:TPU:0, one launch (start us, length us, event | category | flops | bytes accessed | tf_op | source)
XLA Modules:
  0.0 93.8 jit_solution(14830047380113177994)
XLA Ops:
  0.0 3.6 %filter.1 = bf16[2048,256]{1,0:T(8,128)(2,1)} custom-call(s32[8]{0:T(128)} %lengths_hbm.1, f32[2,8,128]{2,1,0:T(8,128)} %taps_hbm.1, bf16[2,8,128,256]{3,2,1,0:T(8,128)(2,1)} %radar.1), custom_call_target="tpu_custom_call" | custom-call | tf_op jit(solution)/shard_map/filter/pallas_call | solution.py:313
  3.6 7.4 %all-to-all-start = ((bf16[16,128,256]{2,1,0:T(8,128)(2,1)}), bf16[16,128,256]{2,1,0:T(8,128)(2,1)S(1)}, u32[]{:S(2)}, u32[]{:S(2)}) async-start(bf16[16,128,256]{2,1,0:T(8,128)(2,1)} %bitcast.47), calls=%async_computation | async-start | bytes 2097152 | tf_op jit(solution)/shard_map/all_to_all | solution.py:345
  11.0 0.6 copy-done.3
  11.8 0.5 copy-done.2
  12.3 0.6 copy-done
  13.0 0.5 collective-permute-start
  13.5 0.8 collective-permute-done
  14.3 1.9 %collective-permute-start.1 = (s32[2,4,16]{2,1,0:T(4,128)S(1)}, s32[2,4,16]{2,1,0:T(4,128)S(1)}, u32[]{:S(2)}, u32[]{:S(2)}) collective-permute-start(s32[2,4,16]{2,1,0:T(4,128)S(1)} %add_select_fusion.4), channel_id=1, source_target_pairs={{0,2},{1,3},{2,0},{3,1},{4,6},{5,7},{6,4},{7,5},{8,10},{9,11},{10,... | collective-permute-start | bytes 1544 | tf_op jit(solution)/shard_map/ppermute | solution.py:253
  16.2 3.2 %collective-permute-done.1 = s32[2,4,16]{2,1,0:T(4,128)S(1)} collective-permute-done((s32[2,4,16]{2,1,0:T(4,128)S(1)}, s32[2,4,16]{2,1,0:T(4,128)S(1)}, u32[]{:S(2)}, u32[]{:S(2)}) %collective-permute-start.1) | collective-permute-done | bytes 544 | tf_op jit(solution)/shard_map/ppermute | solution.py:253
  19.4 0.6 collective-permute-start.2
  20.0 9.2 %collective-permute-done.2 = s32[4,4,16]{2,1,0:T(4,128)S(1)} collective-permute-done((s32[4,4,16]{2,1,0:T(4,128)S(1)}, s32[4,4,16]{2,1,0:T(4,128)S(1)}, u32[]{:S(2)}, u32[]{:S(2)}) %collective-permute-start.2) | collective-permute-done | bytes 1056 | tf_op jit(solution)/shard_map/ppermute | solution.py:253
  29.2 4.4 %collective-permute-start.3 = (s32[8,4,16]{2,1,0:T(4,128)S(1)}, s32[8,4,16]{2,1,0:T(4,128)S(1)}, u32[]{:S(2)}, u32[]{:S(2)}) collective-permute-start(s32[8,4,16]{2,1,0:T(4,128)S(1)} %add_select_fusion.1), channel_id=1, source_target_pairs={{0,8},{1,9},{2,10},{3,11},{4,12},{5,13},{6,14},{7,15},{8,0},{9,1},... | collective-permute-start | bytes 6152 | tf_op jit(solution)/shard_map/ppermute | solution.py:253
  33.7 4.6 %collective-permute-done.3 = s32[8,4,16]{2,1,0:T(4,128)S(1)} collective-permute-done((s32[8,4,16]{2,1,0:T(4,128)S(1)}, s32[8,4,16]{2,1,0:T(4,128)S(1)}, u32[]{:S(2)}, u32[]{:S(2)}) %collective-permute-start.3) | collective-permute-done | bytes 2080 | tf_op jit(solution)/shard_map/ppermute | solution.py:253
  38.3 5.1 %whiten.1 = (bf16[16,256,128]{2,1,0:T(8,128)(2,1)}, bf16[16,256,128]{2,1,0:T(8,128)(2,1)}) custom-call(s32[16]{0:T(128)S(1)} %fusion.7.slots, s32[16]{0:T(128)S(1)} %compare_convert_fusion.crossing, bf16[16,8,16,256]{3,2,1,0:T(8,128)(2,1)S(1)} %bitcast.46), custom_call_target="tpu_custom_call" | custom-call | tf_op jit(solution)/shard_map/whiten/pallas_call | solution.py:355
  43.4 3.6 %all-to-all-start.1 = ((bf16[16,256,128]{2,1,0:T(8,128)(2,1)}), bf16[16,256,128]{2,1,0:T(8,128)(2,1)S(1)}, u32[]{:S(2)}, u32[]{:S(2)}) async-start(bf16[16,256,128]{2,1,0:T(8,128)(2,1)} %get-tuple-element.30), calls=%async_computation.1 | async-start | bytes 2097152 | tf_op jit(solution)/shard_map/all_to_all | solution.py:374
  47.7 0.6 copy-done.4
  48.7 12.6 %all-to-all-done.1.got = bf16[16,256,128]{2,1,0:T(8,128)(2,1)S(1)} async-done(((bf16[16,256,128]{2,1,0:T(8,128)(2,1)}), bf16[16,256,128]{2,1,0:T(8,128)(2,1)S(1)}, u32[]{:S(2)}, u32[]{:S(2)}) %all-to-all-start.1) | async-done | bytes 1048608 | tf_op jit(solution)/shard_map/all_to_all | solution.py:374
  61.4 3.6 %all-to-all-start.2 = ((bf16[16,256,128]{2,1,0:T(8,128)(2,1)}), bf16[16,256,128]{2,1,0:T(8,128)(2,1)S(1)}, u32[]{:S(2)}, u32[]{:S(2)}) async-start(bf16[16,256,128]{2,1,0:T(8,128)(2,1)} %get-tuple-element.38), calls=%async_computation.2 | async-start | bytes 2097152 | tf_op jit(solution)/shard_map/all_to_all | solution.py:374
  64.9 1.3 %far_sum.1 = bf16[8,256,128]{2,1,0:T(8,128)(2,1)S(1)} custom-call(s32[16]{0:T(128)S(1)} %get-tuple-element.39.targets, s32[16]{0:T(128)S(1)} %get-tuple-element.40.starts, f32[16]{0:T(128)S(1)} %bitcast_multiply_fusion.1.scales, f32[4]{0:T(128)S(1)} %convert_element_type.50.kernel, bf16[16,256,128]{2,1,0:T(8,128)(2,1)S(1)} %all-to-all-done.1.got), custom_call_target="tpu_custom_call" | custom-call | tf_op jit(solution)/shard_map/far_sum/pallas_call | solution.py:281
  66.2 1.3 %collective-permute-start.4 = (bf16[8,256,128]{2,1,0:T(8,128)(2,1)S(1)}, bf16[8,256,128]{2,1,0:T(8,128)(2,1)S(1)}, u32[]{:S(2)}, u32[]{:S(2)}) collective-permute-start(bf16[8,256,128]{2,1,0:T(8,128)(2,1)S(1)} %far_sum.1), channel_id=1, source_target_pairs={{0,8},{1,9},{2,10},{3,11},{4,12},{5,13},{6,14},{7,15},{8,0},{9,1},... | collective-permute-start | bytes 1572872 | tf_op jit(solution)/shard_map/ppermute | solution.py:395
  67.6 21.5 %all-to-all-done.2.got = bf16[16,256,128]{2,1,0:T(8,128)(2,1)S(1)} async-done(((bf16[16,256,128]{2,1,0:T(8,128)(2,1)}), bf16[16,256,128]{2,1,0:T(8,128)(2,1)S(1)}, u32[]{:S(2)}, u32[]{:S(2)}) %all-to-all-start.2) | async-done | bytes 1048608 | tf_op jit(solution)/shard_map/all_to_all | solution.py:374
  89.1 1.4 %near_sum.1 = f32[8,256,128]{2,1,0:T(8,128)S(1)} custom-call(s32[16]{0:T(128)S(1)} %get-tuple-element.34.targets, s32[16]{0:T(128)S(1)} %get-tuple-element.35.starts, f32[16]{0:T(128)S(1)} %bitcast_multiply_fusion.scales, f32[4]{0:T(128)S(1)} %convert_element_type.50.kernel, bf16[16,256,128]{2,1,0:T(8,128)(2,1)S(1)} %all-to-all-done.2.got), custom_call_target="tpu_custom_call" | custom-call | tf_op jit(solution)/shard_map/near_sum/pallas_call | solution.py:281
  90.5 2.3 %collective-permute-done.4 = bf16[8,256,128]{2,1,0:T(8,128)(2,1)S(1)} collective-permute-done((bf16[8,256,128]{2,1,0:T(8,128)(2,1)S(1)}, bf16[8,256,128]{2,1,0:T(8,128)(2,1)S(1)}, u32[]{:S(2)}, u32[]{:S(2)}) %collective-permute-start.4) | collective-permute-done | bytes 524320 | tf_op jit(solution)/shard_map/ppermute | solution.py:395
  92.7 1.1 %convert_add_fusion = f32[8,256,128]{2,1,0:T(8,128)} fusion(f32[8,256,128]{2,1,0:T(8,128)S(1)} %near_sum.1, bf16[8,256,128]{2,1,0:T(8,128)(2,1)S(1)} %collective-permute-done.4), kind=kLoop, calls=%fused_computation | loop fusion | flops 524288 | bytes 2621440 | tf_op jit(solution)/shard_map/add | solution.py:399
  (40 shorter events, 1.4 us)
Async XLA Ops:
  3.6 34.7 %all-to-all-start = ((bf16[16,128,256]{2,1,0:T(8,128)(2,1)}), bf16[16,128,256]{2,1,0:T(8,128)(2,1)S(1)}, u32[]{:S(2)}, u32[]{:S(2)}) async-start(bf16[16,128,256]{2,1,0:T(8,128)(2,1)} %bitcast.47), calls=%async_computation | async-start | bytes 2097152 | tf_op jit(solution)/shard_map/all_to_all | solution.py:345
  11.0 0.7 copy-start.3
  11.7 0.7 copy-start.2
  12.3 0.7 copy-start
  12.3 0.7 copy-start.1
  13.0 1.3 %collective-permute-start = (s32[1,4,16]{2,1,0:T(4,128)S(1)}, s32[1,4,16]{2,1,0:T(4,128)S(1)}, u32[]{:S(2)}, u32[]{:S(2)}) collective-permute-start(s32[1,4,16]{2,1,0:T(4,128)S(1)} %add_bitcast_fusion), channel_id=1, source_target_pairs={{0,1},{1,0},{2,3},{3,2},{4,5},{5,4},{6,7},{7,6},{8,9},{9,8},{10,11... | collective-permute-start | bytes 776 | tf_op jit(solution)/shard_map/ppermute | solution.py:253
  14.3 5.1 %collective-permute-start.1 = (s32[2,4,16]{2,1,0:T(4,128)S(1)}, s32[2,4,16]{2,1,0:T(4,128)S(1)}, u32[]{:S(2)}, u32[]{:S(2)}) collective-permute-start(s32[2,4,16]{2,1,0:T(4,128)S(1)} %add_select_fusion.4), channel_id=1, source_target_pairs={{0,2},{1,3},{2,0},{3,1},{4,6},{5,7},{6,4},{7,5},{8,10},{9,11},{10,... | collective-permute-start | bytes 1544 | tf_op jit(solution)/shard_map/ppermute | solution.py:253
  19.4 9.8 %collective-permute-start.2 = (s32[4,4,16]{2,1,0:T(4,128)S(1)}, s32[4,4,16]{2,1,0:T(4,128)S(1)}, u32[]{:S(2)}, u32[]{:S(2)}) collective-permute-start(s32[4,4,16]{2,1,0:T(4,128)S(1)} %add_select_fusion.3), channel_id=1, source_target_pairs={{0,4},{1,5},{2,6},{3,7},{4,0},{5,1},{6,2},{7,3},{8,12},{9,13},{10,... | collective-permute-start | bytes 3080 | tf_op jit(solution)/shard_map/ppermute | solution.py:253
  29.2 9.0 %collective-permute-start.3 = (s32[8,4,16]{2,1,0:T(4,128)S(1)}, s32[8,4,16]{2,1,0:T(4,128)S(1)}, u32[]{:S(2)}, u32[]{:S(2)}) collective-permute-start(s32[8,4,16]{2,1,0:T(4,128)S(1)} %add_select_fusion.1), channel_id=1, source_target_pairs={{0,8},{1,9},{2,10},{3,11},{4,12},{5,13},{6,14},{7,15},{8,0},{9,1},... | collective-permute-start | bytes 6152 | tf_op jit(solution)/shard_map/ppermute | solution.py:253
  43.4 18.0 %all-to-all-start.1 = ((bf16[16,256,128]{2,1,0:T(8,128)(2,1)}), bf16[16,256,128]{2,1,0:T(8,128)(2,1)S(1)}, u32[]{:S(2)}, u32[]{:S(2)}) async-start(bf16[16,256,128]{2,1,0:T(8,128)(2,1)} %get-tuple-element.30), calls=%async_computation.1 | async-start | bytes 2097152 | tf_op jit(solution)/shard_map/all_to_all | solution.py:374
  47.7 0.7 copy-start.4
  61.4 27.7 %all-to-all-start.2 = ((bf16[16,256,128]{2,1,0:T(8,128)(2,1)}), bf16[16,256,128]{2,1,0:T(8,128)(2,1)S(1)}, u32[]{:S(2)}, u32[]{:S(2)}) async-start(bf16[16,256,128]{2,1,0:T(8,128)(2,1)} %get-tuple-element.38), calls=%async_computation.2 | async-start | bytes 2097152 | tf_op jit(solution)/shard_map/all_to_all | solution.py:374
  66.2 26.5 %collective-permute-start.4 = (bf16[8,256,128]{2,1,0:T(8,128)(2,1)S(1)}, bf16[8,256,128]{2,1,0:T(8,128)(2,1)S(1)}, u32[]{:S(2)}, u32[]{:S(2)}) collective-permute-start(bf16[8,256,128]{2,1,0:T(8,128)(2,1)S(1)} %far_sum.1), channel_id=1, source_target_pairs={{0,8},{1,9},{2,10},{3,11},{4,12},{5,13},{6,14},{7,15},{8,0},{9,1},... | collective-permute-start | bytes 1572872 | tf_op jit(solution)/shard_map/ppermute | solution.py:395

commit v4 on v3

--- a/solution.py
+++ b/solution.py
@@ -149,7 +149,7 @@
     ]
 
 
-def whiten_kernel(slots, crossing, lines, leaving, staying, windows, tiles, sems, *, mixed):
+def whiten_kernel(slots, routes, lines, leaving, same, other, windows, tiles, sems, *, mixed):
     senders, line_count, part_rows, ranges_count = lines.shape
     dates = windows.shape[1] // 2
     sides = ranges_count // TILE
@@ -200,22 +200,20 @@
                 tiles[a * sides + side, rows, :] = found[-a % per_side].astype(jnp.bfloat16)
         for a in range(line_count):
             at = a * sides + side
-            copies.append(pltpu.make_async_copy(tiles.at[at], leaving.at[slots[at]], sems.at[at]))
-
-            @pl.when(crossing[at] != 0)
-            def _():
-                copies[-1].start()
-
-            @pl.when(crossing[at] == 0)
-            def _():
-                pltpu.make_async_copy(tiles.at[at], staying.at[slots[at]], sems.at[at]).start()
-
+            routed = [
+                pltpu.make_async_copy(tiles.at[at], buffer.at[slots[at]], sems.at[at])
+                for buffer in (leaving, same, other)
+            ]
+            for route, copy in enumerate(routed):
+                pl.when(routes[at] == route)(copy.start)
+            copies.append(routed[0])
     for copy in copies:
         copy.wait()
 
 
-def map_kernel(targets, starts, scales, kernel, got, out, circulant, total, *, first_row):
-    slot_count, rows_here = got.shape[0], out.shape[1]
+def map_kernel(targets, starts, scales, kernel, *refs, first_row):
+    *arrived, out, circulant, total = refs
+    rows_here = out.shape[1]
     source = lax.broadcasted_iota(jnp.int32, circulant.shape, 0)
     column = lax.broadcasted_iota(jnp.int32, circulant.shape, 1)
     lag = (source - column) & (TILE - 1)
@@ -225,21 +223,25 @@
     circulant[...] = taps
     total[...] = jnp.zeros(total.shape, jnp.float32)
 
-    def group_step(step, carry):
+    def group_step(got, before, each, step, carry):
         products = []
-        for k in range(ARRIVALS):
-            at = step * ARRIVALS + k
+        for k in range(each):
+            at = before + step * each + k
             matrix = circulant[pl.ds(starts[at], TILE), :].astype(jnp.bfloat16)
-            tile = got[at, pl.ds(first_row, rows_here), :]
+            tile = got[step * each + k, pl.ds(first_row, rows_here), :]
             tile = jnp.where(scales[at] > 0.0, tile, jnp.zeros_like(tile))
             product = jnp.dot(tile, matrix, preferred_element_type=jnp.float32)
             products.append(product * scales[at])
-        for k in range(ARRIVALS):
-            target = targets[step * ARRIVALS + k]
+        for k in range(each):
+            target = targets[before + step * each + k]
             total[target] = total[target] + products[k]
         return carry
 
-    lax.fori_loop(0, slot_count // ARRIVALS, group_step, 0)
+    before = 0
+    for got in arrived:
+        each = min(ARRIVALS, got.shape[0])
+        lax.fori_loop(0, got.shape[0] // each, partial(group_step, got, before, each), 0)
+        before += got.shape[0]
     out[...] = total[...].astype(out.dtype)
 
 
@@ -278,15 +280,16 @@
 
 def map_sum(lists, rounded_kernel, tiles, kind, name, first_row, rows_here):
     extent = (MAP_DEV, rows_here, TILE)
+    tiles = tiles if isinstance(tiles, (list, tuple)) else [tiles]
     return pl.pallas_call(
         partial(map_kernel, first_row=first_row),
         out_shape=jax.ShapeDtypeStruct(extent, kind),
-        in_specs=[SMEM, SMEM, SMEM, SMEM, VMEM],
+        in_specs=[SMEM] * 4 + [VMEM] * len(tiles),
         out_specs=VMEM,
         scratch_shapes=[pltpu.VMEM((2 * TILE, TILE), jnp.float32), pltpu.VMEM(extent, jnp.float32)],
         compiler_params=params,
         name=name,
-    )(*lists, rounded_kernel, tiles)
+    )(*lists, rounded_kernel, *tiles)
 
 
 def shards(
@@ -338,12 +341,15 @@
     )
     half = peers // 2
     ranks = jnp.sum(earlier, axis=1).astype(jnp.int32)
-    slots = (owners % half) * CAP + ranks
-    crossing = (owners // half != me // half).astype(jnp.int32)
+    step = (owners % half) ^ (me % half)
+    leaves = owners // half != me // half
+    slots = jnp.where(leaves, owners % half, step // 2) * CAP + ranks
+    routes = jnp.where(leaves, 0, 1 + step % 2)
     details = jnp.stack([owners * CAP + ranks, map_slot, starts_here, correlation], axis=0)[None]
     sent = sent.reshape(peers, line_count * 2 * dates_here, ranges_count)
     got_lines = lax.all_to_all(sent, "date", split_axis=0, concat_axis=0, tiled=True)
     all_details = gathered(details, "date")
+    got_lines, all_details = lax.optimization_barrier((got_lines, all_details))
 
     mixed = dates_here == 8 and peers % 2 == 0
     got_lines = got_lines.reshape(peers, line_count, 2 * dates_here, ranges_count)
@@ -352,11 +358,12 @@
         got_lines = got_lines.transpose(1, 2, 0, 3, 4).reshape(1, line_count, 2 * dates, ranges_count)
     slot_count = half * CAP
     buffer = pltpu.HBM((slot_count, 2 * dates, TILE), jnp.bfloat16)
-    leaving, staying = pl.pallas_call(
+    near_buffer = pltpu.HBM((slot_count // 2, 2 * dates, TILE), jnp.bfloat16)
+    leaving, same, other = pl.pallas_call(
         partial(whiten_kernel, mixed=mixed),
-        out_shape=(buffer, buffer),
+        out_shape=(buffer, near_buffer, near_buffer),
         in_specs=[SMEM, SMEM, VMEM],
-        out_specs=(HBM, HBM),
+        out_specs=(HBM, HBM, HBM),
         scratch_shapes=[
             pltpu.VMEM((window_count, 2 * dates, TILE), jnp.bfloat16),
             pltpu.VMEM((tile_count, 2 * dates, TILE), jnp.bfloat16),
@@ -364,9 +371,10 @@
         ],
         compiler_params=params,
         name="whiten",
-    )(slots, crossing, got_lines)
-    leaving, all_details, resample_kernel = lax.optimization_barrier(
-        (leaving, all_details, resample_kernel)
+    )(slots, routes, got_lines)
+    other = lax.ppermute(other, "date", [(i, i ^ 1) for i in range(peers)])
+    other, all_details, resample_kernel = lax.optimization_barrier(
+        (other, all_details, resample_kernel)
     )
     halves = [list(range(half)), list(range(half, peers))]
 
@@ -379,10 +387,17 @@
     near = lax.dynamic_slice_in_dim(all_details, me // half * half, half, axis=0)
     gathered_here = within_half(leaving)
     far_lists = arrivals((me + half) % peers, near, all_details)
-    near_lists = arrivals(me, near, all_details)
-    gathered_here, staying, far_lists, near_lists, rounded_kernel = lax.optimization_barrier(
-        (gathered_here, staying, far_lists, near_lists, rounded_kernel)
-    )
+    senders = jnp.arange(half, dtype=jnp.int32) ^ (me % half)
+    near_lists = arrivals(me, jnp.take(near, senders, axis=0), all_details)
+    gathered_here, far_lists, near_lists, rounded_kernel = lax.optimization_barrier(
+        (gathered_here, far_lists, near_lists, rounded_kernel)
+    )
+    near_tiles = []
+    for k in range(half // 2):
+        pair = jnp.concatenate([same[k * CAP : (k + 1) * CAP], other[k * CAP : (k + 1) * CAP]], axis=0)
+        if k:
+            pair = lax.ppermute(pair, "date", [(i, i ^ (2 * k)) for i in range(peers)])
+        near_tiles.append(pair)
     across = [(i, (i + half) % peers) for i in range(peers)]
     rows_each = 2 * dates // HALVES
     from_far = []
@@ -394,7 +409,7 @@
             partial_sums, gathered_here = lax.optimization_barrier((partial_sums, gathered_here))
         from_far.append(lax.ppermute(partial_sums, "date", across))
     own_sums = map_sum(
-        near_lists, rounded_kernel, within_half(staying), jnp.float32, "near_sum", 0, 2 * dates
+        near_lists, rounded_kernel, near_tiles, jnp.float32, "near_sum", 0, 2 * dates
     )
     return own_sums + jnp.concatenate(from_far, axis=1).astype(jnp.float32)
 

time: 94.2 us -> 92.2 us (0.979)
  waiting for transfers between devices: 54.3 us -> 49.7 us
  local copies, waits for them, and re-layouts: 2.76 us -> 4.71 us
    all_to_all x2 -> x1, waiting for transfers between devices: 34.2 us -> 10.4 us  [within_half(): lax.all_to_all(tiles, 'date', split_axis=0, concat_axis=0, axis_index_gro...]
    ppermute x0 -> x4, waiting for transfers between devices: none -> 21.5 us  [the longest x3 21.5 us: shards(): pair = lax.ppermute(pair, 'date', [(i, i ^ 2 * k) for i in range(peers)])]
    ppermute x0 -> x4, starting transfers between devices: none -> 3.75 us  [the longest x3 3.68 us: shards(): pair = lax.ppermute(pair, 'date', [(i, i ^ 2 * k) for i in range(peers)])]
    all_to_all x2 -> x1, starting transfers between devices: 7.13 us -> 3.7 us  [within_half(): lax.all_to_all(tiles, 'date', split_axis=0, concat_axis=0, axis_index_gro...]
    ppermute x1, waiting for transfers between devices: 2.29 us -> 0.01 us  [shards(): from_far.append(lax.ppermute(partial_sums, 'date', across))]
    unnamed x10 -> x14, local copies, waits for them, and re-layouts: 2.37 us -> 2.96 us
  transfers between devices with their start and end apart: 8 -> 11, of which waited for: 7 -> 7; matrix products, arithmetic and copies ran while one was open for 1% -> 3% of each run, Pallas kernels for 3% -> 1%
where the time goes in v4:
time: 92.2 us; the launch traced here: 91.9 us
  waiting for transfers between devices  49.7 us (54%)
  starting transfers between devices  23.5 us (25%)
  Pallas kernels  11.2 us (12%)
  local copies, waits for them, and re-layouts  4.71 us (5%)
  other arithmetic  2.41 us (3%)
    ppermute x3, waiting for transfers between devices, shards(): pair = lax.ppermute(pair, 'date', [(i, i ^ 2 * k) for i in range(peers)])  21.5 us
    ppermute x4, waiting for transfers between devices, gathered(): lax.ppermute(block, axis_name, [(i, i ^ step) for i in range(peers)])  17.8 us
    all_to_all x1, waiting for transfers between devices, within_half(): lax.all_to_all(tiles, 'date', split_axis=0, concat_axis=0, axis_index_gro...  10.4 us
    all_to_all x1, starting transfers between devices, shards(): lax.all_to_all(sent, 'date', split_axis=0, concat_axis=0, tiled=True)  7.4 us
    ppermute x4, starting transfers between devices, gathered(): lax.ppermute(block, axis_name, [(i, i ^ step) for i in range(peers)])  7.34 us
    pallas_call x1, Pallas kernels, shards(): pl.pallas_call(partial(whiten_kernel, mixed=mixed), out_shape=(buffer, ne...  5.12 us
    all_to_all x1, starting transfers between devices, within_half(): lax.all_to_all(tiles, 'date', split_axis=0, concat_axis=0, axis_index_gro...  3.7 us
    ppermute x3, starting transfers between devices, shards(): pair = lax.ppermute(pair, 'date', [(i, i ^ 2 * k) for i in range(peers)])  3.68 us
  transfers between devices with their start and end apart: 11, of which 7 were waited for; matrix products, arithmetic and copies ran while one was open for 3% of the time, Pallas kernels for 1%

profile of v4, /device:TPU:0, one launch (start us, length us, event | category | flops | bytes accessed | tf_op | source)
XLA Modules:
  0.0 91.9 jit_solution(9952643283287344773)
XLA Ops:
  0.0 3.6 %filter.1 = bf16[2048,256]{1,0:T(8,128)(2,1)} custom-call(s32[8]{0:T(128)} %lengths_hbm.1, f32[2,8,128]{2,1,0:T(8,128)} %taps_hbm.1, bf16[2,8,128,256]{3,2,1,0:T(8,128)(2,1)} %radar.1), custom_call_target="tpu_custom_call" | custom-call | tf_op jit(solution)/shard_map/filter/pallas_call | solution.py:316
  3.6 7.4 %all-to-all-start = ((bf16[16,128,256]{2,1,0:T(8,128)(2,1)}), bf16[16,128,256]{2,1,0:T(8,128)(2,1)S(1)}, u32[]{:S(2)}, u32[]{:S(2)}) async-start(bf16[16,128,256]{2,1,0:T(8,128)(2,1)} %bitcast.54), calls=%async_computation | async-start | bytes 2097152 | tf_op jit(solution)/shard_map/all_to_all | solution.py:350
  11.0 0.6 copy-done.2
  12.3 0.6 copy-done.3
  13.5 0.8 collective-permute-done
  14.3 1.9 %collective-permute-start.1 = (s32[2,4,16]{2,1,0:T(4,128)S(1)}, s32[2,4,16]{2,1,0:T(4,128)S(1)}, u32[]{:S(2)}, u32[]{:S(2)}) collective-permute-start(s32[2,4,16]{2,1,0:T(4,128)S(1)} %add_select_fusion.4), channel_id=1, source_target_pairs={{0,2},{1,3},{2,0},{3,1},{4,6},{5,7},{6,4},{7,5},{8,10},{9,11},{10,... | collective-permute-start | bytes 1544 | tf_op jit(solution)/shard_map/ppermute | solution.py:255
  16.2 3.2 %collective-permute-done.1 = s32[2,4,16]{2,1,0:T(4,128)S(1)} collective-permute-done((s32[2,4,16]{2,1,0:T(4,128)S(1)}, s32[2,4,16]{2,1,0:T(4,128)S(1)}, u32[]{:S(2)}, u32[]{:S(2)}) %collective-permute-start.1) | collective-permute-done | bytes 544 | tf_op jit(solution)/shard_map/ppermute | solution.py:255
  19.4 0.6 collective-permute-start.2
  20.0 9.2 %collective-permute-done.2 = s32[4,4,16]{2,1,0:T(4,128)S(1)} collective-permute-done((s32[4,4,16]{2,1,0:T(4,128)S(1)}, s32[4,4,16]{2,1,0:T(4,128)S(1)}, u32[]{:S(2)}, u32[]{:S(2)}) %collective-permute-start.2) | collective-permute-done | bytes 1056 | tf_op jit(solution)/shard_map/ppermute | solution.py:255
  29.2 4.4 %collective-permute-start.3 = (s32[8,4,16]{2,1,0:T(4,128)S(1)}, s32[8,4,16]{2,1,0:T(4,128)S(1)}, u32[]{:S(2)}, u32[]{:S(2)}) collective-permute-start(s32[8,4,16]{2,1,0:T(4,128)S(1)} %add_select_fusion.1), channel_id=1, source_target_pairs={{0,8},{1,9},{2,10},{3,11},{4,12},{5,13},{6,14},{7,15},{8,0},{9,1},... | collective-permute-start | bytes 6152 | tf_op jit(solution)/shard_map/ppermute | solution.py:255
  33.7 4.6 %collective-permute-done.3 = s32[8,4,16]{2,1,0:T(4,128)S(1)} collective-permute-done((s32[8,4,16]{2,1,0:T(4,128)S(1)}, s32[8,4,16]{2,1,0:T(4,128)S(1)}, u32[]{:S(2)}, u32[]{:S(2)}) %collective-permute-start.3) | collective-permute-done | bytes 2080 | tf_op jit(solution)/shard_map/ppermute | solution.py:255
  38.3 5.1 %whiten.1 = (bf16[16,256,128]{2,1,0:T(8,128)(2,1)}, bf16[8,256,128]{2,1,0:T(8,128)(2,1)}, bf16[8,256,128]{2,1,0:T(8,128)(2,1)}) custom-call(s32[16]{0:T(128)S(1)} %fusion.7.slots, s32[16]{0:T(128)S(1)} %get-tuple-element.49.routes, bf16[16,8,16,256]{3,2,1,0:T(8,128)(2,1)S(1)} %bitcast.53), custom_call_target="tpu_custom_call" | custom-call | tf_op jit(solution)/shard_map/whiten/pallas_call | solution.py:362
  43.5 3.7 %all-to-all-start.1 = ((bf16[16,256,128]{2,1,0:T(8,128)(2,1)}), bf16[16,256,128]{2,1,0:T(8,128)(2,1)S(1)}, u32[]{:S(2)}, u32[]{:S(2)}) async-start(bf16[16,256,128]{2,1,0:T(8,128)(2,1)} %get-tuple-element.32), calls=%async_computation.1 | async-start | bytes 2097152 | tf_op jit(solution)/shard_map/all_to_all | solution.py:382
  49.1 0.7 slice-done
  51.2 10.4 %all-to-all-done.1.refs_0_ = bf16[16,256,128]{2,1,0:T(8,128)(2,1)S(1)} async-done(((bf16[16,256,128]{2,1,0:T(8,128)(2,1)}), bf16[16,256,128]{2,1,0:T(8,128)(2,1)S(1)}, u32[]{:S(2)}, u32[]{:S(2)}) %all-to-all-start.1) | async-done | bytes 1048608 | tf_op jit(solution)/shard_map/all_to_all | solution.py:382
  61.6 1.3 %far_sum.1 = bf16[8,256,128]{2,1,0:T(8,128)(2,1)S(1)} custom-call(s32[16]{0:T(128)S(1)} %get-tuple-element.43.targets, s32[16]{0:T(128)S(1)} %get-tuple-element.44.starts, f32[16]{0:T(128)S(1)} %bitcast_multiply_fusion.1.scales, f32[4]{0:T(128)S(1)} %convert_element_type.46.kernel, bf16[16,256,128]{2,1,0:T(8,128)(2,1)S(1)} %all-to-all-done.1.refs_0_), custom_call_target="tpu_custom_call" | custom-call | tf_op jit(solution)/shard_map/far_sum/pallas_call | solution.py:284
  62.9 1.3 %collective-permute-start.8 = (bf16[8,256,128]{2,1,0:T(8,128)(2,1)S(1)}, bf16[8,256,128]{2,1,0:T(8,128)(2,1)S(1)}, u32[]{:S(2)}, u32[]{:S(2)}) collective-permute-start(bf16[8,256,128]{2,1,0:T(8,128)(2,1)S(1)} %far_sum.1), channel_id=1, source_target_pairs={{0,8},{1,9},{2,10},{3,11},{4,12},{5,13},{6,14},{7,15},{8,0},{9,1},... | collective-permute-start | bytes 1572872 | tf_op jit(solution)/shard_map/ppermute | solution.py:410
  64.3 1.5 %collective-permute-start.7 = (bf16[4,256,128]{2,1,0:T(8,128)(2,1)S(1)}, bf16[4,256,128]{2,1,0:T(8,128)(2,1)S(1)}, u32[]{:S(2)}, u32[]{:S(2)}) collective-permute-start(bf16[4,256,128]{2,1,0:T(8,128)(2,1)S(1)} %pad_maximum_fusion.3), channel_id=1, source_target_pairs={{0,6},{1,7},{2,4},{3,5},{4,2},{5,3},{6,0},{7,1},{8,14},{9,15},{10,... | collective-permute-start | bytes 786440 | tf_op jit(solution)/shard_map/ppermute | solution.py:399
  65.9 1.5 %collective-permute-start.6 = (bf16[4,256,128]{2,1,0:T(8,128)(2,1)S(1)}, bf16[4,256,128]{2,1,0:T(8,128)(2,1)S(1)}, u32[]{:S(2)}, u32[]{:S(2)}) collective-permute-start(bf16[4,256,128]{2,1,0:T(8,128)(2,1)S(1)} %pad_maximum_fusion.2), channel_id=1, source_target_pairs={{0,4},{1,5},{2,6},{3,7},{4,0},{5,1},{6,2},{7,3},{8,12},{9,13},{10,... | collective-permute-start | bytes 786440 | tf_op jit(solution)/shard_map/ppermute | solution.py:399
  67.4 0.6 collective-permute-start.5
  68.1 14.2 %collective-permute-done.7.refs_3_ = bf16[4,256,128]{2,1,0:T(8,128)(2,1)S(1)} collective-permute-done((bf16[4,256,128]{2,1,0:T(8,128)(2,1)S(1)}, bf16[4,256,128]{2,1,0:T(8,128)(2,1)S(1)}, u32[]{:S(2)}, u32[]{:S(2)}) %collective-permute-start.7) | collective-permute-done | bytes 262176 | tf_op jit(solution)/shard_map/ppermute | solution.py:399
  82.2 7.3 %collective-permute-done.6.refs_2_ = bf16[4,256,128]{2,1,0:T(8,128)(2,1)S(1)} collective-permute-done((bf16[4,256,128]{2,1,0:T(8,128)(2,1)S(1)}, bf16[4,256,128]{2,1,0:T(8,128)(2,1)S(1)}, u32[]{:S(2)}, u32[]{:S(2)}) %collective-permute-start.6) | collective-permute-done | bytes 262176 | tf_op jit(solution)/shard_map/ppermute | solution.py:399
  89.6 1.2 %near_sum.1 = f32[8,256,128]{2,1,0:T(8,128)S(1)} custom-call(s32[16]{0:T(128)S(1)} %get-tuple-element.37.targets, s32[16]{0:T(128)S(1)} %get-tuple-element.38.starts, f32[16]{0:T(128)S(1)} %bitcast_multiply_fusion.scales, f32[4]{0:T(128)S(1)} %convert_element_type.46.kernel, bf16[4,256,128]{2,1,0:T(8,128)(2,1)S(1)} %pad_maximum_fusion.refs_0_, ...), custom_call_target="tpu_custom_call" | custom-call | tf_op jit(solution)/shard_map/near_sum/pallas_call | solution.py:284
  90.8 1.1 %convert_add_fusion = f32[8,256,128]{2,1,0:T(8,128)} fusion(f32[8,256,128]{2,1,0:T(8,128)S(1)} %near_sum.1, bf16[8,256,128]{2,1,0:T(8,128)(2,1)S(1)} %collective-permute-done.8), kind=kLoop, calls=%fused_computation.1 | loop fusion | flops 524288 | bytes 2621440 | tf_op jit(solution)/shard_map/add | solution.py:414
  (68 shorter events, 4.6 us)
Async XLA Ops:
  3.6 34.7 %all-to-all-start = ((bf16[16,128,256]{2,1,0:T(8,128)(2,1)}), bf16[16,128,256]{2,1,0:T(8,128)(2,1)S(1)}, u32[]{:S(2)}, u32[]{:S(2)}) async-start(bf16[16,128,256]{2,1,0:T(8,128)(2,1)} %bitcast.54), calls=%async_computation | async-start | bytes 2097152 | tf_op jit(solution)/shard_map/all_to_all | solution.py:350
  11.0 0.7 copy-start.2
  11.7 0.7 copy-start.5
  12.3 0.7 copy-start.3
  12.3 0.7 copy-start.4
  13.0 1.3 %collective-permute-start = (s32[1,4,16]{2,1,0:T(4,128)S(1)}, s32[1,4,16]{2,1,0:T(4,128)S(1)}, u32[]{:S(2)}, u32[]{:S(2)}) collective-permute-start(s32[1,4,16]{2,1,0:T(4,128)S(1)} %add_bitcast_fusion), channel_id=1, source_target_pairs={{0,1},{1,0},{2,3},{3,2},{4,5},{5,4},{6,7},{7,6},{8,9},{9,8},{10,11... | collective-permute-start | bytes 776 | tf_op jit(solution)/shard_map/ppermute | solution.py:255
  14.3 5.1 %collective-permute-start.1 = (s32[2,4,16]{2,1,0:T(4,128)S(1)}, s32[2,4,16]{2,1,0:T(4,128)S(1)}, u32[]{:S(2)}, u32[]{:S(2)}) collective-permute-start(s32[2,4,16]{2,1,0:T(4,128)S(1)} %add_select_fusion.4), channel_id=1, source_target_pairs={{0,2},{1,3},{2,0},{3,1},{4,6},{5,7},{6,4},{7,5},{8,10},{9,11},{10,... | collective-permute-start | bytes 1544 | tf_op jit(solution)/shard_map/ppermute | solution.py:255
  19.4 9.8 %collective-permute-start.2 = (s32[4,4,16]{2,1,0:T(4,128)S(1)}, s32[4,4,16]{2,1,0:T(4,128)S(1)}, u32[]{:S(2)}, u32[]{:S(2)}) collective-permute-start(s32[4,4,16]{2,1,0:T(4,128)S(1)} %add_select_fusion.3), channel_id=1, source_target_pairs={{0,4},{1,5},{2,6},{3,7},{4,0},{5,1},{6,2},{7,3},{8,12},{9,13},{10,... | collective-permute-start | bytes 3080 | tf_op jit(solution)/shard_map/ppermute | solution.py:255
  29.2 9.0 %collective-permute-start.3 = (s32[8,4,16]{2,1,0:T(4,128)S(1)}, s32[8,4,16]{2,1,0:T(4,128)S(1)}, u32[]{:S(2)}, u32[]{:S(2)}) collective-permute-start(s32[8,4,16]{2,1,0:T(4,128)S(1)} %add_select_fusion.1), channel_id=1, source_target_pairs={{0,8},{1,9},{2,10},{3,11},{4,12},{5,13},{6,14},{7,15},{8,0},{9,1},... | collective-permute-start | bytes 6152 | tf_op jit(solution)/shard_map/ppermute | solution.py:255
  43.4 3.9 %collective-permute-start.4 = (bf16[8,256,128]{2,1,0:T(8,128)(2,1)}, bf16[8,256,128]{2,1,0:T(8,128)(2,1)S(1)}, u32[]{:S(2)}, u32[]{:S(2)}) collective-permute-start(bf16[8,256,128]{2,1,0:T(8,128)(2,1)} %get-tuple-element.33), channel_id=1, source_target_pairs={{0,1},{1,0},{2,3},{3,2},{4,5},{5,4},{6,7},{7,6},{8,9},{9,8},{10,11... | collective-permute-start | bytes 1572872 | tf_op jit(solution)/shard_map/ppermute | solution.py:375
  43.5 3.7 %copy-start = (bf16[8,256,128]{2,1,0:T(8,128)(2,1)S(1)}, bf16[8,256,128]{2,1,0:T(8,128)(2,1)}, u32[]{:S(2)}) copy-start(bf16[8,256,128]{2,1,0:T(8,128)(2,1)} %get-tuple-element.41) | copy-start | bytes 1572868
  43.5 18.1 %all-to-all-start.1 = ((bf16[16,256,128]{2,1,0:T(8,128)(2,1)}), bf16[16,256,128]{2,1,0:T(8,128)(2,1)S(1)}, u32[]{:S(2)}, u32[]{:S(2)}) async-start(bf16[16,256,128]{2,1,0:T(8,128)(2,1)} %get-tuple-element.32), calls=%async_computation.1 | async-start | bytes 2097152 | tf_op jit(solution)/shard_map/all_to_all | solution.py:382
  48.0 0.6 copy-start.1
  49.1 0.7 slice-start
  50.1 0.7 copy-start.6
  62.9 27.8 %collective-permute-start.8 = (bf16[8,256,128]{2,1,0:T(8,128)(2,1)S(1)}, bf16[8,256,128]{2,1,0:T(8,128)(2,1)S(1)}, u32[]{:S(2)}, u32[]{:S(2)}) collective-permute-start(bf16[8,256,128]{2,1,0:T(8,128)(2,1)S(1)} %far_sum.1), channel_id=1, source_target_pairs={{0,8},{1,9},{2,10},{3,11},{4,12},{5,13},{6,14},{7,15},{8,0},{9,1},... | collective-permute-start | bytes 1572872 | tf_op jit(solution)/shard_map/ppermute | solution.py:410
  64.3 17.9 %collective-permute-start.7 = (bf16[4,256,128]{2,1,0:T(8,128)(2,1)S(1)}, bf16[4,256,128]{2,1,0:T(8,128)(2,1)S(1)}, u32[]{:S(2)}, u32[]{:S(2)}) collective-permute-start(bf16[4,256,128]{2,1,0:T(8,128)(2,1)S(1)} %pad_maximum_fusion.3), channel_id=1, source_target_pairs={{0,6},{1,7},{2,4},{3,5},{4,2},{5,3},{6,0},{7,1},{8,14},{9,15},{10,... | collective-permute-start | bytes 786440 | tf_op jit(solution)/shard_map/ppermute | solution.py:399
  65.9 23.7 %collective-permute-start.6 = (bf16[4,256,128]{2,1,0:T(8,128)(2,1)S(1)}, bf16[4,256,128]{2,1,0:T(8,128)(2,1)S(1)}, u32[]{:S(2)}, u32[]{:S(2)}) collective-permute-start(bf16[4,256,128]{2,1,0:T(8,128)(2,1)S(1)} %pad_maximum_fusion.2), channel_id=1, source_target_pairs={{0,4},{1,5},{2,6},{3,7},{4,0},{5,1},{6,2},{7,3},{8,12},{9,13},{10,... | collective-permute-start | bytes 786440 | tf_op jit(solution)/shard_map/ppermute | solution.py:399
  67.4 22.1 %collective-permute-start.5 = (bf16[4,256,128]{2,1,0:T(8,128)(2,1)S(1)}, bf16[4,256,128]{2,1,0:T(8,128)(2,1)S(1)}, u32[]{:S(2)}, u32[]{:S(2)}) collective-permute-start(bf16[4,256,128]{2,1,0:T(8,128)(2,1)S(1)} %pad_maximum_fusion.1), channel_id=1, source_target_pairs={{0,2},{1,3},{2,0},{3,1},{4,6},{5,7},{6,4},{7,5},{8,10},{9,11},{10,... | collective-permute-start | bytes 786440 | tf_op jit(solution)/shard_map/ppermute | solution.py:399

commit v5 on v4

--- a/solution.py
+++ b/solution.py
@@ -16,7 +16,7 @@
 GROUP = 16
 PIECES = 4
 ARRIVALS = 8
-HALVES = 1
+TIED = 1
 
 diag_load = 0.5
 small_eps = 1e-05
@@ -149,7 +149,8 @@
     ]
 
 
-def whiten_kernel(slots, routes, lines, leaving, same, other, windows, tiles, sems, *, mixed):
+def whiten_kernel(slots, routes, lines, *refs, mixed):
+    *buffers, windows, tiles, sems = refs
     senders, line_count, part_rows, ranges_count = lines.shape
     dates = windows.shape[1] // 2
     sides = ranges_count // TILE
@@ -202,7 +203,7 @@
             at = a * sides + side
             routed = [
                 pltpu.make_async_copy(tiles.at[at], buffer.at[slots[at]], sems.at[at])
-                for buffer in (leaving, same, other)
+                for buffer in buffers
             ]
             for route, copy in enumerate(routed):
                 pl.when(routes[at] == route)(copy.start)
@@ -211,9 +212,11 @@
         copy.wait()
 
 
-def map_kernel(targets, starts, scales, kernel, *refs, first_row):
-    *arrived, out, circulant, total = refs
-    rows_here = out.shape[1]
+def map_kernel(targets, starts, scales, kernel, *refs, arrays, first_slot):
+    arrived, rest = refs[:arrays], list(refs[arrays:])
+    total = rest.pop() if rest[-1].shape[0] == MAP_DEV else None
+    *begun, out, circulant = rest
+    total = out if total is None else total
     source = lax.broadcasted_iota(jnp.int32, circulant.shape, 0)
     column = lax.broadcasted_iota(jnp.int32, circulant.shape, 1)
     lag = (source - column) & (TILE - 1)
@@ -221,28 +224,24 @@
     for k in range(KW):
         taps = jnp.where(lag == k, kernel[k], taps)
     circulant[...] = taps
-    total[...] = jnp.zeros(total.shape, jnp.float32)
-
-    def group_step(got, before, each, step, carry):
+    if begun:
+        total[...] = sum(sums[...].astype(jnp.float32) for sums in begun)
+    else:
+        total[...] = jnp.zeros(total.shape, jnp.float32)
+    jobs = [(got, k) for got in arrived for k in range(got.shape[0])]
+    for first in range(0, len(jobs), ARRIVALS):
         products = []
-        for k in range(each):
-            at = before + step * each + k
+        for k, (got, place) in enumerate(jobs[first : first + ARRIVALS]):
+            at = first_slot + first + k
             matrix = circulant[pl.ds(starts[at], TILE), :].astype(jnp.bfloat16)
-            tile = got[step * each + k, pl.ds(first_row, rows_here), :]
+            tile = got[place]
             tile = jnp.where(scales[at] > 0.0, tile, jnp.zeros_like(tile))
-            product = jnp.dot(tile, matrix, preferred_element_type=jnp.float32)
-            products.append(product * scales[at])
-        for k in range(each):
-            target = targets[before + step * each + k]
-            total[target] = total[target] + products[k]
-        return carry
-
-    before = 0
-    for got in arrived:
-        each = min(ARRIVALS, got.shape[0])
-        lax.fori_loop(0, got.shape[0] // each, partial(group_step, got, before, each), 0)
-        before += got.shape[0]
-    out[...] = total[...].astype(out.dtype)
+            products.append(jnp.dot(tile, matrix, preferred_element_type=jnp.float32) * scales[at])
+        for k, product in enumerate(products):
+            target = targets[first_slot + first + k]
+            total[target] = total[target] + product
+    if total is not out:
+        out[...] = total[...].astype(out.dtype)
 
 
 def gathered(block, axis_name):
@@ -278,18 +277,20 @@
     return chosen[:, 0], (TILE - chosen[:, 1]) & (TILE - 1), scales
 
 
-def map_sum(lists, rounded_kernel, tiles, kind, name, first_row, rows_here):
-    extent = (MAP_DEV, rows_here, TILE)
-    tiles = tiles if isinstance(tiles, (list, tuple)) else [tiles]
+def map_sum(lists, rounded_kernel, tiles, kind, name, first_slot, begun=()):
+    extent = (MAP_DEV,) + tiles[0].shape[1:]
+    scratch = [pltpu.VMEM((2 * TILE, TILE), jnp.float32)]
+    if kind != jnp.float32:
+        scratch.append(pltpu.VMEM(extent, jnp.float32))
     return pl.pallas_call(
-        partial(map_kernel, first_row=first_row),
+        partial(map_kernel, arrays=len(tiles), first_slot=first_slot),
         out_shape=jax.ShapeDtypeStruct(extent, kind),
-        in_specs=[SMEM] * 4 + [VMEM] * len(tiles),
+        in_specs=[SMEM] * 4 + [VMEM] * (len(tiles) + len(begun)),
         out_specs=VMEM,
-        scratch_shapes=[pltpu.VMEM((2 * TILE, TILE), jnp.float32), pltpu.VMEM(extent, jnp.float32)],
+        scratch_shapes=scratch,
         compiler_params=params,
         name=name,
-    )(*lists, rounded_kernel, *tiles)
+    )(*lists, rounded_kernel, *tiles, *begun)
 
 
 def shards(
@@ -343,8 +344,8 @@
     ranks = jnp.sum(earlier, axis=1).astype(jnp.int32)
     step = (owners % half) ^ (me % half)
     leaves = owners // half != me // half
-    slots = jnp.where(leaves, owners % half, step // 2) * CAP + ranks
-    routes = jnp.where(leaves, 0, 1 + step % 2)
+    slots = step // 2 * CAP + ranks
+    routes = jnp.where(leaves, 0, 2) + step % 2
     details = jnp.stack([owners * CAP + ranks, map_slot, starts_here, correlation], axis=0)[None]
     sent = sent.reshape(peers, line_count * 2 * dates_here, ranges_count)
     got_lines = lax.all_to_all(sent, "date", split_axis=0, concat_axis=0, tiled=True)
@@ -356,14 +357,12 @@
     if not mixed:
         got_lines = got_lines.reshape(peers, line_count, 2, dates_here, ranges_count)
         got_lines = got_lines.transpose(1, 2, 0, 3, 4).reshape(1, line_count, 2 * dates, ranges_count)
-    slot_count = half * CAP
-    buffer = pltpu.HBM((slot_count, 2 * dates, TILE), jnp.bfloat16)
-    near_buffer = pltpu.HBM((slot_count // 2, 2 * dates, TILE), jnp.bfloat16)
-    leaving, same, other = pl.pallas_call(
+    buffer = pltpu.HBM((half // 2 * CAP, 2 * dates, TILE), jnp.bfloat16)
+    leaving_same, leaving_other, same, other = pl.pallas_call(
         partial(whiten_kernel, mixed=mixed),
-        out_shape=(buffer, near_buffer, near_buffer),
+        out_shape=(buffer,) * 4,
         in_specs=[SMEM, SMEM, VMEM],
-        out_specs=(HBM, HBM, HBM),
+        out_specs=(HBM,) * 4,
         scratch_shapes=[
             pltpu.VMEM((window_count, 2 * dates, TILE), jnp.bfloat16),
             pltpu.VMEM((tile_count, 2 * dates, TILE), jnp.bfloat16),
@@ -372,46 +371,48 @@
         compiler_params=params,
         name="whiten",
     )(slots, routes, got_lines)
-    other = lax.ppermute(other, "date", [(i, i ^ 1) for i in range(peers)])
+
+    def exchanged(values, step):
+        return lax.ppermute(values, "date", [(i, i ^ step) for i in range(peers)])
+
+    def from_chips(mine, received):
+        tiles = []
+        for k in range(half // 2):
+            at = slice(k * CAP, (k + 1) * CAP)
+            tiles += [exchanged(cells[at], 2 * k) if k else cells[at] for cells in (mine, received)]
+        return tiles
+
+    early = half // 2
+    early_slots = early * CAP
+    far_tiles = from_chips(leaving_same, exchanged(leaving_other, 1))
+    other = exchanged(other, 1)
     other, all_details, resample_kernel = lax.optimization_barrier(
         (other, all_details, resample_kernel)
     )
-    halves = [list(range(half)), list(range(half, peers))]
-
-    def within_half(tiles):
-        return lax.all_to_all(
-            tiles, "date", split_axis=0, concat_axis=0, axis_index_groups=halves, tiled=True
-        )
-
     rounded_kernel = lax.optimization_barrier(resample_kernel.astype(jnp.bfloat16)).astype(jnp.float32)
-    near = lax.dynamic_slice_in_dim(all_details, me // half * half, half, axis=0)
-    gathered_here = within_half(leaving)
+    senders = jnp.arange(half, dtype=jnp.int32) ^ (me % half)
+    near = jnp.take(all_details, me // half * half + senders, axis=0)
     far_lists = arrivals((me + half) % peers, near, all_details)
-    senders = jnp.arange(half, dtype=jnp.int32) ^ (me % half)
-    near_lists = arrivals(me, jnp.take(near, senders, axis=0), all_details)
-    gathered_here, far_lists, near_lists, rounded_kernel = lax.optimization_barrier(
-        (gathered_here, far_lists, near_lists, rounded_kernel)
-    )
-    near_tiles = []
-    for k in range(half // 2):
-        pair = jnp.concatenate([same[k * CAP : (k + 1) * CAP], other[k * CAP : (k + 1) * CAP]], axis=0)
-        if k:
-            pair = lax.ppermute(pair, "date", [(i, i ^ (2 * k)) for i in range(peers)])
-        near_tiles.append(pair)
-    across = [(i, (i + half) % peers) for i in range(peers)]
-    rows_each = 2 * dates // HALVES
-    from_far = []
-    for piece in range(HALVES):
-        partial_sums = map_sum(
-            far_lists, rounded_kernel, gathered_here, jnp.bfloat16, "far_sum", piece * rows_each, rows_each
-        )
-        if piece + 1 < HALVES:
-            partial_sums, gathered_here = lax.optimization_barrier((partial_sums, gathered_here))
-        from_far.append(lax.ppermute(partial_sums, "date", across))
-    own_sums = map_sum(
-        near_lists, rounded_kernel, near_tiles, jnp.float32, "near_sum", 0, 2 * dates
-    )
-    return own_sums + jnp.concatenate(from_far, axis=1).astype(jnp.float32)
+    near_lists = arrivals(me, near, all_details)
+    far_begun = map_sum(far_lists, rounded_kernel, far_tiles[:early], jnp.float32, "far_early", 0)
+    partial_sums = map_sum(
+        far_lists, rounded_kernel, far_tiles[early:], jnp.bfloat16, "far_late", early_slots, [far_begun]
+    )
+    partial_sums, same, other, near_lists = lax.optimization_barrier(
+        (partial_sums, same, other, near_lists)
+    )
+    from_far = lax.ppermute(partial_sums, "date", [(i, (i + half) % peers) for i in range(peers)])
+    near_tiles = from_chips(same, other)
+    near_begun = map_sum(near_lists, rounded_kernel, near_tiles[:early], jnp.float32, "near_early", 0)
+    return map_sum(
+        near_lists,
+        rounded_kernel,
+        near_tiles[early:],
+        jnp.float32,
+        "near_late",
+        early_slots,
+        [near_begun, from_far],
+    )
 
 
 def solution(mesh):

time: 92.2 us -> 89.6 us (0.972)
  waiting for transfers between devices: 49.7 us -> 39.7 us
  starting transfers between devices: 23.5 us -> 29.9 us
  Pallas kernels: 11.2 us -> 13.7 us
  other arithmetic: 2.41 us -> 1.11 us
    all_to_all x1 -> x0, waiting for transfers between devices: 10.4 us -> none  [within_half(): lax.all_to_all(tiles, 'date', split_axis=0, concat_axis=0, axis_index_gro...]
    ppermute x5 -> x15, starting transfers between devices: 5.08 us -> 15.2 us  [the longest x14 13.8 us: exchanged(): return lax.ppermute(values, 'date', [(i, i ^ step) for i in range(peers)])]
    all_to_all x1 -> x0, starting transfers between devices: 3.7 us -> none  [within_half(): lax.all_to_all(tiles, 'date', split_axis=0, concat_axis=0, axis_index_gro...]
    pallas_call x3 -> x5, Pallas kernels: 7.65 us -> 10.1 us  [the longest x1 5.11 us: shards(): pl.pallas_call(partial(whiten_kernel, mixed=mixed), out_shape=(buffer,) *...]
    slice x2 -> x4, local copies, waits for them, and re-layouts: 0.07 us -> 1.23 us  [from_chips(): cells[at]]
    add x2, other arithmetic: 1.08 us -> 0.03 us  [the longest x1 0.02 us: shards(): routes = jnp.where(leaves, 0, 2) + step % 2]
    unnamed x14 -> x12, local copies, waits for them, and re-layouts: 2.96 us -> 2.44 us
    ppermute x5 -> x15, waiting for transfers between devices: 21.5 us -> 21.9 us  [the longest x14 21.9 us: exchanged(): return lax.ppermute(values, 'date', [(i, i ^ step) for i in range(peers)])]
  transfers between devices with their start and end apart: 11 -> 20, of which waited for: 7 -> 12; matrix products, arithmetic and copies ran while one was open for 3% -> 4% of each run, Pallas kernels for 1% -> 2%
where the time goes in v5:
time: 89.6 us; the launch traced here: 89.3 us
  waiting for transfers between devices  39.7 us (44%)
  starting transfers between devices  29.9 us (33%)
  Pallas kernels  13.7 us (15%)
  local copies, waits for them, and re-layouts  4.63 us (5%)
  other arithmetic  1.11 us (1%)
    ppermute x14, waiting for transfers between devices, exchanged(): return lax.ppermute(values, 'date', [(i, i ^ step) for i in range(peers)])  21.9 us
    ppermute x4, waiting for transfers between devices, gathered(): lax.ppermute(block, axis_name, [(i, i ^ step) for i in range(peers)])  17.8 us
    ppermute x14, starting transfers between devices, exchanged(): return lax.ppermute(values, 'date', [(i, i ^ step) for i in range(peers)])  13.8 us
    all_to_all x1, starting transfers between devices, shards(): lax.all_to_all(sent, 'date', split_axis=0, concat_axis=0, tiled=True)  7.4 us
    ppermute x4, starting transfers between devices, gathered(): lax.ppermute(block, axis_name, [(i, i ^ step) for i in range(peers)])  7.34 us
    pallas_call x1, Pallas kernels, shards(): pl.pallas_call(partial(whiten_kernel, mixed=mixed), out_shape=(buffer,) *...  5.11 us
    pallas_call x4, Pallas kernels, map_sum(): pl.pallas_call(partial(map_kernel, arrays=len(tiles), first_slot=first_sl...  5 us
    pallas_call x1, Pallas kernels, shards(): pl.pallas_call(filter_kernel, out_shape=pltpu.HBM((rows_count * 2 * dates...  3.58 us
  transfers between devices with their start and end apart: 20, of which 12 were waited for; matrix products, arithmetic and copies ran while one was open for 4% of the time, Pallas kernels for 2%

profile of v5, /device:TPU:0, one launch (start us, length us, event | category | flops | bytes accessed | tf_op | source)
XLA Modules:
  0.0 89.3 jit_solution(6420149953444718552)
XLA Ops:
  0.0 3.6 %filter.1 = bf16[2048,256]{1,0:T(8,128)(2,1)} custom-call(s32[8]{0:T(128)} %lengths_hbm.1, f32[2,8,128]{2,1,0:T(8,128)} %taps_hbm.1, bf16[2,8,128,256]{3,2,1,0:T(8,128)(2,1)} %radar.1), custom_call_target="tpu_custom_call" | custom-call | tf_op jit(solution)/shard_map/filter/pallas_call | solution.py:317
  3.6 7.4 %all-to-all-start = ((bf16[16,128,256]{2,1,0:T(8,128)(2,1)}), bf16[16,128,256]{2,1,0:T(8,128)(2,1)S(1)}, u32[]{:S(2)}, u32[]{:S(2)}) async-start(bf16[16,128,256]{2,1,0:T(8,128)(2,1)} %bitcast.50), calls=%async_computation | async-start | bytes 2097152 | tf_op jit(solution)/shard_map/all_to_all | solution.py:351
  14.3 1.9 %collective-permute-start.1 = (s32[2,4,16]{2,1,0:T(4,128)S(1)}, s32[2,4,16]{2,1,0:T(4,128)S(1)}, u32[]{:S(2)}, u32[]{:S(2)}) collective-permute-start(s32[2,4,16]{2,1,0:T(4,128)S(1)} %add_select_fusion.4), channel_id=1, source_target_pairs={{0,2},{1,3},{2,0},{3,1},{4,6},{5,7},{6,4},{7,5},{8,10},{9,11},{10,... | collective-permute-start | bytes 1544 | tf_op jit(solution)/shard_map/ppermute | solution.py:254
  16.2 3.2 %collective-permute-done.1 = s32[2,4,16]{2,1,0:T(4,128)S(1)} collective-permute-done((s32[2,4,16]{2,1,0:T(4,128)S(1)}, s32[2,4,16]{2,1,0:T(4,128)S(1)}, u32[]{:S(2)}, u32[]{:S(2)}) %collective-permute-start.1) | collective-permute-done | bytes 544 | tf_op jit(solution)/shard_map/ppermute | solution.py:254
  20.0 9.2 %collective-permute-done.2 = s32[4,4,16]{2,1,0:T(4,128)S(1)} collective-permute-done((s32[4,4,16]{2,1,0:T(4,128)S(1)}, s32[4,4,16]{2,1,0:T(4,128)S(1)}, u32[]{:S(2)}, u32[]{:S(2)}) %collective-permute-start.2) | collective-permute-done | bytes 1056 | tf_op jit(solution)/shard_map/ppermute | solution.py:254
  29.2 4.4 %collective-permute-start.3 = (s32[8,4,16]{2,1,0:T(4,128)S(1)}, s32[8,4,16]{2,1,0:T(4,128)S(1)}, u32[]{:S(2)}, u32[]{:S(2)}) collective-permute-start(s32[8,4,16]{2,1,0:T(4,128)S(1)} %add_select_fusion.1), channel_id=1, source_target_pairs={{0,8},{1,9},{2,10},{3,11},{4,12},{5,13},{6,14},{7,15},{8,0},{9,1},... | collective-permute-start | bytes 6152 | tf_op jit(solution)/shard_map/ppermute | solution.py:254
  33.7 4.6 %collective-permute-done.3 = s32[8,4,16]{2,1,0:T(4,128)S(1)} collective-permute-done((s32[8,4,16]{2,1,0:T(4,128)S(1)}, s32[8,4,16]{2,1,0:T(4,128)S(1)}, u32[]{:S(2)}, u32[]{:S(2)}) %collective-permute-start.3) | collective-permute-done | bytes 2080 | tf_op jit(solution)/shard_map/ppermute | solution.py:254
  38.3 5.1 %whiten.1 = (bf16[8,256,128]{2,1,0:T(8,128)(2,1)}, bf16[8,256,128]{2,1,0:T(8,128)(2,1)}, bf16[8,256,128]{2,1,0:T(8,128)(2,1)}, bf16[8,256,128]{2,1,0:T(8,128)(2,1)}) custom-call(s32[16]{0:T(128)S(1)} %multiply_add_fusion.slots, s32[16]{0:T(128)S(1)} %get-tuple-element.49.routes, bf16[16,8,16,256]{3,2,1,0:T(8,128)(2,1)S(1)} %bitcast.49), custom_call_target="tpu_custom_call" | custom-call | tf_op jit(solution)/shard_map/whiten/pallas_call | solution.py:361
  45.2 1.6 %collective-permute-start.10 = (bf16[2,256,128]{2,1,0:T(8,128)(2,1)S(1)}, bf16[2,256,128]{2,1,0:T(8,128)(2,1)S(1)}, u32[]{:S(2)}, u32[]{:S(2)}) collective-permute-start(bf16[2,256,128]{2,1,0:T(8,128)(2,1)S(1)} %get-tuple-element.63), channel_id=1, source_target_pairs={{0,2},{1,3},{2,0},{3,1},{4,6},{5,7},{6,4},{7,5},{8,10},{9,11},{10,... | collective-permute-start | bytes 393224 | tf_op jit(solution)/shard_map/ppermute | solution.py:376
  46.7 2.0 %collective-permute-start.8 = (bf16[2,256,128]{2,1,0:T(8,128)(2,1)S(1)}, bf16[2,256,128]{2,1,0:T(8,128)(2,1)S(1)}, u32[]{:S(2)}, u32[]{:S(2)}) collective-permute-start(bf16[2,256,128]{2,1,0:T(8,128)(2,1)S(1)} %get-tuple-element.65), channel_id=1, source_target_pairs={{0,6},{1,7},{2,4},{3,5},{4,2},{5,3},{6,0},{7,1},{8,14},{9,15},{10,... | collective-permute-start | bytes 393224 | tf_op jit(solution)/shard_map/ppermute | solution.py:376
  50.3 1.6 %collective-permute-start.11 = (bf16[2,256,128]{2,1,0:T(8,128)(2,1)S(1)}, bf16[2,256,128]{2,1,0:T(8,128)(2,1)S(1)}, u32[]{:S(2)}, u32[]{:S(2)}) collective-permute-start(bf16[2,256,128]{2,1,0:T(8,128)(2,1)S(1)} %get-tuple-element.59), channel_id=1, source_target_pairs={{0,2},{1,3},{2,0},{3,1},{4,6},{5,7},{6,4},{7,5},{8,10},{9,11},{10,... | collective-permute-start | bytes 393224 | tf_op jit(solution)/shard_map/ppermute | solution.py:376
  52.8 2.1 %collective-permute-start.9 = (bf16[2,256,128]{2,1,0:T(8,128)(2,1)S(1)}, bf16[2,256,128]{2,1,0:T(8,128)(2,1)S(1)}, u32[]{:S(2)}, u32[]{:S(2)}) collective-permute-start(bf16[2,256,128]{2,1,0:T(8,128)(2,1)S(1)} %get-tuple-element.61), channel_id=1, source_target_pairs={{0,6},{1,7},{2,4},{3,5},{4,2},{5,3},{6,0},{7,1},{8,14},{9,15},{10,... | collective-permute-start | bytes 393224 | tf_op jit(solution)/shard_map/ppermute | solution.py:376
  54.9 3.2 %collective-permute-done.11.refs_3_ = bf16[2,256,128]{2,1,0:T(8,128)(2,1)S(1)} collective-permute-done((bf16[2,256,128]{2,1,0:T(8,128)(2,1)S(1)}, bf16[2,256,128]{2,1,0:T(8,128)(2,1)S(1)}, u32[]{:S(2)}, u32[]{:S(2)}) %collective-permute-start.11) | collective-permute-done | bytes 131104 | tf_op jit(solution)/shard_map/ppermute | solution.py:376
  59.2 1.2 %collective-permute-done.9.refs_3_ = bf16[2,256,128]{2,1,0:T(8,128)(2,1)S(1)} collective-permute-done((bf16[2,256,128]{2,1,0:T(8,128)(2,1)S(1)}, bf16[2,256,128]{2,1,0:T(8,128)(2,1)S(1)}, u32[]{:S(2)}, u32[]{:S(2)}) %collective-permute-start.9) | collective-permute-done | bytes 131104 | tf_op jit(solution)/shard_map/ppermute | solution.py:376
  61.4 1.3 %collective-permute-start.18 = (bf16[8,256,128]{2,1,0:T(8,128)(2,1)S(1)}, bf16[8,256,128]{2,1,0:T(8,128)(2,1)S(1)}, u32[]{:S(2)}, u32[]{:S(2)}) collective-permute-start(bf16[8,256,128]{2,1,0:T(8,128)(2,1)S(1)} %far_late.1), channel_id=1, source_target_pairs={{0,8},{1,9},{2,10},{3,11},{4,12},{5,13},{6,14},{7,15},{8,0},{9,1},... | collective-permute-start | bytes 1572872 | tf_op jit(solution)/shard_map/ppermute | solution.py:404
  63.3 1.6 %collective-permute-start.17 = (bf16[2,256,128]{2,1,0:T(8,128)(2,1)S(1)}, bf16[2,256,128]{2,1,0:T(8,128)(2,1)S(1)}, u32[]{:S(2)}, u32[]{:S(2)}) collective-permute-start(bf16[2,256,128]{2,1,0:T(8,128)(2,1)S(1)} %get-tuple-element.51), channel_id=1, source_target_pairs={{0,2},{1,3},{2,0},{3,1},{4,6},{5,7},{6,4},{7,5},{8,10},{9,11},{10,... | collective-permute-start | bytes 393224 | tf_op jit(solution)/shard_map/ppermute | solution.py:376
  65.7 1.3 %collective-permute-start.13 = (bf16[2,256,128]{2,1,0:T(8,128)(2,1)S(1)}, bf16[2,256,128]{2,1,0:T(8,128)(2,1)S(1)}, u32[]{:S(2)}, u32[]{:S(2)}) collective-permute-start(bf16[2,256,128]{2,1,0:T(8,128)(2,1)S(1)} %get-tuple-element.54), channel_id=1, source_target_pairs={{0,4},{1,5},{2,6},{3,7},{4,0},{5,1},{6,2},{7,3},{8,12},{9,13},{10,... | collective-permute-start | bytes 393224 | tf_op jit(solution)/shard_map/ppermute | solution.py:376
  67.8 1.7 %collective-permute-start.14 = (bf16[2,256,128]{2,1,0:T(8,128)(2,1)S(1)}, bf16[2,256,128]{2,1,0:T(8,128)(2,1)S(1)}, u32[]{:S(2)}, u32[]{:S(2)}) collective-permute-start(bf16[2,256,128]{2,1,0:T(8,128)(2,1)S(1)} %get-tuple-element.57), channel_id=1, source_target_pairs={{0,6},{1,7},{2,4},{3,5},{4,2},{5,3},{6,0},{7,1},{8,14},{9,15},{10,... | collective-permute-start | bytes 393224 | tf_op jit(solution)/shard_map/ppermute | solution.py:376
  69.4 1.2 %collective-permute-done.17.refs_3_ = bf16[2,256,128]{2,1,0:T(8,128)(2,1)S(1)} collective-permute-done((bf16[2,256,128]{2,1,0:T(8,128)(2,1)S(1)}, bf16[2,256,128]{2,1,0:T(8,128)(2,1)S(1)}, u32[]{:S(2)}, u32[]{:S(2)}) %collective-permute-start.17) | collective-permute-done | bytes 131104 | tf_op jit(solution)/shard_map/ppermute | solution.py:376
  71.8 6.1 %collective-permute-done.12.refs_0_ = bf16[2,256,128]{2,1,0:T(8,128)(2,1)S(1)} collective-permute-done((bf16[2,256,128]{2,1,0:T(8,128)(2,1)S(1)}, bf16[2,256,128]{2,1,0:T(8,128)(2,1)S(1)}, u32[]{:S(2)}, u32[]{:S(2)}) %collective-permute-start.12) | collective-permute-done | bytes 131104 | tf_op jit(solution)/shard_map/ppermute | solution.py:376
  77.9 2.8 %collective-permute-done.13.refs_1_ = bf16[2,256,128]{2,1,0:T(8,128)(2,1)S(1)} collective-permute-done((bf16[2,256,128]{2,1,0:T(8,128)(2,1)S(1)}, bf16[2,256,128]{2,1,0:T(8,128)(2,1)S(1)}, u32[]{:S(2)}, u32[]{:S(2)}) %collective-permute-start.13) | collective-permute-done | bytes 131104 | tf_op jit(solution)/shard_map/ppermute | solution.py:376
  80.7 1.4 %collective-permute-done.14.refs_2_ = bf16[2,256,128]{2,1,0:T(8,128)(2,1)S(1)} collective-permute-done((bf16[2,256,128]{2,1,0:T(8,128)(2,1)S(1)}, bf16[2,256,128]{2,1,0:T(8,128)(2,1)S(1)}, u32[]{:S(2)}, u32[]{:S(2)}) %collective-permute-start.14) | collective-permute-done | bytes 131104 | tf_op jit(solution)/shard_map/ppermute | solution.py:376
  82.1 5.2 %collective-permute-done.15.refs_3_ = bf16[2,256,128]{2,1,0:T(8,128)(2,1)S(1)} collective-permute-done((bf16[2,256,128]{2,1,0:T(8,128)(2,1)S(1)}, bf16[2,256,128]{2,1,0:T(8,128)(2,1)S(1)}, u32[]{:S(2)}, u32[]{:S(2)}) %collective-permute-start.15) | collective-permute-done | bytes 131104 | tf_op jit(solution)/shard_map/ppermute | solution.py:376
  87.3 2.0 %near_late.1 = f32[8,256,128]{2,1,0:T(8,128)} custom-call(s32[16]{0:T(128)S(1)} %get-tuple-element.39.targets, s32[16]{0:T(128)S(1)} %get-tuple-element.40.starts, f32[16]{0:T(128)S(1)} %bitcast_multiply_fusion.scales, f32[4]{0:T(128)S(1)} %convert_element_type.40.kernel, bf16[2,256,128]{2,1,0:T(8,128)(2,1)S(1)} %collective-permute-done.12.refs_0_, ...), custom_call_target="tpu_custom_call" | custom-call | tf_op jit(solution)/shard_map/near_late/pallas_call | solution.py:285
  (77 shorter events, 13.5 us)
Async XLA Ops:
  3.6 34.7 %all-to-all-start = ((bf16[16,128,256]{2,1,0:T(8,128)(2,1)}), bf16[16,128,256]{2,1,0:T(8,128)(2,1)S(1)}, u32[]{:S(2)}, u32[]{:S(2)}) async-start(bf16[16,128,256]{2,1,0:T(8,128)(2,1)} %bitcast.50), calls=%async_computation | async-start | bytes 2097152 | tf_op jit(solution)/shard_map/all_to_all | solution.py:351
  11.0 0.7 copy-start.1
  12.3 0.7 copy-start.3
  13.0 1.3 %collective-permute-start = (s32[1,4,16]{2,1,0:T(4,128)S(1)}, s32[1,4,16]{2,1,0:T(4,128)S(1)}, u32[]{:S(2)}, u32[]{:S(2)}) collective-permute-start(s32[1,4,16]{2,1,0:T(4,128)S(1)} %add_bitcast_fusion), channel_id=1, source_target_pairs={{0,1},{1,0},{2,3},{3,2},{4,5},{5,4},{6,7},{7,6},{8,9},{9,8},{10,11... | collective-permute-start | bytes 776 | tf_op jit(solution)/shard_map/ppermute | solution.py:254
  14.3 5.1 %collective-permute-start.1 = (s32[2,4,16]{2,1,0:T(4,128)S(1)}, s32[2,4,16]{2,1,0:T(4,128)S(1)}, u32[]{:S(2)}, u32[]{:S(2)}) collective-permute-start(s32[2,4,16]{2,1,0:T(4,128)S(1)} %add_select_fusion.4), channel_id=1, source_target_pairs={{0,2},{1,3},{2,0},{3,1},{4,6},{5,7},{6,4},{7,5},{8,10},{9,11},{10,... | collective-permute-start | bytes 1544 | tf_op jit(solution)/shard_map/ppermute | solution.py:254
  19.4 9.8 %collective-permute-start.2 = (s32[4,4,16]{2,1,0:T(4,128)S(1)}, s32[4,4,16]{2,1,0:T(4,128)S(1)}, u32[]{:S(2)}, u32[]{:S(2)}) collective-permute-start(s32[4,4,16]{2,1,0:T(4,128)S(1)} %add_select_fusion.3), channel_id=1, source_target_pairs={{0,4},{1,5},{2,6},{3,7},{4,0},{5,1},{6,2},{7,3},{8,12},{9,13},{10,... | collective-permute-start | bytes 3080 | tf_op jit(solution)/shard_map/ppermute | solution.py:254
  29.2 9.0 %collective-permute-start.3 = (s32[8,4,16]{2,1,0:T(4,128)S(1)}, s32[8,4,16]{2,1,0:T(4,128)S(1)}, u32[]{:S(2)}, u32[]{:S(2)}) collective-permute-start(s32[8,4,16]{2,1,0:T(4,128)S(1)} %add_select_fusion.1), channel_id=1, source_target_pairs={{0,8},{1,9},{2,10},{3,11},{4,12},{5,13},{6,14},{7,15},{8,0},{9,1},... | collective-permute-start | bytes 6152 | tf_op jit(solution)/shard_map/ppermute | solution.py:254
  43.4 5.3 %collective-permute-start.4 = (bf16[8,256,128]{2,1,0:T(8,128)(2,1)}, bf16[8,256,128]{2,1,0:T(8,128)(2,1)S(1)}, u32[]{:S(2)}, u32[]{:S(2)}) collective-permute-start(bf16[8,256,128]{2,1,0:T(8,128)(2,1)} %get-tuple-element.31), channel_id=1, source_target_pairs={{0,1},{1,0},{2,3},{3,2},{4,5},{5,4},{6,7},{7,6},{8,9},{9,8},{10,11... | collective-permute-start | bytes 1572872 | tf_op jit(solution)/shard_map/ppermute | solution.py:376
  43.5 6.8 %collective-permute-start.6 = (bf16[8,256,128]{2,1,0:T(8,128)(2,1)}, bf16[8,256,128]{2,1,0:T(8,128)(2,1)S(1)}, u32[]{:S(2)}, u32[]{:S(2)}) collective-permute-start(bf16[8,256,128]{2,1,0:T(8,128)(2,1)} %get-tuple-element.36), channel_id=1, source_target_pairs={{0,1},{1,0},{2,3},{3,2},{4,5},{5,4},{6,7},{7,6},{8,9},{9,8},{10,11... | collective-permute-start | bytes 1572872 | tf_op jit(solution)/shard_map/ppermute | solution.py:376
  45.2 7.6 %collective-permute-start.10 = (bf16[2,256,128]{2,1,0:T(8,128)(2,1)S(1)}, bf16[2,256,128]{2,1,0:T(8,128)(2,1)S(1)}, u32[]{:S(2)}, u32[]{:S(2)}) collective-permute-start(bf16[2,256,128]{2,1,0:T(8,128)(2,1)S(1)} %get-tuple-element.63), channel_id=1, source_target_pairs={{0,2},{1,3},{2,0},{3,1},{4,6},{5,7},{6,4},{7,5},{8,10},{9,11},{10,... | collective-permute-start | bytes 393224 | tf_op jit(solution)/shard_map/ppermute | solution.py:376
  46.7 12.4 %collective-permute-start.5 = (bf16[2,256,128]{2,1,0:T(8,128)(2,1)S(1)}, bf16[2,256,128]{2,1,0:T(8,128)(2,1)S(1)}, u32[]{:S(2)}, u32[]{:S(2)}) collective-permute-start(bf16[2,256,128]{2,1,0:T(8,128)(2,1)S(1)} %get-tuple-element.66), channel_id=1, source_target_pairs={{0,4},{1,5},{2,6},{3,7},{4,0},{5,1},{6,2},{7,3},{8,12},{9,13},{10,... | collective-permute-start | bytes 393224 | tf_op jit(solution)/shard_map/ppermute | solution.py:376
  46.7 12.4 %collective-permute-start.8 = (bf16[2,256,128]{2,1,0:T(8,128)(2,1)S(1)}, bf16[2,256,128]{2,1,0:T(8,128)(2,1)S(1)}, u32[]{:S(2)}, u32[]{:S(2)}) collective-permute-start(bf16[2,256,128]{2,1,0:T(8,128)(2,1)S(1)} %get-tuple-element.65), channel_id=1, source_target_pairs={{0,6},{1,7},{2,4},{3,5},{4,2},{5,3},{6,0},{7,1},{8,14},{9,15},{10,... | collective-permute-start | bytes 393224 | tf_op jit(solution)/shard_map/ppermute | solution.py:376
  50.3 7.8 %collective-permute-start.11 = (bf16[2,256,128]{2,1,0:T(8,128)(2,1)S(1)}, bf16[2,256,128]{2,1,0:T(8,128)(2,1)S(1)}, u32[]{:S(2)}, u32[]{:S(2)}) collective-permute-start(bf16[2,256,128]{2,1,0:T(8,128)(2,1)S(1)} %get-tuple-element.59), channel_id=1, source_target_pairs={{0,2},{1,3},{2,0},{3,1},{4,6},{5,7},{6,4},{7,5},{8,10},{9,11},{10,... | collective-permute-start | bytes 393224 | tf_op jit(solution)/shard_map/ppermute | solution.py:376
  52.1 0.7 copy-start.5
  52.7 6.4 %collective-permute-start.7 = (bf16[2,256,128]{2,1,0:T(8,128)(2,1)S(1)}, bf16[2,256,128]{2,1,0:T(8,128)(2,1)S(1)}, u32[]{:S(2)}, u32[]{:S(2)}) collective-permute-start(bf16[2,256,128]{2,1,0:T(8,128)(2,1)S(1)} %get-tuple-element.62), channel_id=1, source_target_pairs={{0,4},{1,5},{2,6},{3,7},{4,0},{5,1},{6,2},{7,3},{8,12},{9,13},{10,... | collective-permute-start | bytes 393224 | tf_op jit(solution)/shard_map/ppermute | solution.py:376
  52.8 7.5 %collective-permute-start.9 = (bf16[2,256,128]{2,1,0:T(8,128)(2,1)S(1)}, bf16[2,256,128]{2,1,0:T(8,128)(2,1)S(1)}, u32[]{:S(2)}, u32[]{:S(2)}) collective-permute-start(bf16[2,256,128]{2,1,0:T(8,128)(2,1)S(1)} %get-tuple-element.61), channel_id=1, source_target_pairs={{0,6},{1,7},{2,4},{3,5},{4,2},{5,3},{6,0},{7,1},{8,14},{9,15},{10,... | collective-permute-start | bytes 393224 | tf_op jit(solution)/shard_map/ppermute | solution.py:376
  59.1 3.6 %copy-start = (bf16[8,256,128]{2,1,0:T(8,128)(2,1)S(1)}, bf16[8,256,128]{2,1,0:T(8,128)(2,1)}, u32[]{:S(2)}) copy-start(bf16[8,256,128]{2,1,0:T(8,128)(2,1)} %get-tuple-element.42) | copy-start | bytes 1572868
  61.4 25.9 %collective-permute-start.18 = (bf16[8,256,128]{2,1,0:T(8,128)(2,1)S(1)}, bf16[8,256,128]{2,1,0:T(8,128)(2,1)S(1)}, u32[]{:S(2)}, u32[]{:S(2)}) collective-permute-start(bf16[8,256,128]{2,1,0:T(8,128)(2,1)S(1)} %far_late.1), channel_id=1, source_target_pairs={{0,8},{1,9},{2,10},{3,11},{4,12},{5,13},{6,14},{7,15},{8,0},{9,1},... | collective-permute-start | bytes 1572872 | tf_op jit(solution)/shard_map/ppermute | solution.py:404
  62.7 5.0 %collective-permute-start.16 = (bf16[2,256,128]{2,1,0:T(8,128)(2,1)S(1)}, bf16[2,256,128]{2,1,0:T(8,128)(2,1)S(1)}, u32[]{:S(2)}, u32[]{:S(2)}) collective-permute-start(bf16[2,256,128]{2,1,0:T(8,128)(2,1)S(1)} %get-tuple-element.55), channel_id=1, source_target_pairs={{0,2},{1,3},{2,0},{3,1},{4,6},{5,7},{6,4},{7,5},{8,10},{9,11},{10,... | collective-permute-start | bytes 393224 | tf_op jit(solution)/shard_map/ppermute | solution.py:376
  63.3 7.3 %collective-permute-start.17 = (bf16[2,256,128]{2,1,0:T(8,128)(2,1)S(1)}, bf16[2,256,128]{2,1,0:T(8,128)(2,1)S(1)}, u32[]{:S(2)}, u32[]{:S(2)}) collective-permute-start(bf16[2,256,128]{2,1,0:T(8,128)(2,1)S(1)} %get-tuple-element.51), channel_id=1, source_target_pairs={{0,2},{1,3},{2,0},{3,1},{4,6},{5,7},{6,4},{7,5},{8,10},{9,11},{10,... | collective-permute-start | bytes 393224 | tf_op jit(solution)/shard_map/ppermute | solution.py:376
  64.9 13.0 %collective-permute-start.12 = (bf16[2,256,128]{2,1,0:T(8,128)(2,1)S(1)}, bf16[2,256,128]{2,1,0:T(8,128)(2,1)S(1)}, u32[]{:S(2)}, u32[]{:S(2)}) collective-permute-start(bf16[2,256,128]{2,1,0:T(8,128)(2,1)S(1)} %get-tuple-element.58), channel_id=1, source_target_pairs={{0,4},{1,5},{2,6},{3,7},{4,0},{5,1},{6,2},{7,3},{8,12},{9,13},{10,... | collective-permute-start | bytes 393224 | tf_op jit(solution)/shard_map/ppermute | solution.py:376
  65.7 15.0 %collective-permute-start.13 = (bf16[2,256,128]{2,1,0:T(8,128)(2,1)S(1)}, bf16[2,256,128]{2,1,0:T(8,128)(2,1)S(1)}, u32[]{:S(2)}, u32[]{:S(2)}) collective-permute-start(bf16[2,256,128]{2,1,0:T(8,128)(2,1)S(1)} %get-tuple-element.54), channel_id=1, source_target_pairs={{0,4},{1,5},{2,6},{3,7},{4,0},{5,1},{6,2},{7,3},{8,12},{9,13},{10,... | collective-permute-start | bytes 393224 | tf_op jit(solution)/shard_map/ppermute | solution.py:376
  67.8 14.3 %collective-permute-start.14 = (bf16[2,256,128]{2,1,0:T(8,128)(2,1)S(1)}, bf16[2,256,128]{2,1,0:T(8,128)(2,1)S(1)}, u32[]{:S(2)}, u32[]{:S(2)}) collective-permute-start(bf16[2,256,128]{2,1,0:T(8,128)(2,1)S(1)} %get-tuple-element.57), channel_id=1, source_target_pairs={{0,6},{1,7},{2,4},{3,5},{4,2},{5,3},{6,0},{7,1},{8,14},{9,15},{10,... | collective-permute-start | bytes 393224 | tf_op jit(solution)/shard_map/ppermute | solution.py:376
  70.6 16.7 %collective-permute-start.15 = (bf16[2,256,128]{2,1,0:T(8,128)(2,1)S(1)}, bf16[2,256,128]{2,1,0:T(8,128)(2,1)S(1)}, u32[]{:S(2)}, u32[]{:S(2)}) collective-permute-start(bf16[2,256,128]{2,1,0:T(8,128)(2,1)S(1)} %get-tuple-element.53), channel_id=1, source_target_pairs={{0,6},{1,7},{2,4},{3,5},{4,2},{5,3},{6,0},{7,1},{8,14},{9,15},{10,... | collective-permute-start | bytes 393224 | tf_op jit(solution)/shard_map/ppermute | solution.py:376
  (2 other events, 1.3 us)

commit v6 on v5

--- a/solution.py
+++ b/solution.py
@@ -207,7 +207,7 @@
             ]
             for route, copy in enumerate(routed):
                 pl.when(routes[at] == route)(copy.start)
-            copies.append(routed[0])
+            copies.append(pltpu.make_async_copy(tiles.at[at], buffers[0].at[0], sems.at[at]))
     for copy in copies:
         copy.wait()
 
@@ -246,16 +246,10 @@
 
 def gathered(block, axis_name):
     peers = lax.axis_size(axis_name)
-    if peers & (peers - 1):
-        return lax.all_gather(block, axis_name, axis=0, tiled=True)
-    me = lax.axis_index(axis_name)
     step = 1
     while step < peers:
         other = lax.ppermute(block, axis_name, [(i, i ^ step) for i in range(peers)])
-        lower = (me & step) == 0
-        block = jnp.where(
-            lower, jnp.concatenate([block, other], axis=0), jnp.concatenate([other, block], axis=0)
-        )
+        block = jnp.concatenate([block, other], axis=0)
         step *= 2
     return block
 
@@ -331,8 +325,8 @@
         compiler_params=wide_params,
         name="filter",
     )(filter_lengths, filter_taps, radar_stack)
-    sent, tile_owner, map_slot, correlation, offsets = lax.optimization_barrier(
-        (sent, tile_owner, map_slot, correlation, offsets)
+    sent, tile_owner, map_slot, correlation, offsets, resample_kernel = lax.optimization_barrier(
+        (sent, tile_owner, map_slot, correlation, offsets, resample_kernel)
     )
     owners = tile_owner[:, 0]
     tile_iota = jnp.arange(tile_count, dtype=jnp.int32)
@@ -341,28 +335,35 @@
         owners[:, None] == owners[None, :], tile_iota[None, :] < tile_iota[:, None]
     )
     half = peers // 2
+    assert peers & (peers - 1) == 0
     ranks = jnp.sum(earlier, axis=1).astype(jnp.int32)
     step = (owners % half) ^ (me % half)
     leaves = owners // half != me // half
-    slots = step // 2 * CAP + ranks
-    routes = jnp.where(leaves, 0, 2) + step % 2
+    chips = half // 2
+    alone = jnp.logical_and(leaves, step % 2 == 0)
+    slots = jnp.where(alone, 0, step // 2 * CAP) + ranks
+    routes = jnp.where(alone, step // 2, chips + jnp.where(leaves, 0, 1 + step % 2))
     details = jnp.stack([owners * CAP + ranks, map_slot, starts_here, correlation], axis=0)[None]
     sent = sent.reshape(peers, line_count * 2 * dates_here, ranges_count)
     got_lines = lax.all_to_all(sent, "date", split_axis=0, concat_axis=0, tiled=True)
     all_details = gathered(details, "date")
-    got_lines, all_details = lax.optimization_barrier((got_lines, all_details))
+    rounded_kernel = lax.optimization_barrier(resample_kernel.astype(jnp.bfloat16)).astype(jnp.float32)
+    got_lines, all_details, rounded_kernel = lax.optimization_barrier(
+        (got_lines, all_details, rounded_kernel)
+    )
 
     mixed = dates_here == 8 and peers % 2 == 0
     got_lines = got_lines.reshape(peers, line_count, 2 * dates_here, ranges_count)
     if not mixed:
         got_lines = got_lines.reshape(peers, line_count, 2, dates_here, ranges_count)
         got_lines = got_lines.transpose(1, 2, 0, 3, 4).reshape(1, line_count, 2 * dates, ranges_count)
-    buffer = pltpu.HBM((half // 2 * CAP, 2 * dates, TILE), jnp.bfloat16)
-    leaving_same, leaving_other, same, other = pl.pallas_call(
+    buffer = pltpu.HBM((chips * CAP, 2 * dates, TILE), jnp.bfloat16)
+    chip_buffer = pltpu.HBM((CAP, 2 * dates, TILE), jnp.bfloat16)
+    *leaving_same, leaving_other, same, other = pl.pallas_call(
         partial(whiten_kernel, mixed=mixed),
-        out_shape=(buffer,) * 4,
+        out_shape=(chip_buffer,) * chips + (buffer,) * 3,
         in_specs=[SMEM, SMEM, VMEM],
-        out_specs=(HBM,) * 4,
+        out_specs=(HBM,) * (chips + 3),
         scratch_shapes=[
             pltpu.VMEM((window_count, 2 * dates, TILE), jnp.bfloat16),
             pltpu.VMEM((tile_count, 2 * dates, TILE), jnp.bfloat16),
@@ -375,23 +376,22 @@
     def exchanged(values, step):
         return lax.ppermute(values, "date", [(i, i ^ step) for i in range(peers)])
 
+    def by_chip(cells):
+        return [cells[k * CAP : (k + 1) * CAP] for k in range(chips)]
+
     def from_chips(mine, received):
         tiles = []
-        for k in range(half // 2):
-            at = slice(k * CAP, (k + 1) * CAP)
-            tiles += [exchanged(cells[at], 2 * k) if k else cells[at] for cells in (mine, received)]
+        for k, both in enumerate(zip(mine, received)):
+            tiles += [exchanged(cells, 2 * k) if k else cells for cells in both]
         return tiles
 
     early = half // 2
     early_slots = early * CAP
-    far_tiles = from_chips(leaving_same, exchanged(leaving_other, 1))
+    received = exchanged(leaving_other, 1)
+    far_tiles = from_chips(leaving_same, by_chip(received))
     other = exchanged(other, 1)
-    other, all_details, resample_kernel = lax.optimization_barrier(
-        (other, all_details, resample_kernel)
-    )
-    rounded_kernel = lax.optimization_barrier(resample_kernel.astype(jnp.bfloat16)).astype(jnp.float32)
-    senders = jnp.arange(half, dtype=jnp.int32) ^ (me % half)
-    near = jnp.take(all_details, me // half * half + senders, axis=0)
+    other, all_details = lax.optimization_barrier((other, all_details))
+    near = all_details[:half]
     far_lists = arrivals((me + half) % peers, near, all_details)
     near_lists = arrivals(me, near, all_details)
     far_begun = map_sum(far_lists, rounded_kernel, far_tiles[:early], jnp.float32, "far_early", 0)
@@ -402,7 +402,7 @@
         (partial_sums, same, other, near_lists)
     )
     from_far = lax.ppermute(partial_sums, "date", [(i, (i + half) % peers) for i in range(peers)])
-    near_tiles = from_chips(same, other)
+    near_tiles = from_chips(by_chip(same), by_chip(other))
     near_begun = map_sum(near_lists, rounded_kernel, near_tiles[:early], jnp.float32, "near_early", 0)
     return map_sum(
         near_lists,

time: 89.6 us -> 89.1 us (level)
  local copies, waits for them, and re-layouts: 4.63 us -> 2.94 us
  waiting for transfers between devices: 39.7 us -> 40.6 us
    ppermute x14, waiting for transfers between devices: 21.9 us -> 23.5 us  [exchanged(): return lax.ppermute(values, 'date', [(i, i ^ step) for i in range(peers)])]
    slice x4 -> x3, local copies, waits for them, and re-layouts: 1.23 us -> 0.11 us  [by_chip(): return [cells[k * CAP:(k + 1) * CAP] for k in range(chips)]]
    unnamed x12 -> x17, local copies, waits for them, and re-layouts: 2.44 us -> 2.45 us
  transfers between devices with their start and end apart: 20 -> 20, of which waited for: 12 -> 13; matrix products, arithmetic and copies ran while one was open for 4% -> 2% of each run, Pallas kernels for 2% -> 2%
where the time goes in v6:
time: 89.1 us; the launch traced here: 88.9 us
  waiting for transfers between devices  40.6 us (46%)
  starting transfers between devices  30.4 us (34%)
  Pallas kernels  13.7 us (15%)
  local copies, waits for them, and re-layouts  2.94 us (3%)
  other arithmetic  1.02 us (1%)
    ppermute x14, waiting for transfers between devices, exchanged(): return lax.ppermute(values, 'date', [(i, i ^ step) for i in range(peers)])  23.5 us
    ppermute x4, waiting for transfers between devices, gathered(): lax.ppermute(block, axis_name, [(i, i ^ step) for i in range(peers)])  17.1 us
    ppermute x14, starting transfers between devices, exchanged(): return lax.ppermute(values, 'date', [(i, i ^ step) for i in range(peers)])  14.3 us
    all_to_all x1, starting transfers between devices, shards(): lax.all_to_all(sent, 'date', split_axis=0, concat_axis=0, tiled=True)  7.4 us
    ppermute x4, starting transfers between devices, gathered(): lax.ppermute(block, axis_name, [(i, i ^ step) for i in range(peers)])  7.34 us
    pallas_call x1, Pallas kernels, shards(): pl.pallas_call(partial(whiten_kernel, mixed=mixed), out_shape=(chip_buffe...  5.11 us
    pallas_call x4, Pallas kernels, map_sum(): pl.pallas_call(partial(map_kernel, arrays=len(tiles), first_slot=first_sl...  5.01 us
    pallas_call x1, Pallas kernels, shards(): pl.pallas_call(filter_kernel, out_shape=pltpu.HBM((rows_count * 2 * dates...  3.58 us
  transfers between devices with their start and end apart: 20, of which 13 were waited for; matrix products, arithmetic and copies ran while one was open for 2% of the time, Pallas kernels for 2%

profile of v6, /device:TPU:0, one launch (start us, length us, event | category | flops | bytes accessed | tf_op | source)
XLA Modules:
  0.0 88.9 jit_solution(13686483237272715756)
XLA Ops:
  0.0 3.6 %filter.1 = bf16[2048,256]{1,0:T(8,128)(2,1)} custom-call(s32[8]{0:T(128)} %lengths_hbm.1, f32[2,8,128]{2,1,0:T(8,128)} %taps_hbm.1, bf16[2,8,128,256]{3,2,1,0:T(8,128)(2,1)} %radar.1), custom_call_target="tpu_custom_call" | custom-call | tf_op jit(solution)/shard_map/filter/pallas_call | solution.py:311
  3.6 7.4 %all-to-all-start = ((bf16[16,128,256]{2,1,0:T(8,128)(2,1)}), bf16[16,128,256]{2,1,0:T(8,128)(2,1)S(1)}, u32[]{:S(2)}, u32[]{:S(2)}) async-start(bf16[16,128,256]{2,1,0:T(8,128)(2,1)} %bitcast.51), calls=%async_computation | async-start | bytes 2097152 | tf_op jit(solution)/shard_map/all_to_all | solution.py:348
  14.3 1.9 %collective-permute-start.1 = (s32[2,4,16]{2,1,0:T(4,128)S(1)}, s32[2,4,16]{2,1,0:T(4,128)S(1)}, u32[]{:S(2)}, u32[]{:S(2)}) collective-permute-start(s32[2,4,16]{2,1,0:T(4,128)S(1)} %pad_add_fusion.2), channel_id=1, source_target_pairs={{0,2},{1,3},{2,0},{3,1},{4,6},{5,7},{6,4},{7,5},{8,10},{9,11},{10,... | collective-permute-start | bytes 1544 | tf_op jit(solution)/shard_map/ppermute | solution.py:251
  16.2 3.2 %collective-permute-done.1 = s32[2,4,16]{2,1,0:T(4,128)S(1)} collective-permute-done((s32[2,4,16]{2,1,0:T(4,128)S(1)}, s32[2,4,16]{2,1,0:T(4,128)S(1)}, u32[]{:S(2)}, u32[]{:S(2)}) %collective-permute-start.1) | collective-permute-done | bytes 544 | tf_op jit(solution)/shard_map/ppermute | solution.py:251
  20.0 9.2 %collective-permute-done.2 = s32[4,4,16]{2,1,0:T(4,128)S(1)} collective-permute-done((s32[4,4,16]{2,1,0:T(4,128)S(1)}, s32[4,4,16]{2,1,0:T(4,128)S(1)}, u32[]{:S(2)}, u32[]{:S(2)}) %collective-permute-start.2) | collective-permute-done | bytes 1056 | tf_op jit(solution)/shard_map/ppermute | solution.py:251
  29.2 4.4 %collective-permute-start.3 = (s32[8,4,16]{2,1,0:T(4,128)S(1)}, s32[8,4,16]{2,1,0:T(4,128)S(1)}, u32[]{:S(2)}, u32[]{:S(2)}) collective-permute-start(s32[8,4,16]{2,1,0:T(4,128)S(1)} %pad_add_fusion), channel_id=1, source_target_pairs={{0,8},{1,9},{2,10},{3,11},{4,12},{5,13},{6,14},{7,15},{8,0},{9,1},... | collective-permute-start | bytes 6152 | tf_op jit(solution)/shard_map/ppermute | solution.py:251
  33.7 4.6 %collective-permute-done.3 = s32[8,4,16]{2,1,0:T(4,128)S(1)} collective-permute-done((s32[8,4,16]{2,1,0:T(4,128)S(1)}, s32[8,4,16]{2,1,0:T(4,128)S(1)}, u32[]{:S(2)}, u32[]{:S(2)}) %collective-permute-start.3) | collective-permute-done | bytes 2080 | tf_op jit(solution)/shard_map/ppermute | solution.py:251
  38.3 5.1 %whiten.1 = (bf16[2,256,128]{2,1,0:T(8,128)(2,1)}, bf16[2,256,128]{2,1,0:T(8,128)(2,1)}, bf16[2,256,128]{2,1,0:T(8,128)(2,1)}, bf16[2,256,128]{2,1,0:T(8,128)(2,...) custom-call(s32[16]{0:T(128)S(1)} %select_add_fusion.slots, ...), custom_call_target="tpu_custom_call" | custom-call | tf_op jit(solution)/shard_map/whiten/pallas_call | solution.py:362
  44.0 1.5 %collective-permute-start.10 = (bf16[2,256,128]{2,1,0:T(8,128)(2,1)}, bf16[2,256,128]{2,1,0:T(8,128)(2,1)S(1)}, u32[]{:S(2)}, u32[]{:S(2)}) collective-permute-start(bf16[2,256,128]{2,1,0:T(8,128)(2,1)} %get-tuple-element.44), channel_id=1, source_target_pairs={{0,2},{1,3},{2,0},{3,1},{4,6},{5,7},{6,4},{7,5},{8,10},{9,11},{10,... | collective-permute-start | bytes 393224 | tf_op jit(solution)/shard_map/ppermute | solution.py:377
  45.4 2.0 %collective-permute-start.8 = (bf16[2,256,128]{2,1,0:T(8,128)(2,1)}, bf16[2,256,128]{2,1,0:T(8,128)(2,1)S(1)}, u32[]{:S(2)}, u32[]{:S(2)}) collective-permute-start(bf16[2,256,128]{2,1,0:T(8,128)(2,1)} %get-tuple-element.42), channel_id=1, source_target_pairs={{0,6},{1,7},{2,4},{3,5},{4,2},{5,3},{6,0},{7,1},{8,14},{9,15},{10,... | collective-permute-start | bytes 393224 | tf_op jit(solution)/shard_map/ppermute | solution.py:377
  48.4 1.6 %collective-permute-start.11 = (bf16[2,256,128]{2,1,0:T(8,128)(2,1)S(1)}, bf16[2,256,128]{2,1,0:T(8,128)(2,1)S(1)}, u32[]{:S(2)}, u32[]{:S(2)}) collective-permute-start(bf16[2,256,128]{2,1,0:T(8,128)(2,1)S(1)} %get-tuple-element.69), channel_id=1, source_target_pairs={{0,2},{1,3},{2,0},{3,1},{4,6},{5,7},{6,4},{7,5},{8,10},{9,11},{10,... | collective-permute-start | bytes 393224 | tf_op jit(solution)/shard_map/ppermute | solution.py:377
  50.3 2.0 %collective-permute-start.9 = (bf16[2,256,128]{2,1,0:T(8,128)(2,1)S(1)}, bf16[2,256,128]{2,1,0:T(8,128)(2,1)S(1)}, u32[]{:S(2)}, u32[]{:S(2)}) collective-permute-start(bf16[2,256,128]{2,1,0:T(8,128)(2,1)S(1)} %get-tuple-element.71), channel_id=1, source_target_pairs={{0,6},{1,7},{2,4},{3,5},{4,2},{5,3},{6,0},{7,1},{8,14},{9,15},{10,... | collective-permute-start | bytes 393224 | tf_op jit(solution)/shard_map/ppermute | solution.py:377
  52.4 3.6 %collective-permute-done.11.refs_3_ = bf16[2,256,128]{2,1,0:T(8,128)(2,1)S(1)} collective-permute-done((bf16[2,256,128]{2,1,0:T(8,128)(2,1)S(1)}, bf16[2,256,128]{2,1,0:T(8,128)(2,1)S(1)}, u32[]{:S(2)}, u32[]{:S(2)}) %collective-permute-start.11) | collective-permute-done | bytes 131104 | tf_op jit(solution)/shard_map/ppermute | solution.py:377
  57.7 1.6 %collective-permute-done.9.refs_3_ = bf16[2,256,128]{2,1,0:T(8,128)(2,1)S(1)} collective-permute-done((bf16[2,256,128]{2,1,0:T(8,128)(2,1)S(1)}, bf16[2,256,128]{2,1,0:T(8,128)(2,1)S(1)}, u32[]{:S(2)}, u32[]{:S(2)}) %collective-permute-start.9) | collective-permute-done | bytes 131104 | tf_op jit(solution)/shard_map/ppermute | solution.py:377
  60.3 1.3 %collective-permute-start.18 = (bf16[8,256,128]{2,1,0:T(8,128)(2,1)S(1)}, bf16[8,256,128]{2,1,0:T(8,128)(2,1)S(1)}, u32[]{:S(2)}, u32[]{:S(2)}) collective-permute-start(bf16[8,256,128]{2,1,0:T(8,128)(2,1)S(1)} %far_late.1), channel_id=1, source_target_pairs={{0,8},{1,9},{2,10},{3,11},{4,12},{5,13},{6,14},{7,15},{8,0},{9,1},... | collective-permute-start | bytes 1572872 | tf_op jit(solution)/shard_map/ppermute | solution.py:404
  62.3 1.6 %collective-permute-start.17 = (bf16[2,256,128]{2,1,0:T(8,128)(2,1)S(1)}, bf16[2,256,128]{2,1,0:T(8,128)(2,1)S(1)}, u32[]{:S(2)}, u32[]{:S(2)}) collective-permute-start(bf16[2,256,128]{2,1,0:T(8,128)(2,1)S(1)} %get-tuple-element.61), channel_id=1, source_target_pairs={{0,2},{1,3},{2,0},{3,1},{4,6},{5,7},{6,4},{7,5},{8,10},{9,11},{10,... | collective-permute-start | bytes 393224 | tf_op jit(solution)/shard_map/ppermute | solution.py:377
  64.6 1.3 %collective-permute-start.13 = (bf16[2,256,128]{2,1,0:T(8,128)(2,1)S(1)}, bf16[2,256,128]{2,1,0:T(8,128)(2,1)S(1)}, u32[]{:S(2)}, u32[]{:S(2)}) collective-permute-start(bf16[2,256,128]{2,1,0:T(8,128)(2,1)S(1)} %get-tuple-element.64), channel_id=1, source_target_pairs={{0,4},{1,5},{2,6},{3,7},{4,0},{5,1},{6,2},{7,3},{8,12},{9,13},{10,... | collective-permute-start | bytes 393224 | tf_op jit(solution)/shard_map/ppermute | solution.py:377
  65.9 1.3 %collective-permute-done.16.refs_2_ = bf16[2,256,128]{2,1,0:T(8,128)(2,1)S(1)} collective-permute-done((bf16[2,256,128]{2,1,0:T(8,128)(2,1)S(1)}, bf16[2,256,128]{2,1,0:T(8,128)(2,1)S(1)}, u32[]{:S(2)}, u32[]{:S(2)}) %collective-permute-start.16) | collective-permute-done | bytes 131104 | tf_op jit(solution)/shard_map/ppermute | solution.py:377
  67.2 1.6 %collective-permute-start.14 = (bf16[2,256,128]{2,1,0:T(8,128)(2,1)S(1)}, bf16[2,256,128]{2,1,0:T(8,128)(2,1)S(1)}, u32[]{:S(2)}, u32[]{:S(2)}) collective-permute-start(bf16[2,256,128]{2,1,0:T(8,128)(2,1)S(1)} %get-tuple-element.67), channel_id=1, source_target_pairs={{0,6},{1,7},{2,4},{3,5},{4,2},{5,3},{6,0},{7,1},{8,14},{9,15},{10,... | collective-permute-start | bytes 393224 | tf_op jit(solution)/shard_map/ppermute | solution.py:377
  71.3 5.6 %collective-permute-done.12.refs_0_ = bf16[2,256,128]{2,1,0:T(8,128)(2,1)S(1)} collective-permute-done((bf16[2,256,128]{2,1,0:T(8,128)(2,1)S(1)}, bf16[2,256,128]{2,1,0:T(8,128)(2,1)S(1)}, u32[]{:S(2)}, u32[]{:S(2)}) %collective-permute-start.12) | collective-permute-done | bytes 131104 | tf_op jit(solution)/shard_map/ppermute | solution.py:377
  76.8 2.8 %collective-permute-done.13.refs_1_ = bf16[2,256,128]{2,1,0:T(8,128)(2,1)S(1)} collective-permute-done((bf16[2,256,128]{2,1,0:T(8,128)(2,1)S(1)}, bf16[2,256,128]{2,1,0:T(8,128)(2,1)S(1)}, u32[]{:S(2)}, u32[]{:S(2)}) %collective-permute-start.13) | collective-permute-done | bytes 131104 | tf_op jit(solution)/shard_map/ppermute | solution.py:377
  79.6 2.2 %collective-permute-done.14.refs_2_ = bf16[2,256,128]{2,1,0:T(8,128)(2,1)S(1)} collective-permute-done((bf16[2,256,128]{2,1,0:T(8,128)(2,1)S(1)}, bf16[2,256,128]{2,1,0:T(8,128)(2,1)S(1)}, u32[]{:S(2)}, u32[]{:S(2)}) %collective-permute-start.14) | collective-permute-done | bytes 131104 | tf_op jit(solution)/shard_map/ppermute | solution.py:377
  81.8 5.1 %collective-permute-done.15.refs_3_ = bf16[2,256,128]{2,1,0:T(8,128)(2,1)S(1)} collective-permute-done((bf16[2,256,128]{2,1,0:T(8,128)(2,1)S(1)}, bf16[2,256,128]{2,1,0:T(8,128)(2,1)S(1)}, u32[]{:S(2)}, u32[]{:S(2)}) %collective-permute-start.15) | collective-permute-done | bytes 131104 | tf_op jit(solution)/shard_map/ppermute | solution.py:377
  86.9 2.0 %near_late.1 = f32[8,256,128]{2,1,0:T(8,128)} custom-call(s32[16]{0:T(128)S(1)} %get-tuple-element.47.targets, s32[16]{0:T(128)S(1)} %get-tuple-element.48.starts, f32[16]{0:T(128)S(1)} %bitcast_multiply_fusion.scales, f32[4]{0:T(128)S(1)} %convert_element_type.37.kernel, bf16[2,256,128]{2,1,0:T(8,128)(2,1)S(1)} %collective-permute-done.12.refs_0_, ...), custom_call_target="tpu_custom_call" | custom-call | tf_op jit(solution)/shard_map/near_late/pallas_call | solution.py:279
  (76 shorter events, 12.1 us)
Async XLA Ops:
  3.6 34.7 %all-to-all-start = ((bf16[16,128,256]{2,1,0:T(8,128)(2,1)}), bf16[16,128,256]{2,1,0:T(8,128)(2,1)S(1)}, u32[]{:S(2)}, u32[]{:S(2)}) async-start(bf16[16,128,256]{2,1,0:T(8,128)(2,1)} %bitcast.51), calls=%async_computation | async-start | bytes 2097152 | tf_op jit(solution)/shard_map/all_to_all | solution.py:348
  11.0 0.7 copy-start.4
  12.3 0.7 copy-start.3
  13.0 1.3 %collective-permute-start = (s32[1,4,16]{2,1,0:T(4,128)S(1)}, s32[1,4,16]{2,1,0:T(4,128)S(1)}, u32[]{:S(2)}, u32[]{:S(2)}) collective-permute-start(s32[1,4,16]{2,1,0:T(4,128)S(1)} %add_bitcast_fusion), channel_id=1, source_target_pairs={{0,1},{1,0},{2,3},{3,2},{4,5},{5,4},{6,7},{7,6},{8,9},{9,8},{10,11... | collective-permute-start | bytes 776 | tf_op jit(solution)/shard_map/ppermute | solution.py:251
  14.3 5.1 %collective-permute-start.1 = (s32[2,4,16]{2,1,0:T(4,128)S(1)}, s32[2,4,16]{2,1,0:T(4,128)S(1)}, u32[]{:S(2)}, u32[]{:S(2)}) collective-permute-start(s32[2,4,16]{2,1,0:T(4,128)S(1)} %pad_add_fusion.2), channel_id=1, source_target_pairs={{0,2},{1,3},{2,0},{3,1},{4,6},{5,7},{6,4},{7,5},{8,10},{9,11},{10,... | collective-permute-start | bytes 1544 | tf_op jit(solution)/shard_map/ppermute | solution.py:251
  19.4 9.8 %collective-permute-start.2 = (s32[4,4,16]{2,1,0:T(4,128)S(1)}, s32[4,4,16]{2,1,0:T(4,128)S(1)}, u32[]{:S(2)}, u32[]{:S(2)}) collective-permute-start(s32[4,4,16]{2,1,0:T(4,128)S(1)} %pad_add_fusion.1), channel_id=1, source_target_pairs={{0,4},{1,5},{2,6},{3,7},{4,0},{5,1},{6,2},{7,3},{8,12},{9,13},{10,... | collective-permute-start | bytes 3080 | tf_op jit(solution)/shard_map/ppermute | solution.py:251
  29.2 9.0 %collective-permute-start.3 = (s32[8,4,16]{2,1,0:T(4,128)S(1)}, s32[8,4,16]{2,1,0:T(4,128)S(1)}, u32[]{:S(2)}, u32[]{:S(2)}) collective-permute-start(s32[8,4,16]{2,1,0:T(4,128)S(1)} %pad_add_fusion), channel_id=1, source_target_pairs={{0,8},{1,9},{2,10},{3,11},{4,12},{5,13},{6,14},{7,15},{8,0},{9,1},... | collective-permute-start | bytes 6152 | tf_op jit(solution)/shard_map/ppermute | solution.py:251
  43.4 4.1 %collective-permute-start.4 = (bf16[8,256,128]{2,1,0:T(8,128)(2,1)}, bf16[8,256,128]{2,1,0:T(8,128)(2,1)S(1)}, u32[]{:S(2)}, u32[]{:S(2)}) collective-permute-start(bf16[8,256,128]{2,1,0:T(8,128)(2,1)} %get-tuple-element.36), channel_id=1, source_target_pairs={{0,1},{1,0},{2,3},{3,2},{4,5},{5,4},{6,7},{7,6},{8,9},{9,8},{10,11... | collective-permute-start | bytes 1572872 | tf_op jit(solution)/shard_map/ppermute | solution.py:377
  43.5 4.9 %collective-permute-start.6 = (bf16[8,256,128]{2,1,0:T(8,128)(2,1)}, bf16[8,256,128]{2,1,0:T(8,128)(2,1)S(1)}, u32[]{:S(2)}, u32[]{:S(2)}) collective-permute-start(bf16[8,256,128]{2,1,0:T(8,128)(2,1)} %get-tuple-element.41), channel_id=1, source_target_pairs={{0,1},{1,0},{2,3},{3,2},{4,5},{5,4},{6,7},{7,6},{8,9},{9,8},{10,11... | collective-permute-start | bytes 1572872 | tf_op jit(solution)/shard_map/ppermute | solution.py:377
  44.0 6.3 %collective-permute-start.10 = (bf16[2,256,128]{2,1,0:T(8,128)(2,1)}, bf16[2,256,128]{2,1,0:T(8,128)(2,1)S(1)}, u32[]{:S(2)}, u32[]{:S(2)}) collective-permute-start(bf16[2,256,128]{2,1,0:T(8,128)(2,1)} %get-tuple-element.44), channel_id=1, source_target_pairs={{0,2},{1,3},{2,0},{3,1},{4,6},{5,7},{6,4},{7,5},{8,10},{9,11},{10,... | collective-permute-start | bytes 393224 | tf_op jit(solution)/shard_map/ppermute | solution.py:377
  45.4 11.5 %collective-permute-start.5 = (bf16[2,256,128]{2,1,0:T(8,128)(2,1)}, bf16[2,256,128]{2,1,0:T(8,128)(2,1)S(1)}, u32[]{:S(2)}, u32[]{:S(2)}) collective-permute-start(bf16[2,256,128]{2,1,0:T(8,128)(2,1)} %get-tuple-element.40), channel_id=1, source_target_pairs={{0,4},{1,5},{2,6},{3,7},{4,0},{5,1},{6,2},{7,3},{8,12},{9,13},{10,... | collective-permute-start | bytes 393224 | tf_op jit(solution)/shard_map/ppermute | solution.py:377
  45.4 11.5 %collective-permute-start.8 = (bf16[2,256,128]{2,1,0:T(8,128)(2,1)}, bf16[2,256,128]{2,1,0:T(8,128)(2,1)S(1)}, u32[]{:S(2)}, u32[]{:S(2)}) collective-permute-start(bf16[2,256,128]{2,1,0:T(8,128)(2,1)} %get-tuple-element.42), channel_id=1, source_target_pairs={{0,6},{1,7},{2,4},{3,5},{4,2},{5,3},{6,0},{7,1},{8,14},{9,15},{10,... | collective-permute-start | bytes 393224 | tf_op jit(solution)/shard_map/ppermute | solution.py:377
  48.3 7.6 %copy-start = (bf16[2,256,128]{2,1,0:T(8,128)(2,1)S(1)}, bf16[2,256,128]{2,1,0:T(8,128)(2,1)}, u32[]{:S(2)}) copy-start(bf16[2,256,128]{2,1,0:T(8,128)(2,1)} %get-tuple-element.43.refs_0_) | copy-start | bytes 393220
  48.4 7.5 %collective-permute-start.11 = (bf16[2,256,128]{2,1,0:T(8,128)(2,1)S(1)}, bf16[2,256,128]{2,1,0:T(8,128)(2,1)S(1)}, u32[]{:S(2)}, u32[]{:S(2)}) collective-permute-start(bf16[2,256,128]{2,1,0:T(8,128)(2,1)S(1)} %get-tuple-element.69), channel_id=1, source_target_pairs={{0,2},{1,3},{2,0},{3,1},{4,6},{5,7},{6,4},{7,5},{8,10},{9,11},{10,... | collective-permute-start | bytes 393224 | tf_op jit(solution)/shard_map/ppermute | solution.py:377
  50.1 7.5 %collective-permute-start.7 = (bf16[2,256,128]{2,1,0:T(8,128)(2,1)S(1)}, bf16[2,256,128]{2,1,0:T(8,128)(2,1)S(1)}, u32[]{:S(2)}, u32[]{:S(2)}) collective-permute-start(bf16[2,256,128]{2,1,0:T(8,128)(2,1)S(1)} %get-tuple-element.72), channel_id=1, source_target_pairs={{0,4},{1,5},{2,6},{3,7},{4,0},{5,1},{6,2},{7,3},{8,12},{9,13},{10,... | collective-permute-start | bytes 393224 | tf_op jit(solution)/shard_map/ppermute | solution.py:377
  50.3 9.0 %collective-permute-start.9 = (bf16[2,256,128]{2,1,0:T(8,128)(2,1)S(1)}, bf16[2,256,128]{2,1,0:T(8,128)(2,1)S(1)}, u32[]{:S(2)}, u32[]{:S(2)}) collective-permute-start(bf16[2,256,128]{2,1,0:T(8,128)(2,1)S(1)} %get-tuple-element.71), channel_id=1, source_target_pairs={{0,6},{1,7},{2,4},{3,5},{4,2},{5,3},{6,0},{7,1},{8,14},{9,15},{10,... | collective-permute-start | bytes 393224 | tf_op jit(solution)/shard_map/ppermute | solution.py:377
  56.9 4.7 %copy-start.1 = (bf16[8,256,128]{2,1,0:T(8,128)(2,1)S(1)}, bf16[8,256,128]{2,1,0:T(8,128)(2,1)}, u32[]{:S(2)}) copy-start(bf16[8,256,128]{2,1,0:T(8,128)(2,1)} %get-tuple-element.50) | copy-start | bytes 1572868
  60.3 26.6 %collective-permute-start.18 = (bf16[8,256,128]{2,1,0:T(8,128)(2,1)S(1)}, bf16[8,256,128]{2,1,0:T(8,128)(2,1)S(1)}, u32[]{:S(2)}, u32[]{:S(2)}) collective-permute-start(bf16[8,256,128]{2,1,0:T(8,128)(2,1)S(1)} %far_late.1), channel_id=1, source_target_pairs={{0,8},{1,9},{2,10},{3,11},{4,12},{5,13},{6,14},{7,15},{8,0},{9,1},... | collective-permute-start | bytes 1572872 | tf_op jit(solution)/shard_map/ppermute | solution.py:404
  61.7 5.5 %collective-permute-start.16 = (bf16[2,256,128]{2,1,0:T(8,128)(2,1)S(1)}, bf16[2,256,128]{2,1,0:T(8,128)(2,1)S(1)}, u32[]{:S(2)}, u32[]{:S(2)}) collective-permute-start(bf16[2,256,128]{2,1,0:T(8,128)(2,1)S(1)} %get-tuple-element.65), channel_id=1, source_target_pairs={{0,2},{1,3},{2,0},{3,1},{4,6},{5,7},{6,4},{7,5},{8,10},{9,11},{10,... | collective-permute-start | bytes 393224 | tf_op jit(solution)/shard_map/ppermute | solution.py:377
  62.3 7.3 %collective-permute-start.17 = (bf16[2,256,128]{2,1,0:T(8,128)(2,1)S(1)}, bf16[2,256,128]{2,1,0:T(8,128)(2,1)S(1)}, u32[]{:S(2)}, u32[]{:S(2)}) collective-permute-start(bf16[2,256,128]{2,1,0:T(8,128)(2,1)S(1)} %get-tuple-element.61), channel_id=1, source_target_pairs={{0,2},{1,3},{2,0},{3,1},{4,6},{5,7},{6,4},{7,5},{8,10},{9,11},{10,... | collective-permute-start | bytes 393224 | tf_op jit(solution)/shard_map/ppermute | solution.py:377
  63.9 12.9 %collective-permute-start.12 = (bf16[2,256,128]{2,1,0:T(8,128)(2,1)S(1)}, bf16[2,256,128]{2,1,0:T(8,128)(2,1)S(1)}, u32[]{:S(2)}, u32[]{:S(2)}) collective-permute-start(bf16[2,256,128]{2,1,0:T(8,128)(2,1)S(1)} %get-tuple-element.68), channel_id=1, source_target_pairs={{0,4},{1,5},{2,6},{3,7},{4,0},{5,1},{6,2},{7,3},{8,12},{9,13},{10,... | collective-permute-start | bytes 393224 | tf_op jit(solution)/shard_map/ppermute | solution.py:377
  64.6 15.0 %collective-permute-start.13 = (bf16[2,256,128]{2,1,0:T(8,128)(2,1)S(1)}, bf16[2,256,128]{2,1,0:T(8,128)(2,1)S(1)}, u32[]{:S(2)}, u32[]{:S(2)}) collective-permute-start(bf16[2,256,128]{2,1,0:T(8,128)(2,1)S(1)} %get-tuple-element.64), channel_id=1, source_target_pairs={{0,4},{1,5},{2,6},{3,7},{4,0},{5,1},{6,2},{7,3},{8,12},{9,13},{10,... | collective-permute-start | bytes 393224 | tf_op jit(solution)/shard_map/ppermute | solution.py:377
  67.2 14.6 %collective-permute-start.14 = (bf16[2,256,128]{2,1,0:T(8,128)(2,1)S(1)}, bf16[2,256,128]{2,1,0:T(8,128)(2,1)S(1)}, u32[]{:S(2)}, u32[]{:S(2)}) collective-permute-start(bf16[2,256,128]{2,1,0:T(8,128)(2,1)S(1)} %get-tuple-element.67), channel_id=1, source_target_pairs={{0,6},{1,7},{2,4},{3,5},{4,2},{5,3},{6,0},{7,1},{8,14},{9,15},{10,... | collective-permute-start | bytes 393224 | tf_op jit(solution)/shard_map/ppermute | solution.py:377
  69.5 17.4 %collective-permute-start.15 = (bf16[2,256,128]{2,1,0:T(8,128)(2,1)S(1)}, bf16[2,256,128]{2,1,0:T(8,128)(2,1)S(1)}, u32[]{:S(2)}, u32[]{:S(2)}) collective-permute-start(bf16[2,256,128]{2,1,0:T(8,128)(2,1)S(1)} %get-tuple-element.63), channel_id=1, source_target_pairs={{0,6},{1,7},{2,4},{3,5},{4,2},{5,3},{6,0},{7,1},{8,14},{9,15},{10,... | collective-permute-start | bytes 393224 | tf_op jit(solution)/shard_map/ppermute | solution.py:377
  (3 other events, 2.0 us)
